TPU v7x, 128 devices: a whole 4x4x4 slice. The times are simulated.
128 devices in a mesh: cache: 16 (over x, z), cls: 8 (over y, core).
Axes of the slice: x: 4, y: 4, z: 4, core: 2. Of those that a mesh axis runs over, the one named last changes fastest.
Arguments:
- queries: bfloat16 [4096, 1024], P(('cache', 'cls')), may hold values from -14 to 14
- cache_keys: bfloat16 [163840, 1024], P('cache'), may hold values from -6 to 6
- labels: int32 [163840], P('cache'), may hold values from 0 to 10239, as said below
- prototypes: bfloat16 [10240, 1024], P('cls'), may hold values from -1 to 1
Outputs:
- log_probs: float32 [4096, 10240], P('cache', 'cls')
Inputs may be any that keep to these rules, and one draw needn't show every extreme that they name: Split the classes into 16 aligned blocks of 640; the 10240 cached shapes of one index of cache hold at most 1280 labels of one block, and one block, drawn from the seed, holds exactly 1280 labels of every index of cache.
All inputs are finite; a program needn't handle non-finite values.
Results may differ from a plain program's by a relative error of at most 0.0009.
The roundings to bfloat16 on the way count: a program that leaves them out, or rounds other values in their place, can miss the bound.
Values may be sent and summed in bfloat16 or wider, within the bound.
No kernel may reach another device: no remote copies, remote signals or barrier semaphores. Data moves between devices by JAX's collectives and lax.ppermute only.
A program may use at most 192 MiB of HBM per device.

v0:
```python
import jax
import jax.numpy as jnp
from jax import lax
from jax.experimental import pallas as pl
from jax.experimental.pallas import tpu as pltpu
from jax.sharding import PartitionSpec as P

text_scale = 100.0
epsilon = 1e-06
SIDE = 4
CB = 640
CAP = 1280
QT = 256
KT = 256
TAIL = 16


def params(mib=58):
    return pltpu.CompilerParams(vmem_limit_bytes=mib * 1024 * 1024)


def unit_rows(matrix):
    widened = matrix.astype(jnp.float32)
    return (widened / jnp.sqrt(jnp.sum(widened * widened, axis=1, keepdims=True) + epsilon)).astype(
        jnp.bfloat16
    )


def prepare_kernel(rows_ref, labels_ref, unit_ref, hot_ref):
    unit_ref[...] = unit_rows(rows_ref[...])
    classes = lax.broadcasted_iota(jnp.int32, (KT, CB), 1)
    labels = jnp.sum(jnp.where(diagonal(), labels_ref[0], 0), axis=1, keepdims=True)
    hot_ref[...] = jnp.where(labels == classes, 1.0, 0.0).astype(jnp.bfloat16)


def prepare(rows, labels):
    count, width = rows.shape
    return pl.pallas_call(
        prepare_kernel,
        grid=(count // KT,),
        in_specs=[
            pl.BlockSpec((KT, width), lambda i: (i, 0)),
            pl.BlockSpec((1, 1, KT), lambda i: (i, 0, 0)),
        ],
        out_specs=[
            pl.BlockSpec((KT, width), lambda i: (i, 0)),
            pl.BlockSpec((KT, CB), lambda i: (i, 0)),
        ],
        out_shape=[
            jax.ShapeDtypeStruct((count, width), jnp.bfloat16),
            jax.ShapeDtypeStruct((count, CB), jnp.bfloat16),
        ],
        compiler_params=params(),
        cost_estimate=pl.CostEstimate(flops=count * width * 4, bytes_accessed=count * width * 6, transcendentals=count),
        name="prepare",
    )(rows, labels.reshape(count // KT, 1, KT))


def aligned(value):
    return pl.multiple_of(value, QT)


def diagonal():
    shape = (QT, QT)
    return lax.broadcasted_iota(jnp.int32, shape, 0) == lax.broadcasted_iota(jnp.int32, shape, 1)


def encode(values, message_ref, tile, tail_row):
    largest = jnp.maximum(jnp.max(values, axis=1, keepdims=True), 1e-30)
    exponent = jnp.ceil(jnp.log2(largest) - 14.99)
    codes = (values * jnp.exp2(-exponent) + 0.5).astype(jnp.int32)
    message_ref[pl.ds(aligned(tile * QT), QT), :] = codes.astype(jnp.int16)
    along = jnp.sum(jnp.where(diagonal(), exponent, 0.0), axis=0, keepdims=True)
    shape = (TAIL, QT)
    old = message_ref[tail_row : tail_row + TAIL, :QT].astype(jnp.int32)
    new = jnp.broadcast_to(along, shape).astype(jnp.int32)
    at = lax.broadcasted_iota(jnp.int32, shape, 0) == tile
    message_ref[tail_row : tail_row + TAIL, :QT] = jnp.where(at, new, old).astype(jnp.int16)


def clear_tail(message_ref, tail_row):
    message_ref[tail_row : tail_row + TAIL, :] = jnp.zeros((TAIL, CB), jnp.int16)


def decode(message_ref, tile, tail_row):
    shape = (TAIL, QT)
    tail = message_ref[tail_row : tail_row + TAIL, :QT].astype(jnp.float32)
    at = lax.broadcasted_iota(jnp.int32, shape, 0) == tile
    along = jnp.sum(jnp.where(at, tail, 0.0), axis=0, keepdims=True)
    exponent = jnp.sum(jnp.where(diagonal(), along, 0.0), axis=1, keepdims=True)
    codes = message_ref[pl.ds(aligned(tile * QT), QT), :].astype(jnp.float32)
    return codes * jnp.exp2(exponent)


HALF = 2 * QT
HALF_MSG = jax.ShapeDtypeStruct((HALF + TAIL, CB), jnp.int16)
TILE_MSG = jax.ShapeDtypeStruct((QT + TAIL, CB), jnp.int16)
HALF_RAW = jax.ShapeDtypeStruct((HALF, CB), jnp.float32)


SUPER = SIDE * QT
COMMON = 3
TILES = CAP // KT


def super_sums(tiles, wait_keys, wait_hots, q_ref, keys_ref, hot_ref, scores_ref, total_ref):
    width = q_ref.shape[-1]
    sharpness = float(width) ** 0.5
    queries = q_ref[...].reshape(SUPER, width)

    def step(t, carry):
        wait_keys(t)
        keys = keys_ref[pl.ds(aligned(t * KT), KT), :]
        cosine = lax.dot_general(
            queries, keys, (((1,), (1,)), ((), ())), preferred_element_type=jnp.float32
        )
        scores_ref[:, pl.ds(aligned(t * KT), KT)] = jnp.exp(sharpness * cosine).astype(jnp.bfloat16)
        return carry

    lax.fori_loop(0, tiles, step, 0)
    wait_hots()
    cut = COMMON * KT
    total_ref[...] = jnp.dot(
        scores_ref[:, :cut], hot_ref[:cut, :], preferred_element_type=jnp.float32
    )

    @pl.when(tiles > COMMON)
    def _():
        total_ref[...] += jnp.dot(
            scores_ref[:, cut:], hot_ref[cut:, :], preferred_element_type=jnp.float32
        )


def sums(shifts, halves, coded, facts, queries, keys, hots, arrived=()):
    width = keys.shape[1]
    joined = len(arrived)

    def kernel(facts_ref, q_hbm, keys_hbm, hot_hbm, *rest):
        came, outs, next_ref = rest[:joined], rest[joined : joined + 4], rest[joined + 4]
        scratch = rest[joined + 5 :]
        q_ref, keys_ref, hot_ref, scores_ref, total_ref, came_ref, msg_ref = scratch[:7]
        q_sems, key_sems, hot_sems, came_sems, out_sems = scratch[7:]
        for at in range(4):
            next_ref[at] = facts_ref[at]

        def copy_queries(block, part):
            away = shifts[part // 2]
            inner = halves[part // 2] * 2 + part % 2
            outer = lax.rem(facts_ref[block] + away, SIDE)
            chunk = jnp.where(block == 0, outer * SIDE + inner, inner * SIDE + outer)
            return pltpu.make_async_copy(q_hbm.at[chunk], q_ref.at[block, part], q_sems.at[block, part])

        def copy_keys(block, t):
            return pltpu.make_async_copy(
                keys_hbm.at[pl.ds(aligned(block * CAP + t * KT), KT), :],
                keys_ref.at[block, pl.ds(aligned(t * KT), KT), :],
                key_sems.at[block, t],
            )

        def copy_hots(block):
            return pltpu.make_async_copy(
                hot_hbm.at[pl.ds(aligned(block * CAP), CAP), :], hot_ref.at[block], hot_sems.at[block]
            )

        def copy_came(at):
            return pltpu.make_async_copy(came[at], came_ref.at[at], came_sems.at[at])

        def copy_out(at):
            source = msg_ref.at[at] if coded else total_ref.at[at // 2, pl.ds(at % 2 * HALF, HALF), :]
            return pltpu.make_async_copy(source, outs[at], out_sems.at[at])

        for block in range(2):
            for part in range(SIDE):
                copy_queries(block, part).start()

            def start(t, carry, block=block):
                copy_keys(block, t).start()
                return carry

            lax.fori_loop(0, facts_ref[2 + block], start, 0)
            copy_hots(block).start()
        for at in range(joined):
            copy_came(at).start()
        scores_ref[...] = jnp.zeros_like(scores_ref)
        if coded:
            for at in range(4):
                clear_tail(msg_ref.at[at], HALF)

        def run(block, carry):
            for part in range(SIDE):
                copy_queries(block, part).wait()
            super_sums(
                facts_ref[2 + block],
                lambda t: copy_keys(block, t).wait(),
                lambda: copy_hots(block).wait(),
                q_ref.at[block],
                keys_ref.at[block],
                hot_ref.at[block],
                scores_ref,
                total_ref.at[block],
            )
            if joined:
                @pl.when(block == 0)
                def _():
                    for at in range(joined):
                        copy_came(at).wait()

            if joined or coded:
                def body(t, carry):
                    rows = pl.ds(aligned(t * QT), QT)
                    at = 2 * block + t // 2
                    values = total_ref[block, rows, :]
                    if joined:
                        values += decode(came_ref.at[at], t % 2, HALF)
                    if coded:
                        encode(values, msg_ref.at[at], t % 2, HALF)
                    else:
                        total_ref[block, rows, :] = values
                    return carry

                lax.fori_loop(0, SIDE, body, 0)
            for at in range(4):
                @pl.when(block == at // 2)
                def _(at=at):
                    copy_out(at).start()
            return carry

        lax.fori_loop(0, 2, run, 0)
        for at in range(4):
            copy_out(at).wait()

    smem = pl.BlockSpec(memory_space=pltpu.SMEM)
    anywhere = pl.BlockSpec(memory_space=pl.ANY)
    return pl.pallas_call(
        kernel,
        in_specs=[smem] + [anywhere] * (3 + joined),
        out_specs=[anywhere] * 4 + [smem],
        out_shape=[HALF_MSG if coded else HALF_RAW] * 4 + [jax.ShapeDtypeStruct((4,), jnp.int32)],
        scratch_shapes=[
            pltpu.VMEM((2, SIDE, QT, width), jnp.bfloat16),
            pltpu.VMEM((2, CAP, width), jnp.bfloat16),
            pltpu.VMEM((2, CAP, CB), jnp.bfloat16),
            pltpu.VMEM((SUPER, CAP), jnp.bfloat16),
            pltpu.VMEM((2, SUPER, CB), jnp.float32),
            pltpu.VMEM((4,) + HALF_MSG.shape, jnp.int16),
            pltpu.VMEM((4,) + HALF_MSG.shape, jnp.int16),
            pltpu.SemaphoreType.DMA((2, SIDE)),
            pltpu.SemaphoreType.DMA((2, TILES)),
            pltpu.SemaphoreType.DMA((2,)),
            pltpu.SemaphoreType.DMA((4,)),
            pltpu.SemaphoreType.DMA((4,)),
        ],
        compiler_params=params(),
        cost_estimate=pl.CostEstimate(
            flops=2 * 4 * HALF * CAP * (width + CB),
            bytes_accessed=8 * HALF * width,
            transcendentals=2 * HALF * CAP,
        ),
        name="sums",
    )(facts, queries, keys, hots, *arrived)


def turn(place, low, high, low_came, high_came):
    def kernel(place_ref, low_hbm, high_hbm, low_msg, high_msg, own_hbm, plus_hbm, far_hbm, minus_hbm, *scratch):
        raw_ref, came_ref, msg_ref, own_ref, raw_sems, came_sems, out_sems = scratch

        def loads(half):
            raw, came = ((low_hbm, low_msg), (high_hbm, high_msg))[half]
            return (
                pltpu.make_async_copy(raw, raw_ref.at[half], raw_sems.at[half]),
                pltpu.make_async_copy(came, came_ref.at[half], came_sems.at[half]),
            )

        for half in range(2):
            for load in loads(half):
                load.start()
        for k in range(3):
            clear_tail(msg_ref.at[k], QT)
        for half in range(2):
            for load in loads(half):
                load.wait()

        def values(k):
            tile = lax.rem(place_ref[0] + k, SIDE)
            half, at = tile // 2, tile % 2
            return raw_ref[half, pl.ds(aligned(at * QT), QT), :] + decode(came_ref.at[half], at, HALF)

        def body(i, carry):
            k = jnp.where(i == 0, 2, jnp.where(i == 1, 1, 3))
            encode(values(k), msg_ref.at[i], 0, QT)
            return carry

        outs = [
            pltpu.make_async_copy(msg_ref.at[i], out, out_sems.at[i])
            for i, out in enumerate((far_hbm, plus_hbm, minus_hbm))
        ]
        outs.append(pltpu.make_async_copy(own_ref, own_hbm, out_sems.at[3]))
        lax.fori_loop(0, 3, body, 0)
        for out in outs[:3]:
            out.start()
        own_ref[...] = values(0)
        outs[3].start()
        for out in outs:
            out.wait()

    anywhere = pl.BlockSpec(memory_space=pl.ANY)
    return pl.pallas_call(
        kernel,
        in_specs=[pl.BlockSpec(memory_space=pltpu.SMEM)] + [anywhere] * 4,
        out_specs=[anywhere] * 4,
        out_shape=[jax.ShapeDtypeStruct((QT, CB), jnp.float32), TILE_MSG, TILE_MSG, TILE_MSG],
        scratch_shapes=[
            pltpu.VMEM((2, HALF, CB), jnp.float32),
            pltpu.VMEM((2,) + HALF_MSG.shape, jnp.int16),
            pltpu.VMEM((3,) + TILE_MSG.shape, jnp.int16),
            pltpu.VMEM((QT, CB), jnp.float32),
            pltpu.SemaphoreType.DMA((2,)),
            pltpu.SemaphoreType.DMA((2,)),
            pltpu.SemaphoreType.DMA((4,)),
        ],
        compiler_params=params(),
        cost_estimate=pl.CostEstimate(flops=40 * QT * CB, bytes_accessed=40 * QT * CB, transcendentals=0),
        name="turn",
    )(place, low, high, low_came, high_came)


def close(text, own_a, msgs_a, own_b, msgs_b):
    def kernel(text_ref, *rest):
        own, msgs = rest[0:2], (rest[2:5], rest[5:8])
        logits_ref, stats_ref = rest[8:]
        for block in range(2):
            total = own[block][...]
            for msg in msgs[block]:
                total += decode(msg, 0, QT)
            at = slice(block * CB, block * CB + CB)
            logits_ref[:, at] = text_ref[:, at] + total
        logits = logits_ref[...]
        largest = jnp.max(logits, axis=1, keepdims=True)
        total = jnp.sum(jnp.exp(logits - largest), axis=1, keepdims=True)
        eye = diagonal()
        stats_ref[0:1, :] = jnp.sum(jnp.where(eye, largest, 0.0), axis=0, keepdims=True)
        stats_ref[1:2, :] = jnp.sum(jnp.where(eye, total, 0.0), axis=0, keepdims=True)

    return pl.pallas_call(
        kernel,
        out_shape=[
            jax.ShapeDtypeStruct((QT, 2 * CB), jnp.float32),
            jax.ShapeDtypeStruct((2, QT), jnp.float32),
        ],
        compiler_params=params(24),
        cost_estimate=pl.CostEstimate(flops=30 * QT * CB, bytes_accessed=40 * QT * CB, transcendentals=QT * CB),
        name="close",
    )(text, own_a, own_b, *msgs_a, *msgs_b)


def finish(logits, stats):
    def kernel(logits_ref, stats_ref, out_ref):
        largest = jnp.max(stats_ref[:, 0, :], axis=0, keepdims=True)
        total = jnp.sum(stats_ref[:, 1, :] * jnp.exp(stats_ref[:, 0, :] - largest), axis=0, keepdims=True)
        eye = diagonal()
        largest = jnp.sum(jnp.where(eye, largest, 0.0), axis=1, keepdims=True)
        shift = jnp.sum(jnp.where(eye, jnp.log(total), 0.0), axis=1, keepdims=True)
        out_ref[...] = logits_ref[...] - largest - shift

    return pl.pallas_call(
        kernel,
        out_shape=jax.ShapeDtypeStruct(logits.shape, jnp.float32),
        compiler_params=params(24),
        name="finish",
    )(logits, stats)


def shifted(dx, dz):
    return [
        (x * SIDE + z, (x + dx) % SIDE * SIDE + (z + dz) % SIDE) for x in range(SIDE) for z in range(SIDE)
    ]


def send(message, dx, dz):
    return lax.ppermute(message, "cache", shifted(dx, dz))


def per_device(queries, cache_keys, labels, prototypes):
    width = queries.shape[1]
    own = lax.axis_index("cache")
    x, z = own // SIDE, own % SIDE
    low = lax.axis_index("cls") * (2 * CB)

    gathered = lax.all_gather(unit_rows(queries), ("cache", "cls"), axis=0, tiled=True)

    order = lax.sort(labels * 16384 + lax.iota(jnp.int32, labels.shape[0]), is_stable=False)
    start = jnp.sum((labels < low).astype(jnp.int32))
    middle = jnp.sum((labels < low + CB).astype(jnp.int32))
    stop = jnp.sum((labels < low + 2 * CB).astype(jnp.int32))
    padded = jnp.concatenate([order, jnp.zeros((CAP,), jnp.int32)])
    picked = jnp.concatenate(
        [lax.dynamic_slice(padded, (start,), (CAP,)), lax.dynamic_slice(padded, (middle,), (CAP,))]
    )
    counts = jnp.stack([middle - start, stop - middle])
    place = lax.iota(jnp.int32, 2 * CAP)
    block = place // CAP
    valid = place - block * CAP < jnp.where(block == 0, counts[0], counts[1])
    local = jnp.where(valid, picked // 16384 - low - block * CB, -1)
    rows = jnp.take(cache_keys, picked % 16384, axis=0, mode="clip")
    keys, hots = prepare(rows, local)
    tiles = (counts + KT - 1) // KT
    gathered, keys, hots = lax.optimization_barrier((gathered, keys, hots))
    q3 = gathered.reshape(SIDE * SIDE, QT, width)
    facts = jnp.stack([x, z, tiles[0], tiles[1]]).astype(jnp.int32)

    def run(facts, shifts, halves, coded, arrived=()):
        *parts, facts = sums(shifts, halves, coded, facts, q3, keys, hots, arrived)
        return parts, facts

    def send_all(parts):
        a_right, a_left, b_right, b_left = parts
        return send(a_right, 1, 0), send(a_left, -1, 0), send(b_right, 0, 1), send(b_left, 0, -1)

    far, facts = run(facts, (2, 2), (0, 1), True)
    far = send_all(far)
    free, facts = run(facts, (1, 3), (1, 0), True)
    free = send_all(free)
    full, facts = run(facts, (1, 3), (0, 1), True, far)
    full = send_all(full)
    a_low, a_high, b_low, b_high = run(
        facts, (0, 0), (0, 1), False, (free[1], free[0], free[3], free[2])
    )[0]

    text = text_scale * lax.dot_general(
        lax.dynamic_index_in_dim(q3, own, 0, keepdims=False),
        prototypes,
        (((1,), (1,)), ((), ())),
        preferred_element_type=jnp.float32,
    )

    own_a, a_plus, a_far, a_minus = turn(z[None], a_low, a_high, full[0], full[1])
    own_b, b_plus, b_far, b_minus = turn(x[None], b_low, b_high, full[2], full[3])
    a_msgs = send(a_far, 0, 2), send(a_plus, 0, 1), send(a_minus, 0, -1)
    b_msgs = send(b_far, 2, 0), send(b_plus, 1, 0), send(b_minus, -1, 0)

    logits, stats = close(text, own_a, a_msgs, own_b, b_msgs)
    return finish(logits, lax.all_gather(stats, "cls"))


def solution(mesh):
    placed = (P(("cache", "cls"), None), P("cache", None), P("cache"), P("cls", None))
    return jax.shard_map(
        per_device, mesh=mesh, in_specs=placed, out_specs=P("cache", "cls"), check_vma=False
    )
```

profile of v0, /device:TPU:1, one launch (start us, length us, event | category | flops | bytes accessed | tf_op | source)
XLA Modules:
  0.0 218.1 jit_solution(15509481953216107883)
XLA Ops:
  6.5 1.1 fusion.2
  7.7 1.6 fusion.3
  9.2 0.0 all-gather.4.cloned.1.call-update
  9.3 1.5 convert_reduce_fusion
  14.8 6.3 %sort.7 = s32[10240]{0:T(1024)S(1)} sort(s32[10240]{0:T(1024)S(1)} %get-tuple-element.78), dimensions={0}, to_apply=%region_1.2 | sort | flops 143360 | bytes 81920 | tf_op jit(solution)/shard_map/sort | solution.py:391
  22.4 0.1 pad_dynamic-slice_fusion
  23.9 0.1 fusion.4
  23.9 21.8 %gather_fusion = bf16[2560,1024]{1,0:T(8,128)(2,1)} fusion(bf16[10240,1024]{1,0:T(8,128)(2,1)} %param.5, s32[3072]{0:T(1024)S(1)} %pad_clamp_fusion), kind=kCustom, calls=%fused_computation | custom fusion | bytes 10496000 | tf_op jit(solution)/shard_map/jit(_take)/gather | solution.py:404
  45.8 0.7 compare_select_fusion.2.labels_ref
  46.4 9.5 %prepare.1 = (bf16[2560,1024]{1,0:T(8,128)(2,1)}, bf16[2560,640]{1,0:T(8,128)(2,1)}) custom-call(bf16[2560,1024]{1,0:T(8,128)(2,1)} %gather_fusion, s32[10,1,256]{2,1,0:T(1,128)} %compare_select_fusion.2.labels_ref), custom_call_target="tpu_custom_call" | custom-call | flops 10485760 | bytes 15728640 | tf_op jit(solution)/shard_map/prepare/pallas_call | solution.py:38
  55.9 0.1 and_select_fusion.3
  56.0 0.7 pad_add_fusion.facts_ref
  56.6 27.6 %all-gather.4.cloned.1.call-done = bf16[4096,1024]{1,0:T(8,128)(2,1)} async-done(((bf16[32,1024]{1,0:T(8,128)(2,1)}), bf16[4096,1024]{1,0:T(8,128)(2,1)}) %all-gather.4.cloned.1.call-update) | async-done | bytes 8388624 | tf_op jit(solution)/shard_map/all_gather | solution.py:389
  84.3 13.6 %sums.4 = (s16[528,640]{1,0:T(8,128)(2,1)}, s16[528,640]{1,0:T(8,128)(2,1)}, s16[528,640]{1,0:T(8,128)(2,1)}, s16[528,640]{1,0:T(8,128)(2,1)}, s32[4]{0:T(128)}) custom-call(s32[4]{0:T(128)} %pad_add_fusion.facts_ref, bf16[16,256,1024]{2,1,0:T(8,128)(2,1)} %bitcast.11, bf16[2560,1024]{1,0:T(8,128)(2,1)} %get-tuple-element.42.keys_hbm, ...), custom_call_target="tpu_custom_call" | custom-call | flops 8724152320 | bytes 4194304 | tf_op jit(solution)/shard_map/sums/pallas_call | solution.py:234
  97.8 0.1 collective-permute-start
  97.9 2.7 %collective-permute-start.1 = (s16[528,640]{1,0:T(8,128)(2,1)}, s16[528,640]{1,0:T(8,128)(2,1)S(1)}, u32[]{:S(2)}, u32[]{:S(2)}) collective-permute-start(s16[528,640]{1,0:T(8,128)(2,1)} %get-tuple-element.47), channel_id=1, source_target_pairs={{0,96},{8,104},{16,112},{24,120},{32,0},{40,8},{48,16},{56,24},{64... | collective-permute-start | bytes 2027528 | tf_op jit(solution)/shard_map/ppermute | solution.py:380
  100.6 1.0 collective-permute-start.2
  101.6 1.7 collective-permute-start.3
  103.3 13.9 %sums.5 = (s16[528,640]{1,0:T(8,128)(2,1)}, s16[528,640]{1,0:T(8,128)(2,1)}, s16[528,640]{1,0:T(8,128)(2,1)}, s16[528,640]{1,0:T(8,128)(2,1)}, s32[4]{0:T(128)}) custom-call(s32[4]{0:T(128)} %get-tuple-element.44.facts_ref, bf16[16,256,1024]{2,1,0:T(8,128)(2,1)} %bitcast.12, bf16[2560,1024]{1,0:T(8,128)(2,1)} %get-tuple-element.42.keys_hbm, ...), custom_call_target="tpu_custom_call" | custom-call | flops 8724152320 | bytes 4194304 | tf_op jit(solution)/shard_map/sums/pallas_call | solution.py:234
  117.1 0.1 collective-permute-start.4
  117.2 0.0 collective-permute-done.rest_0_
  117.2 0.0 copy-start.12
  117.2 1.4 collective-permute-start.5
  118.7 0.0 collective-permute-done.1.rest_1_
  118.7 2.0 collective-permute-start.6
  120.7 0.0 collective-permute-done.2.rest_2_
  120.7 0.0 collective-permute-start.7
  120.7 0.0 collective-permute-done.3.rest_3_
  120.7 15.0 %sums.6 = (s16[528,640]{1,0:T(8,128)(2,1)}, s16[528,640]{1,0:T(8,128)(2,1)}, s16[528,640]{1,0:T(8,128)(2,1)}, s16[528,640]{1,0:T(8,128)(2,1)}, s32[4]{0:T(128)}) custom-call(s32[4]{0:T(128)} %get-tuple-element.45.facts_ref, bf16[16,256,1024]{2,1,0:T(8,128)(2,1)} %bitcast.13, bf16[2560,1024]{1,0:T(8,128)(2,1)} %get-tuple-element.42.keys_hbm, ...), custom_call_target="tpu_custom_call" | custom-call | flops 8724152320 | bytes 4194304 | tf_op jit(solution)/shard_map/sums/pallas_call | solution.py:234
  135.7 0.1 collective-permute-start.10
  135.8 0.0 collective-permute-done.4.rest_0_
  135.8 2.6 %collective-permute-start.11 = (s16[528,640]{1,0:T(8,128)(2,1)}, s16[528,640]{1,0:T(8,128)(2,1)S(1)}, u32[]{:S(2)}, u32[]{:S(2)}) collective-permute-start(s16[528,640]{1,0:T(8,128)(2,1)} %get-tuple-element.63), channel_id=1, source_target_pairs={{0,24},{8,0},{16,8},{24,16},{32,56},{40,32},{48,40},{56,48},{64,88... | collective-permute-start | bytes 2027528 | tf_op jit(solution)/shard_map/ppermute | solution.py:380
  138.5 0.0 collective-permute-done.5.rest_1_
  138.5 0.9 copy-done.10
  139.4 0.0 collective-permute-start.8
  139.4 0.8 copy-done.11
  140.3 3.9 %collective-permute-start.9 = (s16[528,640]{1,0:T(8,128)(2,1)}, s16[528,640]{1,0:T(8,128)(2,1)S(1)}, u32[]{:S(2)}, u32[]{:S(2)}) collective-permute-start(s16[528,640]{1,0:T(8,128)(2,1)} %get-tuple-element.58), channel_id=1, source_target_pairs={{0,96},{8,104},{16,112},{24,120},{32,0},{40,8},{48,16},{56,24},{64... | collective-permute-start | bytes 2027528 | tf_op jit(solution)/shard_map/ppermute | solution.py:380
  144.2 0.0 collective-permute-done.7.rest_3_
  144.2 13.5 %sums.7 = (f32[512,640]{1,0:T(8,128)}, f32[512,640]{1,0:T(8,128)}, f32[512,640]{1,0:T(8,128)}, f32[512,640]{1,0:T(8,128)}, s32[4]{0:T(128)}) custom-call(s32[4]{0:T(128)} %get-tuple-element.50.facts_ref, bf16[16,256,1024]{2,1,0:T(8,128)(2,1)} %bitcast.14, bf16[2560,1024]{1,0:T(8,128)(2,1)} %get-tuple-element.42.keys_hbm, ...), custom_call_target="tpu_custom_call" | custom-call | flops 8724152320 | bytes 4194304 | tf_op jit(solution)/shard_map/sums/pallas_call | solution.py:234
  157.7 0.0 collective-permute-done.11.high_msg
  157.7 0.8 copy-done.7
  158.5 0.2 copy-done.8
  158.7 4.5 %turn.3 = (f32[256,640]{1,0:T(8,128)}, s16[272,640]{1,0:T(8,128)(2,1)}, s16[272,640]{1,0:T(8,128)(2,1)}, s16[272,640]{1,0:T(8,128)(2,1)}) custom-call(s32[1]{0:T(128)} %bitcast.3.place_ref, f32[512,640]{1,0:T(8,128)} %get-tuple-element.60.low_hbm, f32[512,640]{1,0:T(8,128)} %get-tuple-element.61.high_hbm, s16[528,640]{1,0:T(8,128)(2,1)} %copy-done.7, ...), custom_call_target="tpu_custom_call" | custom-call | flops 6553600 | bytes 6553600 | tf_op jit(solution)/shard_map/turn/pallas_call | solution.py:307
  163.2 1.3 collective-permute-start.15
  164.5 0.2 collective-permute-start.16
  164.7 2.5 %collective-permute-start.17 = (s16[272,640]{1,0:T(8,128)(2,1)}, s16[272,640]{1,0:T(8,128)(2,1)}, u32[]{:S(2)}, u32[]{:S(2)}) collective-permute-start(s16[272,640]{1,0:T(8,128)(2,1)} %get-tuple-element.70), channel_id=1, source_target_pairs={{0,96},{8,104},{16,112},{24,120},{32,0},{40,8},{48,16},{56,24},{64... | collective-permute-start | bytes 1044488 | tf_op jit(solution)/shard_map/ppermute | solution.py:380
  167.2 0.0 collective-permute-done.8.low_msg
  167.2 0.0 collective-permute-done.9.high_msg
  167.2 0.9 copy-done.5
  168.1 0.2 copy-done.6
  168.3 4.4 %turn.2 = (f32[256,640]{1,0:T(8,128)}, s16[272,640]{1,0:T(8,128)(2,1)}, s16[272,640]{1,0:T(8,128)(2,1)}, s16[272,640]{1,0:T(8,128)(2,1)}) custom-call(s32[1]{0:T(128)} %bitcast.2.place_ref, f32[512,640]{1,0:T(8,128)} %get-tuple-element.55.low_hbm, f32[512,640]{1,0:T(8,128)} %get-tuple-element.56.high_hbm, s16[528,640]{1,0:T(8,128)(2,1)} %copy-done.5, ...), custom_call_target="tpu_custom_call" | custom-call | flops 6553600 | bytes 6553600 | tf_op jit(solution)/shard_map/turn/pallas_call | solution.py:307
  172.8 0.6 collective-permute-start.12
  173.4 1.6 collective-permute-start.13
  175.0 0.0 collective-permute-done.15.rest_5_
  175.0 0.7 copy-done.3
  175.7 1.1 collective-permute-start.14
  176.8 2.0 convolution_multiply_fusion.text_ref
  178.8 2.4 %collective-permute-done.16.rest_6_ = s16[272,640]{1,0:T(8,128)(2,1)} collective-permute-done((s16[272,640]{1,0:T(8,128)(2,1)}, s16[272,640]{1,0:T(8,128)(2,1)}, u32[]{:S(2)}, u32[]{:S(2)}) %collective-permute-start.16) | collective-permute-done | bytes 348192 | tf_op jit(solution)/shard_map/ppermute | solution.py:380
  181.2 2.1 collective-permute-done.12.rest_2_
  183.3 8.9 %collective-permute-done.13.rest_3_ = s16[272,640]{1,0:T(8,128)(2,1)} collective-permute-done((s16[272,640]{1,0:T(8,128)(2,1)}, s16[272,640]{1,0:T(8,128)(2,1)}, u32[]{:S(2)}, u32[]{:S(2)}) %collective-permute-start.13) | collective-permute-done | bytes 348192 | tf_op jit(solution)/shard_map/ppermute | solution.py:380
  192.2 0.0 collective-permute-done.14.rest_4_
  192.2 2.4 %close.1 = (f32[256,1280]{1,0:T(8,128)S(1)}, f32[2,256]{1,0:T(2,128)S(1)}) custom-call(f32[256,1280]{1,0:T(8,128)S(1)} %convolution_multiply_fusion.text_ref, f32[256,640]{1,0:T(8,128)S(1)} %copy-done.2, f32[256,640]{1,0:T(8,128)S(1)} %copy-done.1, s16[272,640]{1,0:T(8,128)(2,1)} %collective-permute-done.12.rest_2_, ...), custom_call_target="tpu_custom_call" | custom-call | flops 4915200 | bytes 6553600 | tf_op jit(solution)/shard_map/close/pallas_call | solution.py:344
  194.6 15.4 %all-gather.1.stats_ref = f32[8,2,256]{2,1,0:T(2,128)S(1)} all-gather(f32[1,2,256]{2,1,0:T(2,128)S(1)} %bitcast.10), channel_id=2, replica_groups=mesh['cache'=16,'cls'=8] {'cls'}, dimensions={0}, use_global_device_ids=true | all-gather | bytes 18432 | tf_op jit(solution)/shard_map/all_gather | solution.py:442
  210.0 1.3 finish.1
  (32 shorter events, 0.1 us)
Async XLA Ops:
  6.5 170.3 %copy-start = (bf16[1280,1024]{1,0:T(8,128)(2,1)S(1)}, bf16[1280,1024]{1,0:T(8,128)(2,1)}, u32[]{:S(2)}) copy-start(bf16[1280,1024]{1,0:T(8,128)(2,1)} %param.7) | copy-start | bytes 7864324
  6.5 77.7 %all-gather.4.cloned.1.call-start = ((), (), s32[]{:S(2)}) async-start(), calls=%async_computation | async-start | bytes 8454144 | tf_op jit(solution)/shard_map/all_gather | solution.py:389
  97.8 19.4 %collective-permute-start = (s16[528,640]{1,0:T(8,128)(2,1)}, s16[528,640]{1,0:T(8,128)(2,1)S(1)}, u32[]{:S(2)}, u32[]{:S(2)}) collective-permute-start(s16[528,640]{1,0:T(8,128)(2,1)} %get-tuple-element.46), channel_id=1, source_target_pairs={{0,32},{8,40},{16,48},{24,56},{32,64},{40,72},{48,80},{56,88},{64,... | collective-permute-start | bytes 2027528 | tf_op jit(solution)/shard_map/ppermute | solution.py:380
  97.9 20.8 %collective-permute-start.1 = (s16[528,640]{1,0:T(8,128)(2,1)}, s16[528,640]{1,0:T(8,128)(2,1)S(1)}, u32[]{:S(2)}, u32[]{:S(2)}) collective-permute-start(s16[528,640]{1,0:T(8,128)(2,1)} %get-tuple-element.47), channel_id=1, source_target_pairs={{0,96},{8,104},{16,112},{24,120},{32,0},{40,8},{48,16},{56,24},{64... | collective-permute-start | bytes 2027528 | tf_op jit(solution)/shard_map/ppermute | solution.py:380
  100.6 20.1 %collective-permute-start.2 = (s16[528,640]{1,0:T(8,128)(2,1)}, s16[528,640]{1,0:T(8,128)(2,1)}, u32[]{:S(2)}, u32[]{:S(2)}) collective-permute-start(s16[528,640]{1,0:T(8,128)(2,1)} %get-tuple-element.48), channel_id=1, source_target_pairs={{0,8},{8,16},{16,24},{24,0},{32,40},{40,48},{48,56},{56,32},{64,72... | collective-permute-start | bytes 2027528 | tf_op jit(solution)/shard_map/ppermute | solution.py:380
  101.6 19.1 %collective-permute-start.3 = (s16[528,640]{1,0:T(8,128)(2,1)}, s16[528,640]{1,0:T(8,128)(2,1)}, u32[]{:S(2)}, u32[]{:S(2)}) collective-permute-start(s16[528,640]{1,0:T(8,128)(2,1)} %get-tuple-element.49), channel_id=1, source_target_pairs={{0,24},{8,0},{16,8},{24,16},{32,56},{40,32},{48,40},{56,48},{64,88... | collective-permute-start | bytes 2027528 | tf_op jit(solution)/shard_map/ppermute | solution.py:380
  117.1 18.7 %collective-permute-start.4 = (s16[528,640]{1,0:T(8,128)(2,1)}, s16[528,640]{1,0:T(8,128)(2,1)S(1)}, u32[]{:S(2)}, u32[]{:S(2)}) collective-permute-start(s16[528,640]{1,0:T(8,128)(2,1)} %get-tuple-element.51), channel_id=1, source_target_pairs={{0,96},{8,104},{16,112},{24,120},{32,0},{40,8},{48,16},{56,24},{64... | collective-permute-start | bytes 2027528 | tf_op jit(solution)/shard_map/ppermute | solution.py:380
  117.2 3.5 %copy-start.12 = (s16[528,640]{1,0:T(8,128)(2,1)}, s16[528,640]{1,0:T(8,128)(2,1)S(1)}, u32[]{:S(2)}) copy-start(s16[528,640]{1,0:T(8,128)(2,1)S(1)} %collective-permute-done.rest_0_) | copy-start | bytes 2027524
  117.2 21.2 %collective-permute-start.5 = (s16[528,640]{1,0:T(8,128)(2,1)}, s16[528,640]{1,0:T(8,128)(2,1)S(1)}, u32[]{:S(2)}, u32[]{:S(2)}) collective-permute-start(s16[528,640]{1,0:T(8,128)(2,1)} %get-tuple-element.52), channel_id=1, source_target_pairs={{0,32},{8,40},{16,48},{24,56},{32,64},{40,72},{48,80},{56,88},{64,... | collective-permute-start | bytes 2027528 | tf_op jit(solution)/shard_map/ppermute | solution.py:380
  118.7 2.0 copy-start.13
  118.7 20.7 %collective-permute-start.6 = (s16[528,640]{1,0:T(8,128)(2,1)}, s16[528,640]{1,0:T(8,128)(2,1)S(1)}, u32[]{:S(2)}, u32[]{:S(2)}) collective-permute-start(s16[528,640]{1,0:T(8,128)(2,1)} %get-tuple-element.53), channel_id=1, source_target_pairs={{0,24},{8,0},{16,8},{24,16},{32,56},{40,32},{48,40},{56,48},{64,88... | collective-permute-start | bytes 2027528 | tf_op jit(solution)/shard_map/ppermute | solution.py:380
  120.7 23.5 %collective-permute-start.7 = (s16[528,640]{1,0:T(8,128)(2,1)}, s16[528,640]{1,0:T(8,128)(2,1)}, u32[]{:S(2)}, u32[]{:S(2)}) collective-permute-start(s16[528,640]{1,0:T(8,128)(2,1)} %get-tuple-element.54), channel_id=1, source_target_pairs={{0,8},{8,16},{16,24},{24,0},{32,40},{40,48},{48,56},{56,32},{64,72... | collective-permute-start | bytes 2027528 | tf_op jit(solution)/shard_map/ppermute | solution.py:380
  135.7 21.9 %collective-permute-start.10 = (s16[528,640]{1,0:T(8,128)(2,1)}, s16[528,640]{1,0:T(8,128)(2,1)S(1)}, u32[]{:S(2)}, u32[]{:S(2)}) collective-permute-start(s16[528,640]{1,0:T(8,128)(2,1)} %get-tuple-element.62), channel_id=1, source_target_pairs={{0,8},{8,16},{16,24},{24,0},{32,40},{40,48},{48,56},{56,32},{64,72... | collective-permute-start | bytes 2027528 | tf_op jit(solution)/shard_map/ppermute | solution.py:380
  135.8 8.3 %copy-start.9 = (s16[528,640]{1,0:T(8,128)(2,1)}, s16[528,640]{1,0:T(8,128)(2,1)S(1)}, u32[]{:S(2)}) copy-start(s16[528,640]{1,0:T(8,128)(2,1)S(1)} %collective-permute-done.4.rest_0_) | copy-start | bytes 2027524
  135.8 21.8 %collective-permute-start.11 = (s16[528,640]{1,0:T(8,128)(2,1)}, s16[528,640]{1,0:T(8,128)(2,1)S(1)}, u32[]{:S(2)}, u32[]{:S(2)}) collective-permute-start(s16[528,640]{1,0:T(8,128)(2,1)} %get-tuple-element.63), channel_id=1, source_target_pairs={{0,24},{8,0},{16,8},{24,16},{32,56},{40,32},{48,40},{56,48},{64,88... | collective-permute-start | bytes 2027528 | tf_op jit(solution)/shard_map/ppermute | solution.py:380
  138.5 0.9 copy-start.10
  139.4 27.8 %collective-permute-start.8 = (s16[528,640]{1,0:T(8,128)(2,1)}, s16[528,640]{1,0:T(8,128)(2,1)S(1)}, u32[]{:S(2)}, u32[]{:S(2)}) collective-permute-start(s16[528,640]{1,0:T(8,128)(2,1)} %get-tuple-element.57), channel_id=1, source_target_pairs={{0,32},{8,40},{16,48},{24,56},{32,64},{40,72},{48,80},{56,88},{64,... | collective-permute-start | bytes 2027528 | tf_op jit(solution)/shard_map/ppermute | solution.py:380
  139.4 0.8 copy-start.11
  140.3 26.9 %collective-permute-start.9 = (s16[528,640]{1,0:T(8,128)(2,1)}, s16[528,640]{1,0:T(8,128)(2,1)S(1)}, u32[]{:S(2)}, u32[]{:S(2)}) collective-permute-start(s16[528,640]{1,0:T(8,128)(2,1)} %get-tuple-element.58), channel_id=1, source_target_pairs={{0,96},{8,104},{16,112},{24,120},{32,0},{40,8},{48,16},{56,24},{64... | collective-permute-start | bytes 2027528 | tf_op jit(solution)/shard_map/ppermute | solution.py:380
  157.6 0.9 copy-start.7
  157.7 1.1 copy-start.8
  163.2 11.8 %collective-permute-start.15 = (s16[272,640]{1,0:T(8,128)(2,1)}, s16[272,640]{1,0:T(8,128)(2,1)S(1)}, u32[]{:S(2)}, u32[]{:S(2)}) collective-permute-start(s16[272,640]{1,0:T(8,128)(2,1)} %get-tuple-element.68), channel_id=1, source_target_pairs={{0,64},{8,72},{16,80},{24,88},{32,96},{40,104},{48,112},{56,120},{... | collective-permute-start | bytes 1044488 | tf_op jit(solution)/shard_map/ppermute | solution.py:380
  164.5 16.7 %collective-permute-start.16 = (s16[272,640]{1,0:T(8,128)(2,1)}, s16[272,640]{1,0:T(8,128)(2,1)}, u32[]{:S(2)}, u32[]{:S(2)}) collective-permute-start(s16[272,640]{1,0:T(8,128)(2,1)} %get-tuple-element.69), channel_id=1, source_target_pairs={{0,32},{8,40},{16,48},{24,56},{32,64},{40,72},{48,80},{56,88},{64,... | collective-permute-start | bytes 1044488 | tf_op jit(solution)/shard_map/ppermute | solution.py:380
  164.7 16.5 %collective-permute-start.17 = (s16[272,640]{1,0:T(8,128)(2,1)}, s16[272,640]{1,0:T(8,128)(2,1)}, u32[]{:S(2)}, u32[]{:S(2)}) collective-permute-start(s16[272,640]{1,0:T(8,128)(2,1)} %get-tuple-element.70), channel_id=1, source_target_pairs={{0,96},{8,104},{16,112},{24,120},{32,0},{40,8},{48,16},{56,24},{64... | collective-permute-start | bytes 1044488 | tf_op jit(solution)/shard_map/ppermute | solution.py:380
  167.2 0.9 copy-start.5
  167.2 1.1 copy-start.6
  172.8 19.4 %copy-start.1 = (f32[256,640]{1,0:T(8,128)S(1)}, f32[256,640]{1,0:T(8,128)}, u32[]{:S(2)}) copy-start(f32[256,640]{1,0:T(8,128)} %get-tuple-element.64.rest_1_) | copy-start | bytes 1966084
  172.8 10.5 %collective-permute-start.12 = (s16[272,640]{1,0:T(8,128)(2,1)}, s16[272,640]{1,0:T(8,128)(2,1)}, u32[]{:S(2)}, u32[]{:S(2)}) collective-permute-start(s16[272,640]{1,0:T(8,128)(2,1)} %get-tuple-element.65), channel_id=1, source_target_pairs={{0,16},{8,24},{16,0},{24,8},{32,48},{40,56},{48,32},{56,40},{64,80... | collective-permute-start | bytes 1044488 | tf_op jit(solution)/shard_map/ppermute | solution.py:380
  173.4 18.8 %collective-permute-start.13 = (s16[272,640]{1,0:T(8,128)(2,1)}, s16[272,640]{1,0:T(8,128)(2,1)}, u32[]{:S(2)}, u32[]{:S(2)}) collective-permute-start(s16[272,640]{1,0:T(8,128)(2,1)} %get-tuple-element.66), channel_id=1, source_target_pairs={{0,8},{8,16},{16,24},{24,0},{32,40},{40,48},{48,56},{56,32},{64,72... | collective-permute-start | bytes 1044488 | tf_op jit(solution)/shard_map/ppermute | solution.py:380
  175.0 0.7 copy-start.3
  175.7 16.5 %collective-permute-start.14 = (s16[272,640]{1,0:T(8,128)(2,1)}, s16[272,640]{1,0:T(8,128)(2,1)}, u32[]{:S(2)}, u32[]{:S(2)}) collective-permute-start(s16[272,640]{1,0:T(8,128)(2,1)} %get-tuple-element.67), channel_id=1, source_target_pairs={{0,24},{8,0},{16,8},{24,16},{32,56},{40,32},{48,40},{56,48},{64,88... | collective-permute-start | bytes 1044488 | tf_op jit(solution)/shard_map/ppermute | solution.py:380
  176.8 15.4 %copy-start.2 = (f32[256,640]{1,0:T(8,128)S(1)}, f32[256,640]{1,0:T(8,128)}, u32[]{:S(2)}) copy-start(f32[256,640]{1,0:T(8,128)} %get-tuple-element.59.rest_0_) | copy-start | bytes 1966084
  176.8 15.4 %copy-start.4 = (s16[272,640]{1,0:T(8,128)(2,1)S(1)}, s16[272,640]{1,0:T(8,128)(2,1)}, u32[]{:S(2)}) copy-start(s16[272,640]{1,0:T(8,128)(2,1)} %copy-done.3) | copy-start | bytes 1044484
Sparse Core Ops, SparseCore 0:
  10.3 73.8 all-gather.3
where the time goes:
time: 219 us; the launch traced here: 218 us
  Pallas kernels  78 us (36%)
  waiting for transfers between devices  41 us (19%)
  local copies, waits for them, and re-layouts  26.6 us (12%)
  starting transfers between devices  22.8 us (10%)
  between operations  20.3 us (9%)
  blocking collectives  15.4 us (7%)
  other arithmetic  12 us (5%)
    pallas_call x4, Pallas kernels, sums(): pl.pallas_call(kernel, in_specs=[smem] + [anywhere] * (3 + joined), out_s...  55.9 us
    all_gather x1, waiting for transfers between devices, per_device(): lax.all_gather(unit_rows(queries), ('cache', 'cls'), axis=0, tiled=True)  27.6 us
    ppermute x18, starting transfers between devices, send(): return lax.ppermute(message, 'cache', shifted(dx, dz))  22.8 us
    gather x1, local copies, waits for them, and re-layouts, per_device(): rows = jnp.take(cache_keys, picked % 16384, axis=0, mode='clip')  21.8 us
    all_gather x1, blocking collectives, per_device(): return finish(logits, lax.all_gather(stats, 'cls'))  15.4 us
    ppermute x18, waiting for transfers between devices, send(): return lax.ppermute(message, 'cache', shifted(dx, dz))  13.4 us
    pallas_call x1, Pallas kernels, prepare(): pl.pallas_call(prepare_kernel, grid=(count // KT,), in_specs=[pl.BlockSpe...  9.46 us
    pallas_call x2, Pallas kernels, turn(): pl.pallas_call(kernel, in_specs=[pl.BlockSpec(memory_space=pltpu.SMEM)] +...  8.94 us
  transfers between devices with their start and end apart: 19, of which 4 were waited for; matrix products, arithmetic and copies ran while one was open for 15% of the time, Pallas kernels for 28%

commit v1 on v0

--- a/solution.py
+++ b/solution.py
@@ -1,3 +1,5 @@
+import math
+
 import jax
 import jax.numpy as jnp
 from jax import lax
@@ -15,7 +17,7 @@
 TAIL = 16
 
 
-def params(mib=58):
+def params(mib=36):
     return pltpu.CompilerParams(vmem_limit_bytes=mib * 1024 * 1024)
 
 
@@ -26,34 +28,39 @@
     )
 
 
-def prepare_kernel(rows_ref, labels_ref, unit_ref, hot_ref):
+def prepare_kernel(facts_ref, rows_ref, labels_ref, unit_ref, hot_ref, next_ref):
+    for at in range(4):
+        next_ref[at] = facts_ref[at]
     unit_ref[...] = unit_rows(rows_ref[...])
     classes = lax.broadcasted_iota(jnp.int32, (KT, CB), 1)
     labels = jnp.sum(jnp.where(diagonal(), labels_ref[0], 0), axis=1, keepdims=True)
     hot_ref[...] = jnp.where(labels == classes, 1.0, 0.0).astype(jnp.bfloat16)
 
 
-def prepare(rows, labels):
+def prepare(facts, rows, labels):
     count, width = rows.shape
     return pl.pallas_call(
         prepare_kernel,
         grid=(count // KT,),
         in_specs=[
+            pl.BlockSpec(memory_space=pltpu.SMEM),
             pl.BlockSpec((KT, width), lambda i: (i, 0)),
             pl.BlockSpec((1, 1, KT), lambda i: (i, 0, 0)),
         ],
         out_specs=[
             pl.BlockSpec((KT, width), lambda i: (i, 0)),
             pl.BlockSpec((KT, CB), lambda i: (i, 0)),
+            pl.BlockSpec(memory_space=pltpu.SMEM),
         ],
         out_shape=[
             jax.ShapeDtypeStruct((count, width), jnp.bfloat16),
             jax.ShapeDtypeStruct((count, CB), jnp.bfloat16),
+            jax.ShapeDtypeStruct((4,), jnp.int32),
         ],
         compiler_params=params(),
         cost_estimate=pl.CostEstimate(flops=count * width * 4, bytes_accessed=count * width * 6, transcendentals=count),
         name="prepare",
-    )(rows, labels.reshape(count // KT, 1, KT))
+    )(facts, rows, labels.reshape(count // KT, 1, KT))
 
 
 def aligned(value):
@@ -105,16 +112,16 @@
 
 def super_sums(tiles, wait_keys, wait_hots, q_ref, keys_ref, hot_ref, scores_ref, total_ref):
     width = q_ref.shape[-1]
-    sharpness = float(width) ** 0.5
+    sharpness = float(width) ** 0.5 * math.log2(math.e)
     queries = q_ref[...].reshape(SUPER, width)
 
     def step(t, carry):
         wait_keys(t)
-        keys = keys_ref[pl.ds(aligned(t * KT), KT), :]
+        at = pl.ds(aligned(t * KT), KT)
         cosine = lax.dot_general(
-            queries, keys, (((1,), (1,)), ((), ())), preferred_element_type=jnp.float32
+            queries, keys_ref[at, :], (((1,), (1,)), ((), ())), preferred_element_type=jnp.float32
         )
-        scores_ref[:, pl.ds(aligned(t * KT), KT)] = jnp.exp(sharpness * cosine).astype(jnp.bfloat16)
+        scores_ref[:, at] = jnp.exp2(sharpness * cosine).astype(jnp.bfloat16)
         return carry
 
     lax.fori_loop(0, tiles, step, 0)
@@ -181,7 +188,7 @@
             copy_hots(block).start()
         for at in range(joined):
             copy_came(at).start()
-        scores_ref[...] = jnp.zeros_like(scores_ref)
+        scores_ref[:, COMMON * KT :] = jnp.zeros((SUPER, CAP - COMMON * KT), jnp.bfloat16)
         if coded:
             for at in range(4):
                 clear_tail(msg_ref.at[at], HALF)
@@ -347,7 +354,7 @@
             jax.ShapeDtypeStruct((QT, 2 * CB), jnp.float32),
             jax.ShapeDtypeStruct((2, QT), jnp.float32),
         ],
-        compiler_params=params(24),
+        compiler_params=params(),
         cost_estimate=pl.CostEstimate(flops=30 * QT * CB, bytes_accessed=40 * QT * CB, transcendentals=QT * CB),
         name="close",
     )(text, own_a, own_b, *msgs_a, *msgs_b)
@@ -365,7 +372,7 @@
     return pl.pallas_call(
         kernel,
         out_shape=jax.ShapeDtypeStruct(logits.shape, jnp.float32),
-        compiler_params=params(24),
+        compiler_params=params(),
         name="finish",
     )(logits, stats)
 
@@ -386,7 +393,8 @@
     x, z = own // SIDE, own % SIDE
     low = lax.axis_index("cls") * (2 * CB)
 
-    gathered = lax.all_gather(unit_rows(queries), ("cache", "cls"), axis=0, tiled=True)
+    unit_queries = unit_rows(queries)
+    gathered = lax.all_gather(unit_queries, ("cache", "cls"), axis=0, tiled=True)
 
     order = lax.sort(labels * 16384 + lax.iota(jnp.int32, labels.shape[0]), is_stable=False)
     start = jnp.sum((labels < low).astype(jnp.int32))
@@ -402,11 +410,18 @@
     valid = place - block * CAP < jnp.where(block == 0, counts[0], counts[1])
     local = jnp.where(valid, picked // 16384 - low - block * CB, -1)
     rows = jnp.take(cache_keys, picked % 16384, axis=0, mode="clip")
-    keys, hots = prepare(rows, local)
-    tiles = (counts + KT - 1) // KT
-    gathered, keys, hots = lax.optimization_barrier((gathered, keys, hots))
+    text = text_scale * lax.dot_general(
+        lax.all_gather(unit_queries, "cls", axis=0, tiled=True),
+        prototypes,
+        (((1,), (1,)), ((), ())),
+        preferred_element_type=jnp.float32,
+    )
+    rows, text = lax.optimization_barrier((rows, text))
+    tiles = jnp.maximum((counts + KT - 1) // KT, COMMON)
+    facts = jnp.stack([x, z, tiles[0], tiles[1]]).astype(jnp.int32)
+    keys, hots, facts = prepare(facts, rows, local)
+    gathered, facts = lax.optimization_barrier((gathered, facts))
     q3 = gathered.reshape(SIDE * SIDE, QT, width)
-    facts = jnp.stack([x, z, tiles[0], tiles[1]]).astype(jnp.int32)
 
     def run(facts, shifts, halves, coded, arrived=()):
         *parts, facts = sums(shifts, halves, coded, facts, q3, keys, hots, arrived)
@@ -426,13 +441,6 @@
         facts, (0, 0), (0, 1), False, (free[1], free[0], free[3], free[2])
     )[0]
 
-    text = text_scale * lax.dot_general(
-        lax.dynamic_index_in_dim(q3, own, 0, keepdims=False),
-        prototypes,
-        (((1,), (1,)), ((), ())),
-        preferred_element_type=jnp.float32,
-    )
-
     own_a, a_plus, a_far, a_minus = turn(z[None], a_low, a_high, full[0], full[1])
     own_b, b_plus, b_far, b_minus = turn(x[None], b_low, b_high, full[2], full[3])
     a_msgs = send(a_far, 0, 2), send(a_plus, 0, 1), send(a_minus, 0, -1)

time: 219 us -> 211 us (0.963); the launches traced: 218 us -> 208 us
  waiting for transfers between devices: 41 us -> 25.7 us
  blocking collectives: 15.4 us -> 29.2 us
  Pallas kernels: 78 us -> 65.3 us
  local copies, waits for them, and re-layouts: 26.6 us -> 29.8 us
  starting transfers between devices: 22.8 us -> 25 us
    all_gather x1, waiting for transfers between devices: 27.6 us -> 12.2 us  [per_device(): lax.all_gather(unit_queries, ('cache', 'cls'), axis=0, tiled=True)]
    all_gather x0 -> x1, blocking collectives: none -> 15.1 us  [per_device(): lax.all_gather(unit_queries, 'cls', axis=0, tiled=True)]
    pallas_call x1, Pallas kernels: 9.46 us -> 4.21 us  [prepare(): pl.pallas_call(prepare_kernel, grid=(count // KT,), in_specs=[pl.BlockSpe...]
    pallas_call x2, Pallas kernels: 8.94 us -> 5.12 us  [turn(): pl.pallas_call(kernel, in_specs=[pl.BlockSpec(memory_space=pltpu.SMEM)] +...]
    unnamed x30 -> x16, local copies, waits for them, and re-layouts: 4.69 us -> 7.81 us
    ppermute x18, starting transfers between devices: 22.8 us -> 25 us  [send(): return lax.ppermute(message, 'cache', shifted(dx, dz))]
    pallas_call x4, Pallas kernels: 55.9 us -> 53.7 us  [sums(): pl.pallas_call(kernel, in_specs=[smem] + [anywhere] * (3 + joined), out_s...]
  transfers between devices with their start and end apart: 19 -> 19, of which waited for: 4 -> 4; matrix products, arithmetic and copies ran while one was open for 15% -> 15% of each run, Pallas kernels for 28% -> 24%
where the time goes in v1:
time: 211 us; the launch traced here: 208 us
  Pallas kernels  65.3 us (31%)
  local copies, waits for them, and re-layouts  29.8 us (14%)
  blocking collectives  29.2 us (14%)
  waiting for transfers between devices  25.7 us (12%)
  starting transfers between devices  25 us (12%)
  between operations  19.9 us (9%)
  other arithmetic  10.8 us (5%)
    pallas_call x4, Pallas kernels, sums(): pl.pallas_call(kernel, in_specs=[smem] + [anywhere] * (3 + joined), out_s...  53.7 us
    ppermute x18, starting transfers between devices, send(): return lax.ppermute(message, 'cache', shifted(dx, dz))  25 us
    gather x1, local copies, waits for them, and re-layouts, per_device(): rows = jnp.take(cache_keys, picked % 16384, axis=0, mode='clip')  21.9 us
    all_gather x1, blocking collectives, per_device(): lax.all_gather(unit_queries, 'cls', axis=0, tiled=True)  15.1 us
    all_gather x1, blocking collectives, per_device(): return finish(logits, lax.all_gather(stats, 'cls'))  14 us
    ppermute x18, waiting for transfers between devices, send(): return lax.ppermute(message, 'cache', shifted(dx, dz))  13.5 us
    all_gather x1, waiting for transfers between devices, per_device(): lax.all_gather(unit_queries, ('cache', 'cls'), axis=0, tiled=True)  12.2 us
    unnamed x16, local copies, waits for them, and re-layouts  7.81 us
  transfers between devices with their start and end apart: 19, of which 4 were waited for; matrix products, arithmetic and copies ran while one was open for 15% of the time, Pallas kernels for 24%

profile of v1, /device:TPU:1, one launch (start us, length us, event | category | flops | bytes accessed | tf_op | source)
XLA Modules:
  0.0 207.7 jit_solution(15104212854631250799)
XLA Ops:
  6.5 1.1 fusion
  7.7 1.6 fusion.1
  9.2 0.0 all-gather.4.cloned.1.call-update
  9.3 1.5 convert_reduce_fusion
  15.8 6.3 %sort.7 = s32[10240]{0:T(1024)S(1)} sort(s32[10240]{0:T(1024)S(1)} %get-tuple-element.82), dimensions={0}, to_apply=%region_0.1 | sort | flops 143360 | bytes 81920 | tf_op jit(solution)/shard_map/sort | solution.py:399
  23.4 0.1 pad_dynamic-slice_fusion
  23.5 0.1 fusion.2
  23.6 21.9 %gather_fusion = bf16[2560,1024]{1,0:T(8,128)(2,1)} fusion(bf16[10240,1024]{1,0:T(8,128)(2,1)} %param.5, s32[3072]{0:T(1024)S(1)} %pad_clamp_fusion), kind=kCustom, calls=%fused_computation | custom fusion | bytes 10496000 | tf_op jit(solution)/shard_map/jit(_take)/gather | solution.py:412
  45.5 15.1 %all_gather.12 = bf16[256,1024]{1,0:T(8,128)(2,1)S(1)} all-gather(bf16[32,1024]{1,0:T(8,128)(2,1)S(1)} %copy-done.6), channel_id=1, replica_groups=mesh['cache'=16,'cls'=8] {'cls'}, dimensions={0}, use_global_device_ids=true | all-gather | bytes 589824 | tf_op jit(solution)/shard_map/all_gather | solution.py:414
  60.6 1.9 convolution_multiply_fusion.text_ref
  62.6 0.1 fusion.4
  62.6 0.1 pad_add_fusion.facts_ref
  62.7 0.1 compare_select_fusion.2.labels_ref
  62.8 2.9 %copy-done.2 = bf16[2560,1024]{1,0:T(8,128)(2,1)S(1)} copy-done((bf16[2560,1024]{1,0:T(8,128)(2,1)S(1)}, bf16[2560,1024]{1,0:T(8,128)(2,1)}, u32[]{:S(2)}) %copy-start.2) | copy-done | bytes 5242904
  65.7 4.2 %prepare.1 = (bf16[2560,1024]{1,0:T(8,128)(2,1)S(1)}, bf16[2560,640]{1,0:T(8,128)(2,1)S(1)}, s32[4]{0:T(128)S(1)}) custom-call(s32[4]{0:T(128)S(1)} %pad_add_fusion.facts_ref, bf16[2560,1024]{1,0:T(8,128)(2,1)S(1)} %copy-done.2, s32[10,1,256]{2,1,0:T(1,128)S(1)} %compare_select_fusion.2.labels_ref), custom_call_target="tpu_custom_call" | custom-call | flops 10485760 | bytes 15728640 | tf_op jit(solution)/shard_map/prepare/pallas_call | solution.py:42
  69.9 2.4 %copy-done.4 = bf16[2560,1024]{1,0:T(8,128)(2,1)} copy-done((bf16[2560,1024]{1,0:T(8,128)(2,1)}, bf16[2560,1024]{1,0:T(8,128)(2,1)S(1)}, u32[]{:S(2)}) %copy-start.4) | copy-done | bytes 5242904
  72.3 12.2 %all-gather.4.cloned.1.call-done = bf16[4096,1024]{1,0:T(8,128)(2,1)} async-done(((bf16[32,1024]{1,0:T(8,128)(2,1)}), bf16[4096,1024]{1,0:T(8,128)(2,1)}) %all-gather.4.cloned.1.call-update) | async-done | bytes 8388624 | tf_op jit(solution)/shard_map/all_gather | solution.py:397
  84.6 2.5 %copy-done.5 = bf16[2560,1024]{1,0:T(8,128)(2,1)S(1)} copy-done((bf16[2560,1024]{1,0:T(8,128)(2,1)S(1)}, bf16[2560,1024]{1,0:T(8,128)(2,1)}, u32[]{:S(2)}) %copy-start.5) | copy-done | bytes 5242904
  87.1 13.3 %sums.4 = (s16[528,640]{1,0:T(8,128)(2,1)S(1)}, s16[528,640]{1,0:T(8,128)(2,1)S(1)}, s16[528,640]{1,0:T(8,128)(2,1)S(1)}, s16[528,640]{1,0:T(8,128)(2,1)S(1)}, s32[4]{0:T(128)S(1)}) custom-call(s32[4]{0:T(128)S(1)} %get-tuple-element.44.facts_ref, bf16[16,256,1024]{2,1,0:T(8,128)(2,1)} %bitcast.9, bf16[2560,1024]{1,0:T(8,128)(2,1)S(1)} %copy-done.5, ...), custom_call_target="tpu_custom_call" | custom-call | flops 8724152320 | bytes 4194304 | tf_op jit(solution)/shard_map/sums/pallas_call | solution.py:241
  100.4 0.1 collective-permute-start
  100.4 2.7 %collective-permute-start.1 = (s16[528,640]{1,0:T(8,128)(2,1)S(1)}, s16[528,640]{1,0:T(8,128)(2,1)S(1)}, u32[]{:S(2)}, u32[]{:S(2)}) collective-permute-start(s16[528,640]{1,0:T(8,128)(2,1)S(1)} %get-tuple-element.51), channel_id=1, source_target_pairs={{0,96},{8,104},{16,112},{24,120},{32,0},{40,8},{48,16},{56,24},{64... | collective-permute-start | bytes 2027528 | tf_op jit(solution)/shard_map/ppermute | solution.py:387
  103.1 0.0 collective-permute-start.2
  103.1 2.7 %collective-permute-start.3 = (s16[528,640]{1,0:T(8,128)(2,1)S(1)}, s16[528,640]{1,0:T(8,128)(2,1)S(1)}, u32[]{:S(2)}, u32[]{:S(2)}) collective-permute-start(s16[528,640]{1,0:T(8,128)(2,1)S(1)} %get-tuple-element.53), channel_id=1, source_target_pairs={{0,24},{8,0},{16,8},{24,16},{32,56},{40,32},{48,40},{56,48},{64,88... | collective-permute-start | bytes 2027528 | tf_op jit(solution)/shard_map/ppermute | solution.py:387
  105.8 13.4 %sums.5 = (s16[528,640]{1,0:T(8,128)(2,1)S(1)}, s16[528,640]{1,0:T(8,128)(2,1)S(1)}, s16[528,640]{1,0:T(8,128)(2,1)S(1)}, s16[528,640]{1,0:T(8,128)(2,1)S(1)}, s32[4]{0:T(128)S(1)}) custom-call(s32[4]{0:T(128)S(1)} %get-tuple-element.48.facts_ref, bf16[16,256,1024]{2,1,0:T(8,128)(2,1)} %bitcast.10, bf16[2560,1024]{1,0:T(8,128)(2,1)S(1)} %copy-done.5, ...), custom_call_target="tpu_custom_call" | custom-call | flops 8724152320 | bytes 4194304 | tf_op jit(solution)/shard_map/sums/pallas_call | solution.py:241
  119.2 0.3 collective-permute-start.4
  119.5 0.0 collective-permute-done.rest_0_
  119.5 1.2 collective-permute-start.5
  120.8 0.0 collective-permute-done.1.rest_1_
  120.8 2.6 %collective-permute-start.6 = (s16[528,640]{1,0:T(8,128)(2,1)S(1)}, s16[528,640]{1,0:T(8,128)(2,1)S(1)}, u32[]{:S(2)}, u32[]{:S(2)}) collective-permute-start(s16[528,640]{1,0:T(8,128)(2,1)S(1)} %get-tuple-element.57), channel_id=1, source_target_pairs={{0,24},{8,0},{16,8},{24,16},{32,56},{40,32},{48,40},{56,48},{64,88... | collective-permute-start | bytes 2027528 | tf_op jit(solution)/shard_map/ppermute | solution.py:387
  123.3 0.0 collective-permute-done.2.rest_2_
  123.3 0.0 collective-permute-start.7
  123.3 0.0 collective-permute-done.3.rest_3_
  123.3 14.7 %sums.6 = (s16[528,640]{1,0:T(8,128)(2,1)S(1)}, s16[528,640]{1,0:T(8,128)(2,1)S(1)}, s16[528,640]{1,0:T(8,128)(2,1)S(1)}, s16[528,640]{1,0:T(8,128)(2,1)S(1)}, s32[4]{0:T(128)S(1)}) custom-call(s32[4]{0:T(128)S(1)} %get-tuple-element.49.facts_ref, bf16[16,256,1024]{2,1,0:T(8,128)(2,1)} %bitcast.11, bf16[2560,1024]{1,0:T(8,128)(2,1)S(1)} %copy-done.5, ...), custom_call_target="tpu_custom_call" | custom-call | flops 8724152320 | bytes 4194304 | tf_op jit(solution)/shard_map/sums/pallas_call | solution.py:241
  138.0 0.1 collective-permute-start.8
  138.2 0.0 collective-permute-done.4.rest_0_
  138.2 2.6 %collective-permute-start.9 = (s16[528,640]{1,0:T(8,128)(2,1)S(1)}, s16[528,640]{1,0:T(8,128)(2,1)S(1)}, u32[]{:S(2)}, u32[]{:S(2)}) collective-permute-start(s16[528,640]{1,0:T(8,128)(2,1)S(1)} %get-tuple-element.62), channel_id=1, source_target_pairs={{0,96},{8,104},{16,112},{24,120},{32,0},{40,8},{48,16},{56,24},{64... | collective-permute-start | bytes 2027528 | tf_op jit(solution)/shard_map/ppermute | solution.py:387
  140.8 0.0 collective-permute-done.5.rest_1_
  140.8 0.0 collective-permute-start.10
  140.8 0.0 collective-permute-done.6.rest_2_
  140.8 4.5 %collective-permute-start.11 = (s16[528,640]{1,0:T(8,128)(2,1)S(1)}, s16[528,640]{1,0:T(8,128)(2,1)S(1)}, u32[]{:S(2)}, u32[]{:S(2)}) collective-permute-start(s16[528,640]{1,0:T(8,128)(2,1)S(1)} %get-tuple-element.67), channel_id=1, source_target_pairs={{0,24},{8,0},{16,8},{24,16},{32,56},{40,32},{48,40},{56,48},{64,88... | collective-permute-start | bytes 2027528 | tf_op jit(solution)/shard_map/ppermute | solution.py:387
  145.3 0.0 collective-permute-done.7.rest_3_
  145.3 12.3 %sums.7 = (f32[512,640]{1,0:T(8,128)S(1)}, f32[512,640]{1,0:T(8,128)S(1)}, f32[512,640]{1,0:T(8,128)S(1)}, f32[512,640]{1,0:T(8,128)S(1)}, s32[4]{0:T(128)}) custom-call(s32[4]{0:T(128)S(1)} %get-tuple-element.54.facts_ref, bf16[16,256,1024]{2,1,0:T(8,128)(2,1)} %bitcast.12, bf16[2560,1024]{1,0:T(8,128)(2,1)S(1)} %copy-done.5, ...), custom_call_target="tpu_custom_call" | custom-call | flops 8724152320 | bytes 4194304 | tf_op jit(solution)/shard_map/sums/pallas_call | solution.py:241
  157.6 0.5 collective-permute-done.10.low_msg
  158.1 0.0 collective-permute-done.11.high_msg
  158.1 2.6 %turn.3 = (f32[256,640]{1,0:T(8,128)S(1)}, s16[272,640]{1,0:T(8,128)(2,1)S(1)}, s16[272,640]{1,0:T(8,128)(2,1)S(1)}, s16[272,640]{1,0:T(8,128)(2,1)S(1)}) custom-call(s32[1]{0:T(128)} %bitcast.1.place_ref, f32[512,640]{1,0:T(8,128)S(1)} %get-tuple-element.64.low_hbm, f32[512,640]{1,0:T(8,128)S(1)} %get-tuple-element.65.high_hbm, ...), custom_call_target="tpu_custom_call" | custom-call | flops 6553600 | bytes 6553600 | tf_op jit(solution)/shard_map/turn/pallas_call | solution.py:314
  160.7 0.0 copy-start.3
  160.7 0.1 collective-permute-start.15
  160.8 1.1 collective-permute-start.16
  161.9 2.3 %collective-permute-start.17 = (s16[272,640]{1,0:T(8,128)(2,1)S(1)}, s16[272,640]{1,0:T(8,128)(2,1)S(1)}, u32[]{:S(2)}, u32[]{:S(2)}) collective-permute-start(s16[272,640]{1,0:T(8,128)(2,1)S(1)} %get-tuple-element.74), channel_id=1, source_target_pairs={{0,96},{8,104},{16,112},{24,120},{32,0},{40,8},{48,16},{56,24},{64... | collective-permute-start | bytes 1044488 | tf_op jit(solution)/shard_map/ppermute | solution.py:387
  164.2 0.0 collective-permute-done.8.low_msg
  164.2 0.0 collective-permute-done.9.high_msg
  164.2 2.6 %turn.2 = (f32[256,640]{1,0:T(8,128)S(1)}, s16[272,640]{1,0:T(8,128)(2,1)S(1)}, s16[272,640]{1,0:T(8,128)(2,1)S(1)}, s16[272,640]{1,0:T(8,128)(2,1)S(1)}) custom-call(s32[1]{0:T(128)} %bitcast.place_ref, f32[512,640]{1,0:T(8,128)S(1)} %get-tuple-element.59.low_hbm, f32[512,640]{1,0:T(8,128)S(1)} %get-tuple-element.60.high_hbm, ...), custom_call_target="tpu_custom_call" | custom-call | flops 6553600 | bytes 6553600 | tf_op jit(solution)/shard_map/turn/pallas_call | solution.py:314
  166.8 2.1 %collective-permute-start.12 = (s16[272,640]{1,0:T(8,128)(2,1)S(1)}, s16[272,640]{1,0:T(8,128)(2,1)S(1)}, u32[]{:S(2)}, u32[]{:S(2)}) collective-permute-start(s16[272,640]{1,0:T(8,128)(2,1)S(1)} %get-tuple-element.69), channel_id=1, source_target_pairs={{0,16},{8,24},{16,0},{24,8},{32,48},{40,56},{48,32},{56,40},{64,80... | collective-permute-start | bytes 1044488 | tf_op jit(solution)/shard_map/ppermute | solution.py:387
  168.9 1.0 collective-permute-start.13
  169.9 0.0 collective-permute-done.15.rest_5_
  169.9 1.7 collective-permute-start.14
  171.6 8.2 %collective-permute-done.16.rest_6_ = s16[272,640]{1,0:T(8,128)(2,1)S(1)} collective-permute-done((s16[272,640]{1,0:T(8,128)(2,1)S(1)}, s16[272,640]{1,0:T(8,128)(2,1)S(1)}, u32[]{:S(2)}, u32[]{:S(2)}) %collective-permute-start.16) | collective-permute-done | bytes 348192 | tf_op jit(solution)/shard_map/ppermute | solution.py:387
  179.8 0.0 collective-permute-done.17.rest_7_
  179.8 0.0 collective-permute-done.12.rest_2_
  179.8 4.7 %collective-permute-done.13.rest_3_ = s16[272,640]{1,0:T(8,128)(2,1)S(1)} collective-permute-done((s16[272,640]{1,0:T(8,128)(2,1)S(1)}, s16[272,640]{1,0:T(8,128)(2,1)S(1)}, u32[]{:S(2)}, u32[]{:S(2)}) %collective-permute-start.13) | collective-permute-done | bytes 348192 | tf_op jit(solution)/shard_map/ppermute | solution.py:387
  184.5 0.0 collective-permute-done.14.rest_4_
  184.5 1.0 close.1
  185.5 14.0 %all-gather.1.stats_ref = f32[8,2,256]{2,1,0:T(2,128)S(1)} all-gather(f32[1,2,256]{2,1,0:T(2,128)S(1)} %bitcast.8), channel_id=2, replica_groups=mesh['cache'=16,'cls'=8] {'cls'}, dimensions={0}, use_global_device_ids=true | all-gather | bytes 18432 | tf_op jit(solution)/shard_map/all_gather | solution.py:450
  199.5 1.3 finish.1
  (19 shorter events, 0.1 us)
Async XLA Ops:
  6.5 54.1 %copy-start = (bf16[1280,1024]{1,0:T(8,128)(2,1)S(1)}, bf16[1280,1024]{1,0:T(8,128)(2,1)}, u32[]{:S(2)}) copy-start(bf16[1280,1024]{1,0:T(8,128)(2,1)} %param.7) | copy-start | bytes 7864324
  6.5 78.0 %all-gather.4.cloned.1.call-start = ((), (), s32[]{:S(2)}) async-start(), calls=%async_computation | async-start | bytes 8454144 | tf_op jit(solution)/shard_map/all_gather | solution.py:397
  23.6 21.9 %copy-start.6 = (bf16[32,1024]{1,0:T(8,128)(2,1)S(1)}, bf16[32,1024]{1,0:T(8,128)(2,1)}, u32[]{:S(2)}) copy-start(bf16[32,1024]{1,0:T(8,128)(2,1)} %fusion.1) | copy-start | bytes 196612
  62.8 2.9 %copy-start.2 = (bf16[2560,1024]{1,0:T(8,128)(2,1)S(1)}, bf16[2560,1024]{1,0:T(8,128)(2,1)}, u32[]{:S(2)}) copy-start(bf16[2560,1024]{1,0:T(8,128)(2,1)} %gather_fusion) | copy-start | bytes 15728644
  69.9 2.4 %copy-start.4 = (bf16[2560,1024]{1,0:T(8,128)(2,1)}, bf16[2560,1024]{1,0:T(8,128)(2,1)S(1)}, u32[]{:S(2)}) copy-start(bf16[2560,1024]{1,0:T(8,128)(2,1)S(1)} %get-tuple-element.46.keys_hbm) | copy-start | bytes 15728644
  84.6 2.5 %copy-start.5 = (bf16[2560,1024]{1,0:T(8,128)(2,1)S(1)}, bf16[2560,1024]{1,0:T(8,128)(2,1)}, u32[]{:S(2)}) copy-start(bf16[2560,1024]{1,0:T(8,128)(2,1)} %copy-done.4) | copy-start | bytes 15728644
  100.4 19.2 %collective-permute-start = (s16[528,640]{1,0:T(8,128)(2,1)S(1)}, s16[528,640]{1,0:T(8,128)(2,1)S(1)}, u32[]{:S(2)}, u32[]{:S(2)}) collective-permute-start(s16[528,640]{1,0:T(8,128)(2,1)S(1)} %get-tuple-element.50), channel_id=1, source_target_pairs={{0,32},{8,40},{16,48},{24,56},{32,64},{40,72},{48,80},{56,88},{64,... | collective-permute-start | bytes 2027528 | tf_op jit(solution)/shard_map/ppermute | solution.py:387
  100.4 20.3 %collective-permute-start.1 = (s16[528,640]{1,0:T(8,128)(2,1)S(1)}, s16[528,640]{1,0:T(8,128)(2,1)S(1)}, u32[]{:S(2)}, u32[]{:S(2)}) collective-permute-start(s16[528,640]{1,0:T(8,128)(2,1)S(1)} %get-tuple-element.51), channel_id=1, source_target_pairs={{0,96},{8,104},{16,112},{24,120},{32,0},{40,8},{48,16},{56,24},{64... | collective-permute-start | bytes 2027528 | tf_op jit(solution)/shard_map/ppermute | solution.py:387
  103.1 20.2 %collective-permute-start.2 = (s16[528,640]{1,0:T(8,128)(2,1)S(1)}, s16[528,640]{1,0:T(8,128)(2,1)S(1)}, u32[]{:S(2)}, u32[]{:S(2)}) collective-permute-start(s16[528,640]{1,0:T(8,128)(2,1)S(1)} %get-tuple-element.52), channel_id=1, source_target_pairs={{0,8},{8,16},{16,24},{24,0},{32,40},{40,48},{48,56},{56,32},{64,72... | collective-permute-start | bytes 2027528 | tf_op jit(solution)/shard_map/ppermute | solution.py:387
  103.1 20.2 %collective-permute-start.3 = (s16[528,640]{1,0:T(8,128)(2,1)S(1)}, s16[528,640]{1,0:T(8,128)(2,1)S(1)}, u32[]{:S(2)}, u32[]{:S(2)}) collective-permute-start(s16[528,640]{1,0:T(8,128)(2,1)S(1)} %get-tuple-element.53), channel_id=1, source_target_pairs={{0,24},{8,0},{16,8},{24,16},{32,56},{40,32},{48,40},{56,48},{64,88... | collective-permute-start | bytes 2027528 | tf_op jit(solution)/shard_map/ppermute | solution.py:387
  119.2 18.9 %collective-permute-start.4 = (s16[528,640]{1,0:T(8,128)(2,1)S(1)}, s16[528,640]{1,0:T(8,128)(2,1)S(1)}, u32[]{:S(2)}, u32[]{:S(2)}) collective-permute-start(s16[528,640]{1,0:T(8,128)(2,1)S(1)} %get-tuple-element.55), channel_id=1, source_target_pairs={{0,96},{8,104},{16,112},{24,120},{32,0},{40,8},{48,16},{56,24},{64... | collective-permute-start | bytes 2027528 | tf_op jit(solution)/shard_map/ppermute | solution.py:387
  119.5 21.2 %collective-permute-start.5 = (s16[528,640]{1,0:T(8,128)(2,1)S(1)}, s16[528,640]{1,0:T(8,128)(2,1)S(1)}, u32[]{:S(2)}, u32[]{:S(2)}) collective-permute-start(s16[528,640]{1,0:T(8,128)(2,1)S(1)} %get-tuple-element.56), channel_id=1, source_target_pairs={{0,32},{8,40},{16,48},{24,56},{32,64},{40,72},{48,80},{56,88},{64,... | collective-permute-start | bytes 2027528 | tf_op jit(solution)/shard_map/ppermute | solution.py:387
  120.8 20.0 %collective-permute-start.6 = (s16[528,640]{1,0:T(8,128)(2,1)S(1)}, s16[528,640]{1,0:T(8,128)(2,1)S(1)}, u32[]{:S(2)}, u32[]{:S(2)}) collective-permute-start(s16[528,640]{1,0:T(8,128)(2,1)S(1)} %get-tuple-element.57), channel_id=1, source_target_pairs={{0,24},{8,0},{16,8},{24,16},{32,56},{40,32},{48,40},{56,48},{64,88... | collective-permute-start | bytes 2027528 | tf_op jit(solution)/shard_map/ppermute | solution.py:387
  123.3 21.9 %collective-permute-start.7 = (s16[528,640]{1,0:T(8,128)(2,1)S(1)}, s16[528,640]{1,0:T(8,128)(2,1)S(1)}, u32[]{:S(2)}, u32[]{:S(2)}) collective-permute-start(s16[528,640]{1,0:T(8,128)(2,1)S(1)} %get-tuple-element.58), channel_id=1, source_target_pairs={{0,8},{8,16},{16,24},{24,0},{32,40},{40,48},{48,56},{56,32},{64,72... | collective-permute-start | bytes 2027528 | tf_op jit(solution)/shard_map/ppermute | solution.py:387
  138.0 26.2 %collective-permute-start.8 = (s16[528,640]{1,0:T(8,128)(2,1)S(1)}, s16[528,640]{1,0:T(8,128)(2,1)S(1)}, u32[]{:S(2)}, u32[]{:S(2)}) collective-permute-start(s16[528,640]{1,0:T(8,128)(2,1)S(1)} %get-tuple-element.61), channel_id=1, source_target_pairs={{0,32},{8,40},{16,48},{24,56},{32,64},{40,72},{48,80},{56,88},{64,... | collective-permute-start | bytes 2027528 | tf_op jit(solution)/shard_map/ppermute | solution.py:387
  138.2 26.0 %collective-permute-start.9 = (s16[528,640]{1,0:T(8,128)(2,1)S(1)}, s16[528,640]{1,0:T(8,128)(2,1)S(1)}, u32[]{:S(2)}, u32[]{:S(2)}) collective-permute-start(s16[528,640]{1,0:T(8,128)(2,1)S(1)} %get-tuple-element.62), channel_id=1, source_target_pairs={{0,96},{8,104},{16,112},{24,120},{32,0},{40,8},{48,16},{56,24},{64... | collective-permute-start | bytes 2027528 | tf_op jit(solution)/shard_map/ppermute | solution.py:387
  140.8 17.3 %collective-permute-start.10 = (s16[528,640]{1,0:T(8,128)(2,1)S(1)}, s16[528,640]{1,0:T(8,128)(2,1)S(1)}, u32[]{:S(2)}, u32[]{:S(2)}) collective-permute-start(s16[528,640]{1,0:T(8,128)(2,1)S(1)} %get-tuple-element.66), channel_id=1, source_target_pairs={{0,8},{8,16},{16,24},{24,0},{32,40},{40,48},{48,56},{56,32},{64,72... | collective-permute-start | bytes 2027528 | tf_op jit(solution)/shard_map/ppermute | solution.py:387
  140.8 17.3 %collective-permute-start.11 = (s16[528,640]{1,0:T(8,128)(2,1)S(1)}, s16[528,640]{1,0:T(8,128)(2,1)S(1)}, u32[]{:S(2)}, u32[]{:S(2)}) collective-permute-start(s16[528,640]{1,0:T(8,128)(2,1)S(1)} %get-tuple-element.67), channel_id=1, source_target_pairs={{0,24},{8,0},{16,8},{24,16},{32,56},{40,32},{48,40},{56,48},{64,88... | collective-permute-start | bytes 2027528 | tf_op jit(solution)/shard_map/ppermute | solution.py:387
  160.7 23.8 %copy-start.3 = (f32[256,1280]{1,0:T(8,128)S(1)}, f32[256,1280]{1,0:T(8,128)}, u32[]{:S(2)}) copy-start(f32[256,1280]{1,0:T(8,128)} %convolution_multiply_fusion.text_ref) | copy-start | bytes 3932164
  160.7 9.2 %collective-permute-start.15 = (s16[272,640]{1,0:T(8,128)(2,1)S(1)}, s16[272,640]{1,0:T(8,128)(2,1)S(1)}, u32[]{:S(2)}, u32[]{:S(2)}) collective-permute-start(s16[272,640]{1,0:T(8,128)(2,1)S(1)} %get-tuple-element.72), channel_id=1, source_target_pairs={{0,64},{8,72},{16,80},{24,88},{32,96},{40,104},{48,112},{56,120},{... | collective-permute-start | bytes 1044488 | tf_op jit(solution)/shard_map/ppermute | solution.py:387
  160.8 19.0 %collective-permute-start.16 = (s16[272,640]{1,0:T(8,128)(2,1)S(1)}, s16[272,640]{1,0:T(8,128)(2,1)S(1)}, u32[]{:S(2)}, u32[]{:S(2)}) collective-permute-start(s16[272,640]{1,0:T(8,128)(2,1)S(1)} %get-tuple-element.73), channel_id=1, source_target_pairs={{0,32},{8,40},{16,48},{24,56},{32,64},{40,72},{48,80},{56,88},{64,... | collective-permute-start | bytes 1044488 | tf_op jit(solution)/shard_map/ppermute | solution.py:387
  161.9 17.9 %collective-permute-start.17 = (s16[272,640]{1,0:T(8,128)(2,1)S(1)}, s16[272,640]{1,0:T(8,128)(2,1)S(1)}, u32[]{:S(2)}, u32[]{:S(2)}) collective-permute-start(s16[272,640]{1,0:T(8,128)(2,1)S(1)} %get-tuple-element.74), channel_id=1, source_target_pairs={{0,96},{8,104},{16,112},{24,120},{32,0},{40,8},{48,16},{56,24},{64... | collective-permute-start | bytes 1044488 | tf_op jit(solution)/shard_map/ppermute | solution.py:387
  166.8 13.0 %collective-permute-start.12 = (s16[272,640]{1,0:T(8,128)(2,1)S(1)}, s16[272,640]{1,0:T(8,128)(2,1)S(1)}, u32[]{:S(2)}, u32[]{:S(2)}) collective-permute-start(s16[272,640]{1,0:T(8,128)(2,1)S(1)} %get-tuple-element.69), channel_id=1, source_target_pairs={{0,16},{8,24},{16,0},{24,8},{32,48},{40,56},{48,32},{56,40},{64,80... | collective-permute-start | bytes 1044488 | tf_op jit(solution)/shard_map/ppermute | solution.py:387
  168.9 15.6 %collective-permute-start.13 = (s16[272,640]{1,0:T(8,128)(2,1)S(1)}, s16[272,640]{1,0:T(8,128)(2,1)S(1)}, u32[]{:S(2)}, u32[]{:S(2)}) collective-permute-start(s16[272,640]{1,0:T(8,128)(2,1)S(1)} %get-tuple-element.70), channel_id=1, source_target_pairs={{0,8},{8,16},{16,24},{24,0},{32,40},{40,48},{48,56},{56,32},{64,72... | collective-permute-start | bytes 1044488 | tf_op jit(solution)/shard_map/ppermute | solution.py:387
  169.9 14.6 %collective-permute-start.14 = (s16[272,640]{1,0:T(8,128)(2,1)S(1)}, s16[272,640]{1,0:T(8,128)(2,1)S(1)}, u32[]{:S(2)}, u32[]{:S(2)}) collective-permute-start(s16[272,640]{1,0:T(8,128)(2,1)S(1)} %get-tuple-element.71), channel_id=1, source_target_pairs={{0,24},{8,0},{16,8},{24,16},{32,56},{40,32},{48,40},{56,48},{64,88... | collective-permute-start | bytes 1044488 | tf_op jit(solution)/shard_map/ppermute | solution.py:387
  184.5 16.3 %copy-start.1 = (bf16[1280,1024]{1,0:T(8,128)(2,1)S(1)}, bf16[1280,1024]{1,0:T(8,128)(2,1)}, u32[]{:S(2)}) copy-start(bf16[1280,1024]{1,0:T(8,128)(2,1)} %param.7) | copy-start | bytes 7864324
Sparse Core Ops, SparseCore 0:
  10.3 74.2 all-gather.3

commit v2 on v1

--- a/solution.py
+++ b/solution.py
@@ -17,7 +17,7 @@
 TAIL = 16
 
 
-def params(mib=36):
+def params(mib=44):
     return pltpu.CompilerParams(vmem_limit_bytes=mib * 1024 * 1024)
 
 
@@ -61,6 +61,19 @@
         cost_estimate=pl.CostEstimate(flops=count * width * 4, bytes_accessed=count * width * 6, transcendentals=count),
         name="prepare",
     )(facts, rows, labels.reshape(count // KT, 1, KT))
+
+
+def unit_kernel(rows_ref, unit_ref):
+    unit_ref[...] = unit_rows(rows_ref[...])
+
+
+def unit_small(rows):
+    return pl.pallas_call(
+        unit_kernel,
+        out_shape=jax.ShapeDtypeStruct(rows.shape, jnp.bfloat16),
+        compiler_params=params(),
+        name="unit",
+    )(rows)
 
 
 def aligned(value):
@@ -393,7 +406,7 @@
     x, z = own // SIDE, own % SIDE
     low = lax.axis_index("cls") * (2 * CB)
 
-    unit_queries = unit_rows(queries)
+    unit_queries = unit_small(queries)
     gathered = lax.all_gather(unit_queries, ("cache", "cls"), axis=0, tiled=True)
 
     order = lax.sort(labels * 16384 + lax.iota(jnp.int32, labels.shape[0]), is_stable=False)

time: 211 us -> 207 us (0.981)
  blocking collectives: 29.2 us -> 39.9 us
  starting transfers between devices: 25 us -> 18.1 us
  Pallas kernels: 65.3 us -> 69.9 us
  local copies, waits for them, and re-layouts: 29.8 us -> 25.4 us
  waiting for transfers between devices: 25.7 us -> 22.1 us
  other arithmetic: 10.8 us -> 8.14 us
    all_gather x1, blocking collectives: 14 us -> 24.4 us  [per_device(): return finish(logits, lax.all_gather(stats, 'cls'))]
    ppermute x18, starting transfers between devices: 25 us -> 18.1 us  [send(): return lax.ppermute(message, 'cache', shifted(dx, dz))]
    unnamed x16 -> x14, local copies, waits for them, and re-layouts: 7.81 us -> 3.42 us
    pallas_call x1, Pallas kernels: 4.21 us -> 7.85 us  [prepare(): pl.pallas_call(prepare_kernel, grid=(count // KT,), in_specs=[pl.BlockSpe...]
    ppermute x18, waiting for transfers between devices: 13.5 us -> 10.1 us  [send(): return lax.ppermute(message, 'cache', shifted(dx, dz))]
  transfers between devices with their start and end apart: 19 -> 19, of which waited for: 4 -> 5; matrix products, arithmetic and copies ran while one was open for 15% -> 16% of each run, Pallas kernels for 24% -> 26%
where the time goes in v2:
time: 207 us; the launch traced here: 205 us
  Pallas kernels  69.9 us (34%)
  blocking collectives  39.9 us (19%)
  local copies, waits for them, and re-layouts  25.4 us (12%)
  waiting for transfers between devices  22.1 us (11%)
  between operations  19.9 us (10%)
  starting transfers between devices  18.1 us (9%)
  other arithmetic  8.14 us (4%)
    pallas_call x4, Pallas kernels, sums(): pl.pallas_call(kernel, in_specs=[smem] + [anywhere] * (3 + joined), out_s...  53.9 us
    all_gather x1, blocking collectives, per_device(): return finish(logits, lax.all_gather(stats, 'cls'))  24.4 us
    gather x1, local copies, waits for them, and re-layouts, per_device(): rows = jnp.take(cache_keys, picked % 16384, axis=0, mode='clip')  21.8 us
    ppermute x18, starting transfers between devices, send(): return lax.ppermute(message, 'cache', shifted(dx, dz))  18.1 us
    all_gather x1, blocking collectives, per_device(): lax.all_gather(unit_queries, 'cls', axis=0, tiled=True)  15.5 us
    all_gather x1, waiting for transfers between devices, per_device(): lax.all_gather(unit_queries, ('cache', 'cls'), axis=0, tiled=True)  11.9 us
    ppermute x18, waiting for transfers between devices, send(): return lax.ppermute(message, 'cache', shifted(dx, dz))  10.1 us
    pallas_call x1, Pallas kernels, prepare(): pl.pallas_call(prepare_kernel, grid=(count // KT,), in_specs=[pl.BlockSpe...  7.85 us
  transfers between devices with their start and end apart: 19, of which 5 were waited for; matrix products, arithmetic and copies ran while one was open for 16% of the time, Pallas kernels for 26%

profile of v2, /device:TPU:1, one launch (start us, length us, event | category | flops | bytes accessed | tf_op | source)
XLA Modules:
  0.0 205.3 jit_solution(3777769255879634492)
XLA Ops:
  6.5 0.0 all-gather.4.cloned.1.call-start
  6.5 1.0 copy-done.3
  7.5 0.7 unit.1
  8.3 0.0 all-gather.4.cloned.1.call-update
  8.3 1.5 convert_reduce_fusion
  14.8 6.3 %sort.7 = s32[10240]{0:T(1024)S(1)} sort(s32[10240]{0:T(1024)S(1)} %get-tuple-element.82), dimensions={0}, to_apply=%region_0.1 | sort | flops 143360 | bytes 81920 | tf_op jit(solution)/shard_map/sort | solution.py:412
  22.4 0.1 pad_dynamic-slice_fusion
  22.6 0.1 fusion
  22.6 21.8 %gather_fusion = bf16[2560,1024]{1,0:T(8,128)(2,1)} fusion(bf16[10240,1024]{1,0:T(8,128)(2,1)} %param.5, s32[3072]{0:T(1024)S(1)} %pad_clamp_fusion), kind=kCustom, calls=%fused_computation | custom fusion | bytes 10496000 | tf_op jit(solution)/shard_map/jit(_take)/gather | solution.py:425
  44.5 15.5 %all_gather.12 = bf16[256,1024]{1,0:T(8,128)(2,1)S(1)} all-gather(bf16[32,1024]{1,0:T(8,128)(2,1)} %unit.1), channel_id=1, replica_groups=mesh['cache'=16,'cls'=8] {'cls'}, dimensions={0}, use_global_device_ids=true | all-gather | bytes 589824 | tf_op jit(solution)/shard_map/all_gather | solution.py:427
  59.9 1.9 convolution_multiply_fusion.text_ref
  61.9 0.1 fusion.2
  62.0 0.1 pad_add_fusion.facts_ref
  62.1 0.1 compare_select_fusion.2.labels_ref
  62.1 7.8 %prepare.1 = (bf16[2560,1024]{1,0:T(8,128)(2,1)S(1)}, bf16[2560,640]{1,0:T(8,128)(2,1)S(1)}, s32[4]{0:T(128)S(1)}) custom-call(s32[4]{0:T(128)S(1)} %pad_add_fusion.facts_ref, bf16[2560,1024]{1,0:T(8,128)(2,1)} %gather_fusion, s32[10,1,256]{2,1,0:T(1,128)S(1)} %compare_select_fusion.2.labels_ref), custom_call_target="tpu_custom_call" | custom-call | flops 10485760 | bytes 15728640 | tf_op jit(solution)/shard_map/prepare/pallas_call | solution.py:42
  70.0 2.4 %copy-done.4 = bf16[2560,1024]{1,0:T(8,128)(2,1)} copy-done((bf16[2560,1024]{1,0:T(8,128)(2,1)}, bf16[2560,1024]{1,0:T(8,128)(2,1)S(1)}, u32[]{:S(2)}) %copy-start.4) | copy-done | bytes 5242904
  72.4 11.9 %all-gather.4.cloned.1.call-done = bf16[4096,1024]{1,0:T(8,128)(2,1)} async-done(((bf16[32,1024]{1,0:T(8,128)(2,1)}), bf16[4096,1024]{1,0:T(8,128)(2,1)}) %all-gather.4.cloned.1.call-update) | async-done | bytes 8388624 | tf_op jit(solution)/shard_map/all_gather | solution.py:410
  84.4 13.3 %sums.4 = (s16[528,640]{1,0:T(8,128)(2,1)S(1)}, s16[528,640]{1,0:T(8,128)(2,1)S(1)}, s16[528,640]{1,0:T(8,128)(2,1)S(1)}, s16[528,640]{1,0:T(8,128)(2,1)S(1)}, s32[4]{0:T(128)S(1)}) custom-call(s32[4]{0:T(128)S(1)} %get-tuple-element.44.facts_ref, bf16[16,256,1024]{2,1,0:T(8,128)(2,1)} %bitcast.9, bf16[2560,1024]{1,0:T(8,128)(2,1)} %copy-done.4, ...), custom_call_target="tpu_custom_call" | custom-call | flops 8724152320 | bytes 4194304 | tf_op jit(solution)/shard_map/sums/pallas_call | solution.py:254
  97.7 0.1 collective-permute-start
  97.8 2.7 %collective-permute-start.1 = (s16[528,640]{1,0:T(8,128)(2,1)S(1)}, s16[528,640]{1,0:T(8,128)(2,1)S(1)}, u32[]{:S(2)}, u32[]{:S(2)}) collective-permute-start(s16[528,640]{1,0:T(8,128)(2,1)S(1)} %get-tuple-element.51), channel_id=1, source_target_pairs={{0,96},{8,104},{16,112},{24,120},{32,0},{40,8},{48,16},{56,24},{64... | collective-permute-start | bytes 2027528 | tf_op jit(solution)/shard_map/ppermute | solution.py:400
  100.4 0.0 collective-permute-start.2
  100.5 2.6 %collective-permute-start.3 = (s16[528,640]{1,0:T(8,128)(2,1)S(1)}, s16[528,640]{1,0:T(8,128)(2,1)S(1)}, u32[]{:S(2)}, u32[]{:S(2)}) collective-permute-start(s16[528,640]{1,0:T(8,128)(2,1)S(1)} %get-tuple-element.53), channel_id=1, source_target_pairs={{0,24},{8,0},{16,8},{24,16},{32,56},{40,32},{48,40},{56,48},{64,88... | collective-permute-start | bytes 2027528 | tf_op jit(solution)/shard_map/ppermute | solution.py:400
  103.1 13.7 %sums.5 = (s16[528,640]{1,0:T(8,128)(2,1)S(1)}, s16[528,640]{1,0:T(8,128)(2,1)S(1)}, s16[528,640]{1,0:T(8,128)(2,1)S(1)}, s16[528,640]{1,0:T(8,128)(2,1)S(1)}, s32[4]{0:T(128)S(1)}) custom-call(s32[4]{0:T(128)S(1)} %get-tuple-element.48.facts_ref, bf16[16,256,1024]{2,1,0:T(8,128)(2,1)} %bitcast.10, bf16[2560,1024]{1,0:T(8,128)(2,1)} %copy-done.4, ...), custom_call_target="tpu_custom_call" | custom-call | flops 8724152320 | bytes 4194304 | tf_op jit(solution)/shard_map/sums/pallas_call | solution.py:254
  116.8 0.1 collective-permute-start.4
  116.9 0.0 collective-permute-done.rest_0_
  116.9 1.4 collective-permute-start.5
  118.3 0.0 collective-permute-done.1.rest_1_
  118.4 0.0 collective-permute-start.6
  118.4 0.0 collective-permute-done.2.rest_2_
  118.4 1.5 collective-permute-start.7
  119.8 0.0 collective-permute-done.3.rest_3_
  119.8 0.0 copy-done.5
  119.8 14.7 %sums.6 = (s16[528,640]{1,0:T(8,128)(2,1)S(1)}, s16[528,640]{1,0:T(8,128)(2,1)S(1)}, s16[528,640]{1,0:T(8,128)(2,1)S(1)}, s16[528,640]{1,0:T(8,128)(2,1)S(1)}, s32[4]{0:T(128)S(1)}) custom-call(s32[4]{0:T(128)S(1)} %get-tuple-element.49.facts_ref, bf16[16,256,1024]{2,1,0:T(8,128)(2,1)} %bitcast.11, bf16[2560,1024]{1,0:T(8,128)(2,1)} %copy-done.4, ...), custom_call_target="tpu_custom_call" | custom-call | flops 8724152320 | bytes 4194304 | tf_op jit(solution)/shard_map/sums/pallas_call | solution.py:254
  134.5 0.1 collective-permute-start.8
  134.6 0.0 collective-permute-done.4.rest_0_
  134.6 2.7 %collective-permute-start.9 = (s16[528,640]{1,0:T(8,128)(2,1)S(1)}, s16[528,640]{1,0:T(8,128)(2,1)S(1)}, u32[]{:S(2)}, u32[]{:S(2)}) collective-permute-start(s16[528,640]{1,0:T(8,128)(2,1)S(1)} %get-tuple-element.62), channel_id=1, source_target_pairs={{0,96},{8,104},{16,112},{24,120},{32,0},{40,8},{48,16},{56,24},{64... | collective-permute-start | bytes 2027528 | tf_op jit(solution)/shard_map/ppermute | solution.py:400
  137.3 0.0 collective-permute-done.5.rest_1_
  137.3 0.0 collective-permute-start.10
  137.3 0.0 collective-permute-done.6.rest_2_
  137.3 2.7 %collective-permute-start.11 = (s16[528,640]{1,0:T(8,128)(2,1)S(1)}, s16[528,640]{1,0:T(8,128)(2,1)S(1)}, u32[]{:S(2)}, u32[]{:S(2)}) collective-permute-start(s16[528,640]{1,0:T(8,128)(2,1)S(1)} %get-tuple-element.67), channel_id=1, source_target_pairs={{0,24},{8,0},{16,8},{24,16},{32,56},{40,32},{48,40},{56,48},{64,88... | collective-permute-start | bytes 2027528 | tf_op jit(solution)/shard_map/ppermute | solution.py:400
  140.0 0.0 collective-permute-done.7.rest_3_
  140.0 12.2 %sums.7 = (f32[512,640]{1,0:T(8,128)S(1)}, f32[512,640]{1,0:T(8,128)S(1)}, f32[512,640]{1,0:T(8,128)S(1)}, f32[512,640]{1,0:T(8,128)S(1)}, s32[4]{0:T(128)}) custom-call(s32[4]{0:T(128)S(1)} %get-tuple-element.54.facts_ref, bf16[16,256,1024]{2,1,0:T(8,128)(2,1)} %bitcast.12, bf16[2560,1024]{1,0:T(8,128)(2,1)} %copy-done.4, bf16[2560,640]{1,0:T(8,128)(2,1)} %copy-done.5, ...), custom_call_target="tpu_custom_call" | custom-call | flops 8724152320 | bytes 4194304 | tf_op jit(solution)/shard_map/sums/pallas_call | solution.py:254
  152.2 0.0 collective-permute-done.10.low_msg
  152.2 0.0 collective-permute-done.11.high_msg
  152.2 2.6 %turn.3 = (f32[256,640]{1,0:T(8,128)S(1)}, s16[272,640]{1,0:T(8,128)(2,1)S(1)}, s16[272,640]{1,0:T(8,128)(2,1)S(1)}, s16[272,640]{1,0:T(8,128)(2,1)S(1)}) custom-call(s32[1]{0:T(128)} %bitcast.1.place_ref, f32[512,640]{1,0:T(8,128)S(1)} %get-tuple-element.64.low_hbm, f32[512,640]{1,0:T(8,128)S(1)} %get-tuple-element.65.high_hbm, ...), custom_call_target="tpu_custom_call" | custom-call | flops 6553600 | bytes 6553600 | tf_op jit(solution)/shard_map/turn/pallas_call | solution.py:327
  154.8 0.0 copy-start.2
  154.8 0.1 collective-permute-start.15
  154.9 0.7 collective-permute-start.16
  155.6 2.0 collective-permute-start.17
  157.6 0.0 collective-permute-done.8.low_msg
  157.6 0.0 collective-permute-done.9.high_msg
  157.6 2.6 %turn.2 = (f32[256,640]{1,0:T(8,128)S(1)}, s16[272,640]{1,0:T(8,128)(2,1)S(1)}, s16[272,640]{1,0:T(8,128)(2,1)S(1)}, s16[272,640]{1,0:T(8,128)(2,1)S(1)}) custom-call(s32[1]{0:T(128)} %bitcast.place_ref, f32[512,640]{1,0:T(8,128)S(1)} %get-tuple-element.59.low_hbm, f32[512,640]{1,0:T(8,128)S(1)} %get-tuple-element.60.high_hbm, ...), custom_call_target="tpu_custom_call" | custom-call | flops 6553600 | bytes 6553600 | tf_op jit(solution)/shard_map/turn/pallas_call | solution.py:327
  160.2 0.1 collective-permute-start.12
  160.3 0.9 collective-permute-start.13
  161.2 1.4 collective-permute-done.15.rest_5_
  162.6 0.4 collective-permute-start.14
  163.0 3.3 %collective-permute-done.16.rest_6_ = s16[272,640]{1,0:T(8,128)(2,1)S(1)} collective-permute-done((s16[272,640]{1,0:T(8,128)(2,1)S(1)}, s16[272,640]{1,0:T(8,128)(2,1)S(1)}, u32[]{:S(2)}, u32[]{:S(2)}) %collective-permute-start.16) | collective-permute-done | bytes 348192 | tf_op jit(solution)/shard_map/ppermute | solution.py:400
  166.4 0.0 collective-permute-done.17.rest_7_
  166.4 1.9 collective-permute-done.12.rest_2_
  168.3 3.5 %collective-permute-done.13.rest_3_ = s16[272,640]{1,0:T(8,128)(2,1)S(1)} collective-permute-done((s16[272,640]{1,0:T(8,128)(2,1)S(1)}, s16[272,640]{1,0:T(8,128)(2,1)S(1)}, u32[]{:S(2)}, u32[]{:S(2)}) %collective-permute-start.13) | collective-permute-done | bytes 348192 | tf_op jit(solution)/shard_map/ppermute | solution.py:400
  171.7 0.0 collective-permute-done.14.rest_4_
  171.8 1.0 close.1
  172.8 24.4 %all-gather.1.stats_ref = f32[8,2,256]{2,1,0:T(2,128)S(1)} all-gather(f32[1,2,256]{2,1,0:T(2,128)S(1)} %bitcast.8), channel_id=2, replica_groups=mesh['cache'=16,'cls'=8] {'cls'}, dimensions={0}, use_global_device_ids=true | all-gather | bytes 18432 | tf_op jit(solution)/shard_map/all_gather | solution.py:463
  197.2 1.3 finish.1
  (15 shorter events, 0.1 us)
Async XLA Ops:
  6.5 53.4 %copy-start = (bf16[1280,1024]{1,0:T(8,128)(2,1)S(1)}, bf16[1280,1024]{1,0:T(8,128)(2,1)}, u32[]{:S(2)}) copy-start(bf16[1280,1024]{1,0:T(8,128)(2,1)} %param.7) | copy-start | bytes 7864324
  6.5 77.8 %all-gather.4.cloned.1.call-start = ((), (), s32[]{:S(2)}) async-start(), calls=%async_computation | async-start | bytes 8454144 | tf_op jit(solution)/shard_map/all_gather | solution.py:410
  6.5 1.0 copy-start.3
  70.0 2.4 %copy-start.4 = (bf16[2560,1024]{1,0:T(8,128)(2,1)}, bf16[2560,1024]{1,0:T(8,128)(2,1)S(1)}, u32[]{:S(2)}) copy-start(bf16[2560,1024]{1,0:T(8,128)(2,1)S(1)} %get-tuple-element.46.keys_hbm) | copy-start | bytes 15728644
  72.4 47.4 %copy-start.5 = (bf16[2560,640]{1,0:T(8,128)(2,1)}, bf16[2560,640]{1,0:T(8,128)(2,1)S(1)}, u32[]{:S(2)}) copy-start(bf16[2560,640]{1,0:T(8,128)(2,1)S(1)} %get-tuple-element.47.hot_hbm) | copy-start | bytes 9830404
  97.7 19.2 %collective-permute-start = (s16[528,640]{1,0:T(8,128)(2,1)S(1)}, s16[528,640]{1,0:T(8,128)(2,1)S(1)}, u32[]{:S(2)}, u32[]{:S(2)}) collective-permute-start(s16[528,640]{1,0:T(8,128)(2,1)S(1)} %get-tuple-element.50), channel_id=1, source_target_pairs={{0,32},{8,40},{16,48},{24,56},{32,64},{40,72},{48,80},{56,88},{64,... | collective-permute-start | bytes 2027528 | tf_op jit(solution)/shard_map/ppermute | solution.py:400
  97.8 20.6 %collective-permute-start.1 = (s16[528,640]{1,0:T(8,128)(2,1)S(1)}, s16[528,640]{1,0:T(8,128)(2,1)S(1)}, u32[]{:S(2)}, u32[]{:S(2)}) collective-permute-start(s16[528,640]{1,0:T(8,128)(2,1)S(1)} %get-tuple-element.51), channel_id=1, source_target_pairs={{0,96},{8,104},{16,112},{24,120},{32,0},{40,8},{48,16},{56,24},{64... | collective-permute-start | bytes 2027528 | tf_op jit(solution)/shard_map/ppermute | solution.py:400
  100.4 17.9 %collective-permute-start.2 = (s16[528,640]{1,0:T(8,128)(2,1)S(1)}, s16[528,640]{1,0:T(8,128)(2,1)S(1)}, u32[]{:S(2)}, u32[]{:S(2)}) collective-permute-start(s16[528,640]{1,0:T(8,128)(2,1)S(1)} %get-tuple-element.52), channel_id=1, source_target_pairs={{0,8},{8,16},{16,24},{24,0},{32,40},{40,48},{48,56},{56,32},{64,72... | collective-permute-start | bytes 2027528 | tf_op jit(solution)/shard_map/ppermute | solution.py:400
  100.5 19.3 %collective-permute-start.3 = (s16[528,640]{1,0:T(8,128)(2,1)S(1)}, s16[528,640]{1,0:T(8,128)(2,1)S(1)}, u32[]{:S(2)}, u32[]{:S(2)}) collective-permute-start(s16[528,640]{1,0:T(8,128)(2,1)S(1)} %get-tuple-element.53), channel_id=1, source_target_pairs={{0,24},{8,0},{16,8},{24,16},{32,56},{40,32},{48,40},{56,48},{64,88... | collective-permute-start | bytes 2027528 | tf_op jit(solution)/shard_map/ppermute | solution.py:400
  116.8 17.8 %collective-permute-start.4 = (s16[528,640]{1,0:T(8,128)(2,1)S(1)}, s16[528,640]{1,0:T(8,128)(2,1)S(1)}, u32[]{:S(2)}, u32[]{:S(2)}) collective-permute-start(s16[528,640]{1,0:T(8,128)(2,1)S(1)} %get-tuple-element.55), channel_id=1, source_target_pairs={{0,96},{8,104},{16,112},{24,120},{32,0},{40,8},{48,16},{56,24},{64... | collective-permute-start | bytes 2027528 | tf_op jit(solution)/shard_map/ppermute | solution.py:400
  116.9 20.4 %collective-permute-start.5 = (s16[528,640]{1,0:T(8,128)(2,1)S(1)}, s16[528,640]{1,0:T(8,128)(2,1)S(1)}, u32[]{:S(2)}, u32[]{:S(2)}) collective-permute-start(s16[528,640]{1,0:T(8,128)(2,1)S(1)} %get-tuple-element.56), channel_id=1, source_target_pairs={{0,32},{8,40},{16,48},{24,56},{32,64},{40,72},{48,80},{56,88},{64,... | collective-permute-start | bytes 2027528 | tf_op jit(solution)/shard_map/ppermute | solution.py:400
  118.4 18.9 %collective-permute-start.6 = (s16[528,640]{1,0:T(8,128)(2,1)S(1)}, s16[528,640]{1,0:T(8,128)(2,1)S(1)}, u32[]{:S(2)}, u32[]{:S(2)}) collective-permute-start(s16[528,640]{1,0:T(8,128)(2,1)S(1)} %get-tuple-element.57), channel_id=1, source_target_pairs={{0,24},{8,0},{16,8},{24,16},{32,56},{40,32},{48,40},{56,48},{64,88... | collective-permute-start | bytes 2027528 | tf_op jit(solution)/shard_map/ppermute | solution.py:400
  118.4 21.6 %collective-permute-start.7 = (s16[528,640]{1,0:T(8,128)(2,1)S(1)}, s16[528,640]{1,0:T(8,128)(2,1)S(1)}, u32[]{:S(2)}, u32[]{:S(2)}) collective-permute-start(s16[528,640]{1,0:T(8,128)(2,1)S(1)} %get-tuple-element.58), channel_id=1, source_target_pairs={{0,8},{8,16},{16,24},{24,0},{32,40},{40,48},{48,56},{56,32},{64,72... | collective-permute-start | bytes 2027528 | tf_op jit(solution)/shard_map/ppermute | solution.py:400
  134.5 23.1 %collective-permute-start.8 = (s16[528,640]{1,0:T(8,128)(2,1)S(1)}, s16[528,640]{1,0:T(8,128)(2,1)S(1)}, u32[]{:S(2)}, u32[]{:S(2)}) collective-permute-start(s16[528,640]{1,0:T(8,128)(2,1)S(1)} %get-tuple-element.61), channel_id=1, source_target_pairs={{0,32},{8,40},{16,48},{24,56},{32,64},{40,72},{48,80},{56,88},{64,... | collective-permute-start | bytes 2027528 | tf_op jit(solution)/shard_map/ppermute | solution.py:400
  134.6 23.0 %collective-permute-start.9 = (s16[528,640]{1,0:T(8,128)(2,1)S(1)}, s16[528,640]{1,0:T(8,128)(2,1)S(1)}, u32[]{:S(2)}, u32[]{:S(2)}) collective-permute-start(s16[528,640]{1,0:T(8,128)(2,1)S(1)} %get-tuple-element.62), channel_id=1, source_target_pairs={{0,96},{8,104},{16,112},{24,120},{32,0},{40,8},{48,16},{56,24},{64... | collective-permute-start | bytes 2027528 | tf_op jit(solution)/shard_map/ppermute | solution.py:400
  137.3 14.9 %collective-permute-start.10 = (s16[528,640]{1,0:T(8,128)(2,1)S(1)}, s16[528,640]{1,0:T(8,128)(2,1)S(1)}, u32[]{:S(2)}, u32[]{:S(2)}) collective-permute-start(s16[528,640]{1,0:T(8,128)(2,1)S(1)} %get-tuple-element.66), channel_id=1, source_target_pairs={{0,8},{8,16},{16,24},{24,0},{32,40},{40,48},{48,56},{56,32},{64,72... | collective-permute-start | bytes 2027528 | tf_op jit(solution)/shard_map/ppermute | solution.py:400
  137.3 14.9 %collective-permute-start.11 = (s16[528,640]{1,0:T(8,128)(2,1)S(1)}, s16[528,640]{1,0:T(8,128)(2,1)S(1)}, u32[]{:S(2)}, u32[]{:S(2)}) collective-permute-start(s16[528,640]{1,0:T(8,128)(2,1)S(1)} %get-tuple-element.67), channel_id=1, source_target_pairs={{0,24},{8,0},{16,8},{24,16},{32,56},{40,32},{48,40},{56,48},{64,88... | collective-permute-start | bytes 2027528 | tf_op jit(solution)/shard_map/ppermute | solution.py:400
  154.8 17.0 %copy-start.2 = (f32[256,1280]{1,0:T(8,128)S(1)}, f32[256,1280]{1,0:T(8,128)}, u32[]{:S(2)}) copy-start(f32[256,1280]{1,0:T(8,128)} %convolution_multiply_fusion.text_ref) | copy-start | bytes 3932164
  154.8 7.8 %collective-permute-start.15 = (s16[272,640]{1,0:T(8,128)(2,1)S(1)}, s16[272,640]{1,0:T(8,128)(2,1)S(1)}, u32[]{:S(2)}, u32[]{:S(2)}) collective-permute-start(s16[272,640]{1,0:T(8,128)(2,1)S(1)} %get-tuple-element.72), channel_id=1, source_target_pairs={{0,64},{8,72},{16,80},{24,88},{32,96},{40,104},{48,112},{56,120},{... | collective-permute-start | bytes 1044488 | tf_op jit(solution)/shard_map/ppermute | solution.py:400
  154.9 11.5 %collective-permute-start.16 = (s16[272,640]{1,0:T(8,128)(2,1)S(1)}, s16[272,640]{1,0:T(8,128)(2,1)S(1)}, u32[]{:S(2)}, u32[]{:S(2)}) collective-permute-start(s16[272,640]{1,0:T(8,128)(2,1)S(1)} %get-tuple-element.73), channel_id=1, source_target_pairs={{0,32},{8,40},{16,48},{24,56},{32,64},{40,72},{48,80},{56,88},{64,... | collective-permute-start | bytes 1044488 | tf_op jit(solution)/shard_map/ppermute | solution.py:400
  155.6 10.8 %collective-permute-start.17 = (s16[272,640]{1,0:T(8,128)(2,1)S(1)}, s16[272,640]{1,0:T(8,128)(2,1)S(1)}, u32[]{:S(2)}, u32[]{:S(2)}) collective-permute-start(s16[272,640]{1,0:T(8,128)(2,1)S(1)} %get-tuple-element.74), channel_id=1, source_target_pairs={{0,96},{8,104},{16,112},{24,120},{32,0},{40,8},{48,16},{56,24},{64... | collective-permute-start | bytes 1044488 | tf_op jit(solution)/shard_map/ppermute | solution.py:400
  160.2 8.1 %collective-permute-start.12 = (s16[272,640]{1,0:T(8,128)(2,1)S(1)}, s16[272,640]{1,0:T(8,128)(2,1)S(1)}, u32[]{:S(2)}, u32[]{:S(2)}) collective-permute-start(s16[272,640]{1,0:T(8,128)(2,1)S(1)} %get-tuple-element.69), channel_id=1, source_target_pairs={{0,16},{8,24},{16,0},{24,8},{32,48},{40,56},{48,32},{56,40},{64,80... | collective-permute-start | bytes 1044488 | tf_op jit(solution)/shard_map/ppermute | solution.py:400
  160.3 11.4 %collective-permute-start.13 = (s16[272,640]{1,0:T(8,128)(2,1)S(1)}, s16[272,640]{1,0:T(8,128)(2,1)S(1)}, u32[]{:S(2)}, u32[]{:S(2)}) collective-permute-start(s16[272,640]{1,0:T(8,128)(2,1)S(1)} %get-tuple-element.70), channel_id=1, source_target_pairs={{0,8},{8,16},{16,24},{24,0},{32,40},{40,48},{48,56},{56,32},{64,72... | collective-permute-start | bytes 1044488 | tf_op jit(solution)/shard_map/ppermute | solution.py:400
  162.6 9.1 %collective-permute-start.14 = (s16[272,640]{1,0:T(8,128)(2,1)S(1)}, s16[272,640]{1,0:T(8,128)(2,1)S(1)}, u32[]{:S(2)}, u32[]{:S(2)}) collective-permute-start(s16[272,640]{1,0:T(8,128)(2,1)S(1)} %get-tuple-element.71), channel_id=1, source_target_pairs={{0,24},{8,0},{16,8},{24,16},{32,56},{40,32},{48,40},{56,48},{64,88... | collective-permute-start | bytes 1044488 | tf_op jit(solution)/shard_map/ppermute | solution.py:400
  171.8 26.7 %copy-start.1 = (bf16[1280,1024]{1,0:T(8,128)(2,1)S(1)}, bf16[1280,1024]{1,0:T(8,128)(2,1)}, u32[]{:S(2)}) copy-start(bf16[1280,1024]{1,0:T(8,128)(2,1)} %param.7) | copy-start | bytes 7864324
Sparse Core Ops, SparseCore 0:
  10.3 73.9 all-gather.3

commit v3 on v2

--- a/solution.py
+++ b/solution.py
@@ -17,7 +17,7 @@
 TAIL = 16
 
 
-def params(mib=44):
+def params(mib=36):
     return pltpu.CompilerParams(vmem_limit_bytes=mib * 1024 * 1024)
 
 
@@ -120,16 +120,14 @@
 
 SUPER = SIDE * QT
 COMMON = 3
-TILES = CAP // KT
-
-
-def super_sums(tiles, wait_keys, wait_hots, q_ref, keys_ref, hot_ref, scores_ref, total_ref):
+
+
+def super_sums(tiles, q_ref, keys_ref, hot_ref, scores_ref, total_ref):
     width = q_ref.shape[-1]
     sharpness = float(width) ** 0.5 * math.log2(math.e)
     queries = q_ref[...].reshape(SUPER, width)
 
     def step(t, carry):
-        wait_keys(t)
         at = pl.ds(aligned(t * KT), KT)
         cosine = lax.dot_general(
             queries, keys_ref[at, :], (((1,), (1,)), ((), ())), preferred_element_type=jnp.float32
@@ -138,7 +136,6 @@
         return carry
 
     lax.fori_loop(0, tiles, step, 0)
-    wait_hots()
     cut = COMMON * KT
     total_ref[...] = jnp.dot(
         scores_ref[:, :cut], hot_ref[:cut, :], preferred_element_type=jnp.float32
@@ -155,11 +152,10 @@
     width = keys.shape[1]
     joined = len(arrived)
 
-    def kernel(facts_ref, q_hbm, keys_hbm, hot_hbm, *rest):
+    def kernel(facts_ref, q_hbm, keys_ref, hot_ref, *rest):
         came, outs, next_ref = rest[:joined], rest[joined : joined + 4], rest[joined + 4]
         scratch = rest[joined + 5 :]
-        q_ref, keys_ref, hot_ref, scores_ref, total_ref, came_ref, msg_ref = scratch[:7]
-        q_sems, key_sems, hot_sems, came_sems, out_sems = scratch[7:]
+        q_ref, scores_ref, total_ref, came_ref, msg_ref, q_sems, came_sems, out_sems = scratch
         for at in range(4):
             next_ref[at] = facts_ref[at]
 
@@ -170,18 +166,6 @@
             chunk = jnp.where(block == 0, outer * SIDE + inner, inner * SIDE + outer)
             return pltpu.make_async_copy(q_hbm.at[chunk], q_ref.at[block, part], q_sems.at[block, part])
 
-        def copy_keys(block, t):
-            return pltpu.make_async_copy(
-                keys_hbm.at[pl.ds(aligned(block * CAP + t * KT), KT), :],
-                keys_ref.at[block, pl.ds(aligned(t * KT), KT), :],
-                key_sems.at[block, t],
-            )
-
-        def copy_hots(block):
-            return pltpu.make_async_copy(
-                hot_hbm.at[pl.ds(aligned(block * CAP), CAP), :], hot_ref.at[block], hot_sems.at[block]
-            )
-
         def copy_came(at):
             return pltpu.make_async_copy(came[at], came_ref.at[at], came_sems.at[at])
 
@@ -192,13 +176,6 @@
         for block in range(2):
             for part in range(SIDE):
                 copy_queries(block, part).start()
-
-            def start(t, carry, block=block):
-                copy_keys(block, t).start()
-                return carry
-
-            lax.fori_loop(0, facts_ref[2 + block], start, 0)
-            copy_hots(block).start()
         for at in range(joined):
             copy_came(at).start()
         scores_ref[:, COMMON * KT :] = jnp.zeros((SUPER, CAP - COMMON * KT), jnp.bfloat16)
@@ -211,11 +188,9 @@
                 copy_queries(block, part).wait()
             super_sums(
                 facts_ref[2 + block],
-                lambda t: copy_keys(block, t).wait(),
-                lambda: copy_hots(block).wait(),
                 q_ref.at[block],
-                keys_ref.at[block],
-                hot_ref.at[block],
+                keys_ref.at[pl.ds(aligned(block * CAP), CAP), :],
+                hot_ref.at[pl.ds(aligned(block * CAP), CAP), :],
                 scores_ref,
                 total_ref.at[block],
             )
@@ -249,24 +224,20 @@
         for at in range(4):
             copy_out(at).wait()
 
-    smem = pl.BlockSpec(memory_space=pltpu.SMEM)
+    vmem, smem = pl.BlockSpec(memory_space=pltpu.VMEM), pl.BlockSpec(memory_space=pltpu.SMEM)
     anywhere = pl.BlockSpec(memory_space=pl.ANY)
     return pl.pallas_call(
         kernel,
-        in_specs=[smem] + [anywhere] * (3 + joined),
+        in_specs=[smem, anywhere, vmem, vmem] + [anywhere] * joined,
         out_specs=[anywhere] * 4 + [smem],
         out_shape=[HALF_MSG if coded else HALF_RAW] * 4 + [jax.ShapeDtypeStruct((4,), jnp.int32)],
         scratch_shapes=[
             pltpu.VMEM((2, SIDE, QT, width), jnp.bfloat16),
-            pltpu.VMEM((2, CAP, width), jnp.bfloat16),
-            pltpu.VMEM((2, CAP, CB), jnp.bfloat16),
             pltpu.VMEM((SUPER, CAP), jnp.bfloat16),
             pltpu.VMEM((2, SUPER, CB), jnp.float32),
             pltpu.VMEM((4,) + HALF_MSG.shape, jnp.int16),
             pltpu.VMEM((4,) + HALF_MSG.shape, jnp.int16),
             pltpu.SemaphoreType.DMA((2, SIDE)),
-            pltpu.SemaphoreType.DMA((2, TILES)),
-            pltpu.SemaphoreType.DMA((2,)),
             pltpu.SemaphoreType.DMA((4,)),
             pltpu.SemaphoreType.DMA((4,)),
         ],

time: 207 us -> 206 us (level)
  blocking collectives: 39.9 us -> 27.9 us
  starting transfers between devices: 18.1 us -> 24.8 us
  waiting for transfers between devices: 22.1 us -> 28.5 us
  Pallas kernels: 69.9 us -> 64.1 us
  local copies, waits for them, and re-layouts: 25.4 us -> 30.5 us
    all_gather x1, blocking collectives: 24.4 us -> 12.2 us  [per_device(): return finish(logits, lax.all_gather(stats, 'cls'))]
    ppermute x18, starting transfers between devices: 18.1 us -> 24.8 us  [send(): return lax.ppermute(message, 'cache', shifted(dx, dz))]
    ppermute x18, waiting for transfers between devices: 10.1 us -> 15.7 us  [send(): return lax.ppermute(message, 'cache', shifted(dx, dz))]
    unnamed x14 -> x16, local copies, waits for them, and re-layouts: 3.42 us -> 8.54 us
    pallas_call x1, Pallas kernels: 7.85 us -> 4.21 us  [prepare(): pl.pallas_call(prepare_kernel, grid=(count // KT,), in_specs=[pl.BlockSpe...]
    pallas_call x4, Pallas kernels: 53.9 us -> 51.7 us  [sums(): pl.pallas_call(kernel, in_specs=[smem, anywhere, vmem, vmem] + [anywhere]...]
  transfers between devices with their start and end apart: 19 -> 19, of which waited for: 5 -> 6; matrix products, arithmetic and copies ran while one was open for 16% -> 16% of each run, Pallas kernels for 26% -> 23%
where the time goes in v3:
time: 206 us
  Pallas kernels  64.1 us (31%)
  local copies, waits for them, and re-layouts  30.5 us (15%)
  waiting for transfers between devices  28.5 us (14%)
  blocking collectives  27.9 us (14%)
  starting transfers between devices  24.8 us (12%)
  between operations  19.9 us (10%)
  other arithmetic  8.11 us (4%)
    pallas_call x4, Pallas kernels, sums(): pl.pallas_call(kernel, in_specs=[smem, anywhere, vmem, vmem] + [anywhere]...  51.7 us
    ppermute x18, starting transfers between devices, send(): return lax.ppermute(message, 'cache', shifted(dx, dz))  24.8 us
    gather x1, local copies, waits for them, and re-layouts, per_device(): rows = jnp.take(cache_keys, picked % 16384, axis=0, mode='clip')  21.8 us
    ppermute x18, waiting for transfers between devices, send(): return lax.ppermute(message, 'cache', shifted(dx, dz))  15.7 us
    all_gather x1, blocking collectives, per_device(): lax.all_gather(unit_queries, 'cls', axis=0, tiled=True)  15.6 us
    all_gather x1, waiting for transfers between devices, per_device(): lax.all_gather(unit_queries, ('cache', 'cls'), axis=0, tiled=True)  12.8 us
    all_gather x1, blocking collectives, per_device(): return finish(logits, lax.all_gather(stats, 'cls'))  12.2 us
    unnamed x16, local copies, waits for them, and re-layouts  8.54 us
  transfers between devices with their start and end apart: 19, of which 6 were waited for; matrix products, arithmetic and copies ran while one was open for 16% of the time, Pallas kernels for 23%

profile of v3, /device:TPU:1, one launch (start us, length us, event | category | flops | bytes accessed | tf_op | source)
XLA Modules:
  0.0 205.7 jit_solution(9119024173156519626)
XLA Ops:
  6.5 1.0 copy-done.4
  7.5 0.7 unit.1
  8.2 0.0 all-gather.4.cloned.1.call-update
  8.3 1.5 convert_reduce_fusion
  14.9 6.3 %sort.7 = s32[10240]{0:T(1024)S(1)} sort(s32[10240]{0:T(1024)S(1)} %get-tuple-element.82), dimensions={0}, to_apply=%region_0.1 | sort | flops 143360 | bytes 81920 | tf_op jit(solution)/shard_map/sort | solution.py:383
  22.4 0.1 pad_dynamic-slice_fusion
  22.6 0.1 fusion
  22.7 21.8 %gather_fusion = bf16[2560,1024]{1,0:T(8,128)(2,1)} fusion(bf16[10240,1024]{1,0:T(8,128)(2,1)} %param.5, s32[3072]{0:T(1024)S(1)} %pad_clamp_fusion), kind=kCustom, calls=%fused_computation | custom fusion | bytes 10496000 | tf_op jit(solution)/shard_map/jit(_take)/gather | solution.py:396
  44.5 15.6 %all_gather.12 = bf16[256,1024]{1,0:T(8,128)(2,1)S(1)} all-gather(bf16[32,1024]{1,0:T(8,128)(2,1)} %unit.1), channel_id=1, replica_groups=mesh['cache'=16,'cls'=8] {'cls'}, dimensions={0}, use_global_device_ids=true | all-gather | bytes 589824 | tf_op jit(solution)/shard_map/all_gather | solution.py:398
  60.1 1.9 convolution_multiply_fusion.text_ref
  62.0 0.1 fusion.2
  62.1 0.1 pad_add_fusion.facts_ref
  62.2 0.1 compare_select_fusion.2.labels_ref
  62.3 2.6 %copy-done.2 = bf16[2560,1024]{1,0:T(8,128)(2,1)S(1)} copy-done((bf16[2560,1024]{1,0:T(8,128)(2,1)S(1)}, bf16[2560,1024]{1,0:T(8,128)(2,1)}, u32[]{:S(2)}) %copy-start.2) | copy-done | bytes 5242904
  65.0 4.2 %prepare.1 = (bf16[2560,1024]{1,0:T(8,128)(2,1)S(1)}, bf16[2560,640]{1,0:T(8,128)(2,1)S(1)}, s32[4]{0:T(128)S(1)}) custom-call(s32[4]{0:T(128)S(1)} %pad_add_fusion.facts_ref, bf16[2560,1024]{1,0:T(8,128)(2,1)S(1)} %copy-done.2, s32[10,1,256]{2,1,0:T(1,128)S(1)} %compare_select_fusion.2.labels_ref), custom_call_target="tpu_custom_call" | custom-call | flops 10485760 | bytes 15728640 | tf_op jit(solution)/shard_map/prepare/pallas_call | solution.py:42
  69.2 2.4 %copy-done.5 = bf16[2560,1024]{1,0:T(8,128)(2,1)} copy-done((bf16[2560,1024]{1,0:T(8,128)(2,1)}, bf16[2560,1024]{1,0:T(8,128)(2,1)S(1)}, u32[]{:S(2)}) %copy-start.5) | copy-done | bytes 5242904
  71.6 12.8 %all-gather.4.cloned.1.call-done = bf16[4096,1024]{1,0:T(8,128)(2,1)} async-done(((bf16[32,1024]{1,0:T(8,128)(2,1)}), bf16[4096,1024]{1,0:T(8,128)(2,1)}) %all-gather.4.cloned.1.call-update) | async-done | bytes 8388624 | tf_op jit(solution)/shard_map/all_gather | solution.py:381
  84.3 2.5 %copy-done.6 = bf16[2560,1024]{1,0:T(8,128)(2,1)S(1)} copy-done((bf16[2560,1024]{1,0:T(8,128)(2,1)S(1)}, bf16[2560,1024]{1,0:T(8,128)(2,1)}, u32[]{:S(2)}) %copy-start.6) | copy-done | bytes 5242904
  86.8 12.9 %sums.4 = (s16[528,640]{1,0:T(8,128)(2,1)S(1)}, s16[528,640]{1,0:T(8,128)(2,1)S(1)}, s16[528,640]{1,0:T(8,128)(2,1)S(1)}, s16[528,640]{1,0:T(8,128)(2,1)S(1)}, s32[4]{0:T(128)S(1)}) custom-call(s32[4]{0:T(128)S(1)} %get-tuple-element.44.facts_ref, bf16[16,256,1024]{2,1,0:T(8,128)(2,1)} %bitcast.9, bf16[2560,1024]{1,0:T(8,128)(2,1)S(1)} %copy-done.6, ...), custom_call_target="tpu_custom_call" | custom-call | flops 8724152320 | bytes 4194304 | tf_op jit(solution)/shard_map/sums/pallas_call | solution.py:229
  99.8 1.7 collective-permute-start
  101.5 1.0 collective-permute-start.1
  102.5 0.0 collective-permute-start.2
  102.5 2.7 %collective-permute-start.3 = (s16[528,640]{1,0:T(8,128)(2,1)S(1)}, s16[528,640]{1,0:T(8,128)(2,1)S(1)}, u32[]{:S(2)}, u32[]{:S(2)}) collective-permute-start(s16[528,640]{1,0:T(8,128)(2,1)S(1)} %get-tuple-element.53), channel_id=1, source_target_pairs={{0,24},{8,0},{16,8},{24,16},{32,56},{40,32},{48,40},{56,48},{64,88... | collective-permute-start | bytes 2027528 | tf_op jit(solution)/shard_map/ppermute | solution.py:371
  105.2 13.1 %sums.5 = (s16[528,640]{1,0:T(8,128)(2,1)S(1)}, s16[528,640]{1,0:T(8,128)(2,1)S(1)}, s16[528,640]{1,0:T(8,128)(2,1)S(1)}, s16[528,640]{1,0:T(8,128)(2,1)S(1)}, s32[4]{0:T(128)S(1)}) custom-call(s32[4]{0:T(128)S(1)} %get-tuple-element.48.facts_ref, bf16[16,256,1024]{2,1,0:T(8,128)(2,1)} %bitcast.10, bf16[2560,1024]{1,0:T(8,128)(2,1)S(1)} %copy-done.6, ...), custom_call_target="tpu_custom_call" | custom-call | flops 8724152320 | bytes 4194304 | tf_op jit(solution)/shard_map/sums/pallas_call | solution.py:229
  118.3 0.9 collective-permute-start.4
  119.1 0.0 collective-permute-done.rest_0_
  119.1 1.3 collective-permute-start.5
  120.4 0.0 collective-permute-done.1.rest_1_
  120.4 0.0 collective-permute-start.6
  120.4 0.0 collective-permute-done.2.rest_2_
  120.4 1.5 collective-permute-start.7
  121.9 0.0 collective-permute-done.3.rest_3_
  121.9 13.9 %sums.6 = (s16[528,640]{1,0:T(8,128)(2,1)S(1)}, s16[528,640]{1,0:T(8,128)(2,1)S(1)}, s16[528,640]{1,0:T(8,128)(2,1)S(1)}, s16[528,640]{1,0:T(8,128)(2,1)S(1)}, s32[4]{0:T(128)S(1)}) custom-call(s32[4]{0:T(128)S(1)} %get-tuple-element.49.facts_ref, bf16[16,256,1024]{2,1,0:T(8,128)(2,1)} %bitcast.11, bf16[2560,1024]{1,0:T(8,128)(2,1)S(1)} %copy-done.6, ...), custom_call_target="tpu_custom_call" | custom-call | flops 8724152320 | bytes 4194304 | tf_op jit(solution)/shard_map/sums/pallas_call | solution.py:229
  135.8 3.1 %collective-permute-start.8 = (s16[528,640]{1,0:T(8,128)(2,1)S(1)}, s16[528,640]{1,0:T(8,128)(2,1)S(1)}, u32[]{:S(2)}, u32[]{:S(2)}) collective-permute-start(s16[528,640]{1,0:T(8,128)(2,1)S(1)} %get-tuple-element.61), channel_id=1, source_target_pairs={{0,32},{8,40},{16,48},{24,56},{32,64},{40,72},{48,80},{56,88},{64,... | collective-permute-start | bytes 2027528 | tf_op jit(solution)/shard_map/ppermute | solution.py:371
  138.9 0.0 collective-permute-done.4.rest_0_
  138.9 0.0 collective-permute-start.9
  139.0 0.0 collective-permute-done.5.rest_1_
  139.0 0.1 collective-permute-start.10
  139.1 0.0 collective-permute-done.6.rest_2_
  139.1 2.6 %collective-permute-start.11 = (s16[528,640]{1,0:T(8,128)(2,1)S(1)}, s16[528,640]{1,0:T(8,128)(2,1)S(1)}, u32[]{:S(2)}, u32[]{:S(2)}) collective-permute-start(s16[528,640]{1,0:T(8,128)(2,1)S(1)} %get-tuple-element.67), channel_id=1, source_target_pairs={{0,24},{8,0},{16,8},{24,16},{32,56},{40,32},{48,40},{56,48},{64,88... | collective-permute-start | bytes 2027528 | tf_op jit(solution)/shard_map/ppermute | solution.py:371
  141.7 0.0 collective-permute-done.7.rest_3_
  141.7 11.8 %sums.7 = (f32[512,640]{1,0:T(8,128)S(1)}, f32[512,640]{1,0:T(8,128)S(1)}, f32[512,640]{1,0:T(8,128)S(1)}, f32[512,640]{1,0:T(8,128)S(1)}, s32[4]{0:T(128)}) custom-call(s32[4]{0:T(128)S(1)} %get-tuple-element.54.facts_ref, bf16[16,256,1024]{2,1,0:T(8,128)(2,1)} %bitcast.12, bf16[2560,1024]{1,0:T(8,128)(2,1)S(1)} %copy-done.6, ...), custom_call_target="tpu_custom_call" | custom-call | flops 8724152320 | bytes 4194304 | tf_op jit(solution)/shard_map/sums/pallas_call | solution.py:229
  153.6 0.6 collective-permute-done.10.low_msg
  154.1 0.7 collective-permute-done.11.high_msg
  154.8 2.6 %turn.3 = (f32[256,640]{1,0:T(8,128)S(1)}, s16[272,640]{1,0:T(8,128)(2,1)S(1)}, s16[272,640]{1,0:T(8,128)(2,1)S(1)}, s16[272,640]{1,0:T(8,128)(2,1)S(1)}) custom-call(s32[1]{0:T(128)} %bitcast.1.place_ref, f32[512,640]{1,0:T(8,128)S(1)} %get-tuple-element.64.low_hbm, f32[512,640]{1,0:T(8,128)S(1)} %get-tuple-element.65.high_hbm, ...), custom_call_target="tpu_custom_call" | custom-call | flops 6553600 | bytes 6553600 | tf_op jit(solution)/shard_map/turn/pallas_call | solution.py:298
  157.4 0.0 copy-start.3
  157.4 3.2 %collective-permute-start.15 = (s16[272,640]{1,0:T(8,128)(2,1)S(1)}, s16[272,640]{1,0:T(8,128)(2,1)S(1)}, u32[]{:S(2)}, u32[]{:S(2)}) collective-permute-start(s16[272,640]{1,0:T(8,128)(2,1)S(1)} %get-tuple-element.72), channel_id=1, source_target_pairs={{0,64},{8,72},{16,80},{24,88},{32,96},{40,104},{48,112},{56,120},{... | collective-permute-start | bytes 1044488 | tf_op jit(solution)/shard_map/ppermute | solution.py:371
  160.6 1.0 collective-permute-start.16
  161.6 1.7 collective-permute-start.17
  163.3 0.0 collective-permute-done.8.low_msg
  163.3 0.0 collective-permute-done.9.high_msg
  163.3 2.6 %turn.2 = (f32[256,640]{1,0:T(8,128)S(1)}, s16[272,640]{1,0:T(8,128)(2,1)S(1)}, s16[272,640]{1,0:T(8,128)(2,1)S(1)}, s16[272,640]{1,0:T(8,128)(2,1)S(1)}) custom-call(s32[1]{0:T(128)} %bitcast.place_ref, f32[512,640]{1,0:T(8,128)S(1)} %get-tuple-element.59.low_hbm, f32[512,640]{1,0:T(8,128)S(1)} %get-tuple-element.60.high_hbm, ...), custom_call_target="tpu_custom_call" | custom-call | flops 6553600 | bytes 6553600 | tf_op jit(solution)/shard_map/turn/pallas_call | solution.py:298
  165.9 1.3 collective-permute-start.12
  167.1 1.4 collective-permute-start.13
  168.6 0.0 collective-permute-done.15.rest_5_
  168.6 1.2 collective-permute-start.14
  169.8 5.9 %collective-permute-done.16.rest_6_ = s16[272,640]{1,0:T(8,128)(2,1)S(1)} collective-permute-done((s16[272,640]{1,0:T(8,128)(2,1)S(1)}, s16[272,640]{1,0:T(8,128)(2,1)S(1)}, u32[]{:S(2)}, u32[]{:S(2)}) %collective-permute-start.16) | collective-permute-done | bytes 348192 | tf_op jit(solution)/shard_map/ppermute | solution.py:371
  175.8 0.8 collective-permute-done.17.rest_7_
  176.6 0.0 collective-permute-done.12.rest_2_
  176.6 7.6 %collective-permute-done.13.rest_3_ = s16[272,640]{1,0:T(8,128)(2,1)S(1)} collective-permute-done((s16[272,640]{1,0:T(8,128)(2,1)S(1)}, s16[272,640]{1,0:T(8,128)(2,1)S(1)}, u32[]{:S(2)}, u32[]{:S(2)}) %collective-permute-start.13) | collective-permute-done | bytes 348192 | tf_op jit(solution)/shard_map/ppermute | solution.py:371
  184.3 0.0 collective-permute-done.14.rest_4_
  184.3 1.0 close.1
  185.3 12.2 %all-gather.1.stats_ref = f32[8,2,256]{2,1,0:T(2,128)S(1)} all-gather(f32[1,2,256]{2,1,0:T(2,128)S(1)} %bitcast.8), channel_id=2, replica_groups=mesh['cache'=16,'cls'=8] {'cls'}, dimensions={0}, use_global_device_ids=true | all-gather | bytes 18432 | tf_op jit(solution)/shard_map/all_gather | solution.py:434
  197.5 1.3 finish.1
  (17 shorter events, 0.1 us)
Async XLA Ops:
  6.5 53.6 %copy-start = (bf16[1280,1024]{1,0:T(8,128)(2,1)S(1)}, bf16[1280,1024]{1,0:T(8,128)(2,1)}, u32[]{:S(2)}) copy-start(bf16[1280,1024]{1,0:T(8,128)(2,1)} %param.7) | copy-start | bytes 7864324
  6.5 77.8 %all-gather.4.cloned.1.call-start = ((), (), s32[]{:S(2)}) async-start(), calls=%async_computation | async-start | bytes 8454144 | tf_op jit(solution)/shard_map/all_gather | solution.py:381
  6.5 1.0 copy-start.4
  62.3 2.6 %copy-start.2 = (bf16[2560,1024]{1,0:T(8,128)(2,1)S(1)}, bf16[2560,1024]{1,0:T(8,128)(2,1)}, u32[]{:S(2)}) copy-start(bf16[2560,1024]{1,0:T(8,128)(2,1)} %gather_fusion) | copy-start | bytes 15728644
  69.2 2.4 %copy-start.5 = (bf16[2560,1024]{1,0:T(8,128)(2,1)}, bf16[2560,1024]{1,0:T(8,128)(2,1)S(1)}, u32[]{:S(2)}) copy-start(bf16[2560,1024]{1,0:T(8,128)(2,1)S(1)} %get-tuple-element.46.keys_ref) | copy-start | bytes 15728644
  84.3 2.5 %copy-start.6 = (bf16[2560,1024]{1,0:T(8,128)(2,1)S(1)}, bf16[2560,1024]{1,0:T(8,128)(2,1)}, u32[]{:S(2)}) copy-start(bf16[2560,1024]{1,0:T(8,128)(2,1)} %copy-done.5) | copy-start | bytes 15728644
  99.8 19.4 %collective-permute-start = (s16[528,640]{1,0:T(8,128)(2,1)S(1)}, s16[528,640]{1,0:T(8,128)(2,1)S(1)}, u32[]{:S(2)}, u32[]{:S(2)}) collective-permute-start(s16[528,640]{1,0:T(8,128)(2,1)S(1)} %get-tuple-element.50), channel_id=1, source_target_pairs={{0,32},{8,40},{16,48},{24,56},{32,64},{40,72},{48,80},{56,88},{64,... | collective-permute-start | bytes 2027528 | tf_op jit(solution)/shard_map/ppermute | solution.py:371
  101.5 18.9 %collective-permute-start.1 = (s16[528,640]{1,0:T(8,128)(2,1)S(1)}, s16[528,640]{1,0:T(8,128)(2,1)S(1)}, u32[]{:S(2)}, u32[]{:S(2)}) collective-permute-start(s16[528,640]{1,0:T(8,128)(2,1)S(1)} %get-tuple-element.51), channel_id=1, source_target_pairs={{0,96},{8,104},{16,112},{24,120},{32,0},{40,8},{48,16},{56,24},{64... | collective-permute-start | bytes 2027528 | tf_op jit(solution)/shard_map/ppermute | solution.py:371
  102.5 17.9 %collective-permute-start.2 = (s16[528,640]{1,0:T(8,128)(2,1)S(1)}, s16[528,640]{1,0:T(8,128)(2,1)S(1)}, u32[]{:S(2)}, u32[]{:S(2)}) collective-permute-start(s16[528,640]{1,0:T(8,128)(2,1)S(1)} %get-tuple-element.52), channel_id=1, source_target_pairs={{0,8},{8,16},{16,24},{24,0},{32,40},{40,48},{48,56},{56,32},{64,72... | collective-permute-start | bytes 2027528 | tf_op jit(solution)/shard_map/ppermute | solution.py:371
  102.5 19.4 %collective-permute-start.3 = (s16[528,640]{1,0:T(8,128)(2,1)S(1)}, s16[528,640]{1,0:T(8,128)(2,1)S(1)}, u32[]{:S(2)}, u32[]{:S(2)}) collective-permute-start(s16[528,640]{1,0:T(8,128)(2,1)S(1)} %get-tuple-element.53), channel_id=1, source_target_pairs={{0,24},{8,0},{16,8},{24,16},{32,56},{40,32},{48,40},{56,48},{64,88... | collective-permute-start | bytes 2027528 | tf_op jit(solution)/shard_map/ppermute | solution.py:371
  118.3 20.7 %collective-permute-start.4 = (s16[528,640]{1,0:T(8,128)(2,1)S(1)}, s16[528,640]{1,0:T(8,128)(2,1)S(1)}, u32[]{:S(2)}, u32[]{:S(2)}) collective-permute-start(s16[528,640]{1,0:T(8,128)(2,1)S(1)} %get-tuple-element.55), channel_id=1, source_target_pairs={{0,96},{8,104},{16,112},{24,120},{32,0},{40,8},{48,16},{56,24},{64... | collective-permute-start | bytes 2027528 | tf_op jit(solution)/shard_map/ppermute | solution.py:371
  119.1 19.8 %collective-permute-start.5 = (s16[528,640]{1,0:T(8,128)(2,1)S(1)}, s16[528,640]{1,0:T(8,128)(2,1)S(1)}, u32[]{:S(2)}, u32[]{:S(2)}) collective-permute-start(s16[528,640]{1,0:T(8,128)(2,1)S(1)} %get-tuple-element.56), channel_id=1, source_target_pairs={{0,32},{8,40},{16,48},{24,56},{32,64},{40,72},{48,80},{56,88},{64,... | collective-permute-start | bytes 2027528 | tf_op jit(solution)/shard_map/ppermute | solution.py:371
  120.4 18.7 %collective-permute-start.6 = (s16[528,640]{1,0:T(8,128)(2,1)S(1)}, s16[528,640]{1,0:T(8,128)(2,1)S(1)}, u32[]{:S(2)}, u32[]{:S(2)}) collective-permute-start(s16[528,640]{1,0:T(8,128)(2,1)S(1)} %get-tuple-element.57), channel_id=1, source_target_pairs={{0,24},{8,0},{16,8},{24,16},{32,56},{40,32},{48,40},{56,48},{64,88... | collective-permute-start | bytes 2027528 | tf_op jit(solution)/shard_map/ppermute | solution.py:371
  120.4 21.3 %collective-permute-start.7 = (s16[528,640]{1,0:T(8,128)(2,1)S(1)}, s16[528,640]{1,0:T(8,128)(2,1)S(1)}, u32[]{:S(2)}, u32[]{:S(2)}) collective-permute-start(s16[528,640]{1,0:T(8,128)(2,1)S(1)} %get-tuple-element.58), channel_id=1, source_target_pairs={{0,8},{8,16},{16,24},{24,0},{32,40},{40,48},{48,56},{56,32},{64,72... | collective-permute-start | bytes 2027528 | tf_op jit(solution)/shard_map/ppermute | solution.py:371
  135.8 27.5 %collective-permute-start.8 = (s16[528,640]{1,0:T(8,128)(2,1)S(1)}, s16[528,640]{1,0:T(8,128)(2,1)S(1)}, u32[]{:S(2)}, u32[]{:S(2)}) collective-permute-start(s16[528,640]{1,0:T(8,128)(2,1)S(1)} %get-tuple-element.61), channel_id=1, source_target_pairs={{0,32},{8,40},{16,48},{24,56},{32,64},{40,72},{48,80},{56,88},{64,... | collective-permute-start | bytes 2027528 | tf_op jit(solution)/shard_map/ppermute | solution.py:371
  138.9 24.3 %collective-permute-start.9 = (s16[528,640]{1,0:T(8,128)(2,1)S(1)}, s16[528,640]{1,0:T(8,128)(2,1)S(1)}, u32[]{:S(2)}, u32[]{:S(2)}) collective-permute-start(s16[528,640]{1,0:T(8,128)(2,1)S(1)} %get-tuple-element.62), channel_id=1, source_target_pairs={{0,96},{8,104},{16,112},{24,120},{32,0},{40,8},{48,16},{56,24},{64... | collective-permute-start | bytes 2027528 | tf_op jit(solution)/shard_map/ppermute | solution.py:371
  139.0 15.2 %collective-permute-start.10 = (s16[528,640]{1,0:T(8,128)(2,1)S(1)}, s16[528,640]{1,0:T(8,128)(2,1)S(1)}, u32[]{:S(2)}, u32[]{:S(2)}) collective-permute-start(s16[528,640]{1,0:T(8,128)(2,1)S(1)} %get-tuple-element.66), channel_id=1, source_target_pairs={{0,8},{8,16},{16,24},{24,0},{32,40},{40,48},{48,56},{56,32},{64,72... | collective-permute-start | bytes 2027528 | tf_op jit(solution)/shard_map/ppermute | solution.py:371
  139.1 15.7 %collective-permute-start.11 = (s16[528,640]{1,0:T(8,128)(2,1)S(1)}, s16[528,640]{1,0:T(8,128)(2,1)S(1)}, u32[]{:S(2)}, u32[]{:S(2)}) collective-permute-start(s16[528,640]{1,0:T(8,128)(2,1)S(1)} %get-tuple-element.67), channel_id=1, source_target_pairs={{0,24},{8,0},{16,8},{24,16},{32,56},{40,32},{48,40},{56,48},{64,88... | collective-permute-start | bytes 2027528 | tf_op jit(solution)/shard_map/ppermute | solution.py:371
  157.4 26.9 %copy-start.3 = (f32[256,1280]{1,0:T(8,128)S(1)}, f32[256,1280]{1,0:T(8,128)}, u32[]{:S(2)}) copy-start(f32[256,1280]{1,0:T(8,128)} %convolution_multiply_fusion.text_ref) | copy-start | bytes 3932164
  157.4 11.2 %collective-permute-start.15 = (s16[272,640]{1,0:T(8,128)(2,1)S(1)}, s16[272,640]{1,0:T(8,128)(2,1)S(1)}, u32[]{:S(2)}, u32[]{:S(2)}) collective-permute-start(s16[272,640]{1,0:T(8,128)(2,1)S(1)} %get-tuple-element.72), channel_id=1, source_target_pairs={{0,64},{8,72},{16,80},{24,88},{32,96},{40,104},{48,112},{56,120},{... | collective-permute-start | bytes 1044488 | tf_op jit(solution)/shard_map/ppermute | solution.py:371
  160.6 15.2 %collective-permute-start.16 = (s16[272,640]{1,0:T(8,128)(2,1)S(1)}, s16[272,640]{1,0:T(8,128)(2,1)S(1)}, u32[]{:S(2)}, u32[]{:S(2)}) collective-permute-start(s16[272,640]{1,0:T(8,128)(2,1)S(1)} %get-tuple-element.73), channel_id=1, source_target_pairs={{0,32},{8,40},{16,48},{24,56},{32,64},{40,72},{48,80},{56,88},{64,... | collective-permute-start | bytes 1044488 | tf_op jit(solution)/shard_map/ppermute | solution.py:371
  161.6 15.0 %collective-permute-start.17 = (s16[272,640]{1,0:T(8,128)(2,1)S(1)}, s16[272,640]{1,0:T(8,128)(2,1)S(1)}, u32[]{:S(2)}, u32[]{:S(2)}) collective-permute-start(s16[272,640]{1,0:T(8,128)(2,1)S(1)} %get-tuple-element.74), channel_id=1, source_target_pairs={{0,96},{8,104},{16,112},{24,120},{32,0},{40,8},{48,16},{56,24},{64... | collective-permute-start | bytes 1044488 | tf_op jit(solution)/shard_map/ppermute | solution.py:371
  165.9 10.8 %collective-permute-start.12 = (s16[272,640]{1,0:T(8,128)(2,1)S(1)}, s16[272,640]{1,0:T(8,128)(2,1)S(1)}, u32[]{:S(2)}, u32[]{:S(2)}) collective-permute-start(s16[272,640]{1,0:T(8,128)(2,1)S(1)} %get-tuple-element.69), channel_id=1, source_target_pairs={{0,16},{8,24},{16,0},{24,8},{32,48},{40,56},{48,32},{56,40},{64,80... | collective-permute-start | bytes 1044488 | tf_op jit(solution)/shard_map/ppermute | solution.py:371
  167.1 17.1 %collective-permute-start.13 = (s16[272,640]{1,0:T(8,128)(2,1)S(1)}, s16[272,640]{1,0:T(8,128)(2,1)S(1)}, u32[]{:S(2)}, u32[]{:S(2)}) collective-permute-start(s16[272,640]{1,0:T(8,128)(2,1)S(1)} %get-tuple-element.70), channel_id=1, source_target_pairs={{0,8},{8,16},{16,24},{24,0},{32,40},{40,48},{48,56},{56,32},{64,72... | collective-permute-start | bytes 1044488 | tf_op jit(solution)/shard_map/ppermute | solution.py:371
  168.6 15.7 %collective-permute-start.14 = (s16[272,640]{1,0:T(8,128)(2,1)S(1)}, s16[272,640]{1,0:T(8,128)(2,1)S(1)}, u32[]{:S(2)}, u32[]{:S(2)}) collective-permute-start(s16[272,640]{1,0:T(8,128)(2,1)S(1)} %get-tuple-element.71), channel_id=1, source_target_pairs={{0,24},{8,0},{16,8},{24,16},{32,56},{40,32},{48,40},{56,48},{64,88... | collective-permute-start | bytes 1044488 | tf_op jit(solution)/shard_map/ppermute | solution.py:371
  184.3 14.6 %copy-start.1 = (bf16[1280,1024]{1,0:T(8,128)(2,1)S(1)}, bf16[1280,1024]{1,0:T(8,128)(2,1)}, u32[]{:S(2)}) copy-start(bf16[1280,1024]{1,0:T(8,128)(2,1)} %param.7) | copy-start | bytes 7864324
Sparse Core Ops, SparseCore 0:
  10.3 73.9 all-gather.3

commit v4 on v3

--- a/solution.py
+++ b/solution.py
@@ -127,25 +127,29 @@
     sharpness = float(width) ** 0.5 * math.log2(math.e)
     queries = q_ref[...].reshape(SUPER, width)
 
-    def step(t, carry):
-        at = pl.ds(aligned(t * KT), KT)
+    def scores(rows, at):
         cosine = lax.dot_general(
-            queries, keys_ref[at, :], (((1,), (1,)), ((), ())), preferred_element_type=jnp.float32
+            rows, keys_ref[at, :], (((1,), (1,)), ((), ())), preferred_element_type=jnp.float32
         )
-        scores_ref[:, at] = jnp.exp2(sharpness * cosine).astype(jnp.bfloat16)
+        return jnp.exp2(sharpness * cosine).astype(jnp.bfloat16)
+
+    cut = COMMON * KT
+    for t in range(COMMON):
+        at = pl.ds(t * KT, KT)
+        scores_ref[:, at] = scores(queries, at)
+    total_ref[...] = jnp.dot(scores_ref[...], hot_ref[:cut, :], preferred_element_type=jnp.float32)
+
+    def rest(i, carry):
+        half = lax.rem(i, 2)
+        at = pl.ds(aligned((COMMON + lax.div(i, 2)) * KT), KT)
+        rows = pl.ds(aligned(half * HALF), HALF)
+        part = q_ref[pl.ds(half * 2, 2)].reshape(HALF, width)
+        total_ref[rows, :] += jnp.dot(
+            scores(part, at), hot_ref[at, :], preferred_element_type=jnp.float32
+        )
         return carry
 
-    lax.fori_loop(0, tiles, step, 0)
-    cut = COMMON * KT
-    total_ref[...] = jnp.dot(
-        scores_ref[:, :cut], hot_ref[:cut, :], preferred_element_type=jnp.float32
-    )
-
-    @pl.when(tiles > COMMON)
-    def _():
-        total_ref[...] += jnp.dot(
-            scores_ref[:, cut:], hot_ref[cut:, :], preferred_element_type=jnp.float32
-        )
+    lax.fori_loop(0, 2 * (tiles - COMMON), rest, 0)
 
 
 def sums(shifts, halves, coded, facts, queries, keys, hots, arrived=()):
@@ -178,7 +182,6 @@
                 copy_queries(block, part).start()
         for at in range(joined):
             copy_came(at).start()
-        scores_ref[:, COMMON * KT :] = jnp.zeros((SUPER, CAP - COMMON * KT), jnp.bfloat16)
         if coded:
             for at in range(4):
                 clear_tail(msg_ref.at[at], HALF)
@@ -233,7 +236,7 @@
         out_shape=[HALF_MSG if coded else HALF_RAW] * 4 + [jax.ShapeDtypeStruct((4,), jnp.int32)],
         scratch_shapes=[
             pltpu.VMEM((2, SIDE, QT, width), jnp.bfloat16),
-            pltpu.VMEM((SUPER, CAP), jnp.bfloat16),
+            pltpu.VMEM((SUPER, COMMON * KT), jnp.bfloat16),
             pltpu.VMEM((2, SUPER, CB), jnp.float32),
             pltpu.VMEM((4,) + HALF_MSG.shape, jnp.int16),
             pltpu.VMEM((4,) + HALF_MSG.shape, jnp.int16),

time: 206 us -> 211 us (1.024)
  blocking collectives: 27.9 us -> 37.3 us
  Pallas kernels: 64.1 us -> 60.5 us
  starting transfers between devices: 24.8 us -> 27 us
    all_gather x1, blocking collectives: 12.2 us -> 21.7 us  [per_device(): return finish(logits, lax.all_gather(stats, 'cls'))]
    pallas_call x4, Pallas kernels: 51.7 us -> 48.1 us  [sums(): pl.pallas_call(kernel, in_specs=[smem, anywhere, vmem, vmem] + [anywhere]...]
    ppermute x18, starting transfers between devices: 24.8 us -> 27 us  [send(): return lax.ppermute(message, 'cache', shifted(dx, dz))]
  transfers between devices with their start and end apart: 19 -> 19, of which waited for: 6 -> 5; matrix products, arithmetic and copies ran while one was open for 16% -> 15% of each run, Pallas kernels for 23% -> 21%
where the time goes in v4:
time: 211 us; the launch traced here: 212 us
  Pallas kernels  60.5 us (29%)
  blocking collectives  37.3 us (18%)
  local copies, waits for them, and re-layouts  30.5 us (14%)
  starting transfers between devices  27 us (13%)
  waiting for transfers between devices  26.4 us (13%)
  between operations  19.9 us (9%)
  other arithmetic  8.11 us (4%)
    pallas_call x4, Pallas kernels, sums(): pl.pallas_call(kernel, in_specs=[smem, anywhere, vmem, vmem] + [anywhere]...  48.1 us
    ppermute x18, starting transfers between devices, send(): return lax.ppermute(message, 'cache', shifted(dx, dz))  27 us
    gather x1, local copies, waits for them, and re-layouts, per_device(): rows = jnp.take(cache_keys, picked % 16384, axis=0, mode='clip')  21.8 us
    all_gather x1, blocking collectives, per_device(): return finish(logits, lax.all_gather(stats, 'cls'))  21.7 us
    all_gather x1, blocking collectives, per_device(): lax.all_gather(unit_queries, 'cls', axis=0, tiled=True)  15.6 us
    ppermute x18, waiting for transfers between devices, send(): return lax.ppermute(message, 'cache', shifted(dx, dz))  13.7 us
    all_gather x1, waiting for transfers between devices, per_device(): lax.all_gather(unit_queries, ('cache', 'cls'), axis=0, tiled=True)  12.8 us
    unnamed x16, local copies, waits for them, and re-layouts  8.54 us
  transfers between devices with their start and end apart: 19, of which 5 were waited for; matrix products, arithmetic and copies ran while one was open for 15% of the time, Pallas kernels for 21%

profile of v4, /device:TPU:1, one launch (start us, length us, event | category | flops | bytes accessed | tf_op | source)
XLA Modules:
  0.0 211.7 jit_solution(12255807549008247685)
XLA Ops:
  6.5 1.0 copy-done.4
  7.5 0.7 unit.1
  8.2 0.0 all-gather.4.cloned.1.call-update
  8.3 1.5 convert_reduce_fusion
  14.9 6.3 %sort.7 = s32[10240]{0:T(1024)S(1)} sort(s32[10240]{0:T(1024)S(1)} %get-tuple-element.82), dimensions={0}, to_apply=%region_0.1 | sort | flops 143360 | bytes 81920 | tf_op jit(solution)/shard_map/sort | solution.py:386
  22.4 0.1 pad_dynamic-slice_fusion
  22.6 0.1 fusion
  22.7 21.8 %gather_fusion = bf16[2560,1024]{1,0:T(8,128)(2,1)} fusion(bf16[10240,1024]{1,0:T(8,128)(2,1)} %param.5, s32[3072]{0:T(1024)S(1)} %pad_clamp_fusion), kind=kCustom, calls=%fused_computation | custom fusion | bytes 10496000 | tf_op jit(solution)/shard_map/jit(_take)/gather | solution.py:399
  44.5 15.6 %all_gather.12 = bf16[256,1024]{1,0:T(8,128)(2,1)S(1)} all-gather(bf16[32,1024]{1,0:T(8,128)(2,1)} %unit.1), channel_id=1, replica_groups=mesh['cache'=16,'cls'=8] {'cls'}, dimensions={0}, use_global_device_ids=true | all-gather | bytes 589824 | tf_op jit(solution)/shard_map/all_gather | solution.py:401
  60.1 1.9 convolution_multiply_fusion.text_ref
  62.0 0.1 fusion.2
  62.1 0.1 pad_add_fusion.facts_ref
  62.2 0.1 compare_select_fusion.2.labels_ref
  62.3 2.6 %copy-done.2 = bf16[2560,1024]{1,0:T(8,128)(2,1)S(1)} copy-done((bf16[2560,1024]{1,0:T(8,128)(2,1)S(1)}, bf16[2560,1024]{1,0:T(8,128)(2,1)}, u32[]{:S(2)}) %copy-start.2) | copy-done | bytes 5242904
  65.0 4.2 %prepare.1 = (bf16[2560,1024]{1,0:T(8,128)(2,1)S(1)}, bf16[2560,640]{1,0:T(8,128)(2,1)S(1)}, s32[4]{0:T(128)S(1)}) custom-call(s32[4]{0:T(128)S(1)} %pad_add_fusion.facts_ref, bf16[2560,1024]{1,0:T(8,128)(2,1)S(1)} %copy-done.2, s32[10,1,256]{2,1,0:T(1,128)S(1)} %compare_select_fusion.2.labels_ref), custom_call_target="tpu_custom_call" | custom-call | flops 10485760 | bytes 15728640 | tf_op jit(solution)/shard_map/prepare/pallas_call | solution.py:42
  69.2 2.4 %copy-done.5 = bf16[2560,1024]{1,0:T(8,128)(2,1)} copy-done((bf16[2560,1024]{1,0:T(8,128)(2,1)}, bf16[2560,1024]{1,0:T(8,128)(2,1)S(1)}, u32[]{:S(2)}) %copy-start.5) | copy-done | bytes 5242904
  71.6 12.8 %all-gather.4.cloned.1.call-done = bf16[4096,1024]{1,0:T(8,128)(2,1)} async-done(((bf16[32,1024]{1,0:T(8,128)(2,1)}), bf16[4096,1024]{1,0:T(8,128)(2,1)}) %all-gather.4.cloned.1.call-update) | async-done | bytes 8388624 | tf_op jit(solution)/shard_map/all_gather | solution.py:384
  84.3 2.5 %copy-done.6 = bf16[2560,1024]{1,0:T(8,128)(2,1)S(1)} copy-done((bf16[2560,1024]{1,0:T(8,128)(2,1)S(1)}, bf16[2560,1024]{1,0:T(8,128)(2,1)}, u32[]{:S(2)}) %copy-start.6) | copy-done | bytes 5242904
  86.8 12.0 %sums.4 = (s16[528,640]{1,0:T(8,128)(2,1)S(1)}, s16[528,640]{1,0:T(8,128)(2,1)S(1)}, s16[528,640]{1,0:T(8,128)(2,1)S(1)}, s16[528,640]{1,0:T(8,128)(2,1)S(1)}, s32[4]{0:T(128)S(1)}) custom-call(s32[4]{0:T(128)S(1)} %get-tuple-element.44.facts_ref, bf16[16,256,1024]{2,1,0:T(8,128)(2,1)} %bitcast.9, bf16[2560,1024]{1,0:T(8,128)(2,1)S(1)} %copy-done.6, ...), custom_call_target="tpu_custom_call" | custom-call | flops 8724152320 | bytes 4194304 | tf_op jit(solution)/shard_map/sums/pallas_call | solution.py:232
  98.8 0.1 collective-permute-start
  98.9 2.7 %collective-permute-start.1 = (s16[528,640]{1,0:T(8,128)(2,1)S(1)}, s16[528,640]{1,0:T(8,128)(2,1)S(1)}, u32[]{:S(2)}, u32[]{:S(2)}) collective-permute-start(s16[528,640]{1,0:T(8,128)(2,1)S(1)} %get-tuple-element.51), channel_id=1, source_target_pairs={{0,96},{8,104},{16,112},{24,120},{32,0},{40,8},{48,16},{56,24},{64... | collective-permute-start | bytes 2027528 | tf_op jit(solution)/shard_map/ppermute | solution.py:374
  101.6 0.0 collective-permute-start.2
  101.6 2.7 %collective-permute-start.3 = (s16[528,640]{1,0:T(8,128)(2,1)S(1)}, s16[528,640]{1,0:T(8,128)(2,1)S(1)}, u32[]{:S(2)}, u32[]{:S(2)}) collective-permute-start(s16[528,640]{1,0:T(8,128)(2,1)S(1)} %get-tuple-element.53), channel_id=1, source_target_pairs={{0,24},{8,0},{16,8},{24,16},{32,56},{40,32},{48,40},{56,48},{64,88... | collective-permute-start | bytes 2027528 | tf_op jit(solution)/shard_map/ppermute | solution.py:374
  104.3 12.2 %sums.5 = (s16[528,640]{1,0:T(8,128)(2,1)S(1)}, s16[528,640]{1,0:T(8,128)(2,1)S(1)}, s16[528,640]{1,0:T(8,128)(2,1)S(1)}, s16[528,640]{1,0:T(8,128)(2,1)S(1)}, s32[4]{0:T(128)S(1)}) custom-call(s32[4]{0:T(128)S(1)} %get-tuple-element.48.facts_ref, bf16[16,256,1024]{2,1,0:T(8,128)(2,1)} %bitcast.10, bf16[2560,1024]{1,0:T(8,128)(2,1)S(1)} %copy-done.6, ...), custom_call_target="tpu_custom_call" | custom-call | flops 8724152320 | bytes 4194304 | tf_op jit(solution)/shard_map/sums/pallas_call | solution.py:232
  116.5 1.3 collective-permute-start.4
  117.7 0.0 collective-permute-done.rest_0_
  117.7 0.3 collective-permute-start.5
  118.0 0.0 collective-permute-done.1.rest_1_
  118.0 3.4 %collective-permute-start.6 = (s16[528,640]{1,0:T(8,128)(2,1)S(1)}, s16[528,640]{1,0:T(8,128)(2,1)S(1)}, u32[]{:S(2)}, u32[]{:S(2)}) collective-permute-start(s16[528,640]{1,0:T(8,128)(2,1)S(1)} %get-tuple-element.57), channel_id=1, source_target_pairs={{0,24},{8,0},{16,8},{24,16},{32,56},{40,32},{48,40},{56,48},{64,88... | collective-permute-start | bytes 2027528 | tf_op jit(solution)/shard_map/ppermute | solution.py:374
  121.4 0.0 collective-permute-done.2.rest_2_
  121.4 0.0 collective-permute-start.7
  121.4 0.0 collective-permute-done.3.rest_3_
  121.4 13.0 %sums.6 = (s16[528,640]{1,0:T(8,128)(2,1)S(1)}, s16[528,640]{1,0:T(8,128)(2,1)S(1)}, s16[528,640]{1,0:T(8,128)(2,1)S(1)}, s16[528,640]{1,0:T(8,128)(2,1)S(1)}, s32[4]{0:T(128)S(1)}) custom-call(s32[4]{0:T(128)S(1)} %get-tuple-element.49.facts_ref, bf16[16,256,1024]{2,1,0:T(8,128)(2,1)} %bitcast.11, bf16[2560,1024]{1,0:T(8,128)(2,1)S(1)} %copy-done.6, ...), custom_call_target="tpu_custom_call" | custom-call | flops 8724152320 | bytes 4194304 | tf_op jit(solution)/shard_map/sums/pallas_call | solution.py:232
  134.4 0.5 collective-permute-start.8
  134.9 0.0 collective-permute-done.4.rest_0_
  134.9 2.2 %collective-permute-start.9 = (s16[528,640]{1,0:T(8,128)(2,1)S(1)}, s16[528,640]{1,0:T(8,128)(2,1)S(1)}, u32[]{:S(2)}, u32[]{:S(2)}) collective-permute-start(s16[528,640]{1,0:T(8,128)(2,1)S(1)} %get-tuple-element.62), channel_id=1, source_target_pairs={{0,96},{8,104},{16,112},{24,120},{32,0},{40,8},{48,16},{56,24},{64... | collective-permute-start | bytes 2027528 | tf_op jit(solution)/shard_map/ppermute | solution.py:374
  137.1 0.0 collective-permute-done.5.rest_1_
  137.1 0.0 collective-permute-start.10
  137.1 0.0 collective-permute-done.6.rest_2_
  137.2 4.8 %collective-permute-start.11 = (s16[528,640]{1,0:T(8,128)(2,1)S(1)}, s16[528,640]{1,0:T(8,128)(2,1)S(1)}, u32[]{:S(2)}, u32[]{:S(2)}) collective-permute-start(s16[528,640]{1,0:T(8,128)(2,1)S(1)} %get-tuple-element.67), channel_id=1, source_target_pairs={{0,24},{8,0},{16,8},{24,16},{32,56},{40,32},{48,40},{56,48},{64,88... | collective-permute-start | bytes 2027528 | tf_op jit(solution)/shard_map/ppermute | solution.py:374
  142.0 0.0 collective-permute-done.7.rest_3_
  142.0 10.9 %sums.7 = (f32[512,640]{1,0:T(8,128)S(1)}, f32[512,640]{1,0:T(8,128)S(1)}, f32[512,640]{1,0:T(8,128)S(1)}, f32[512,640]{1,0:T(8,128)S(1)}, s32[4]{0:T(128)}) custom-call(s32[4]{0:T(128)S(1)} %get-tuple-element.54.facts_ref, bf16[16,256,1024]{2,1,0:T(8,128)(2,1)} %bitcast.12, bf16[2560,1024]{1,0:T(8,128)(2,1)S(1)} %copy-done.6, ...), custom_call_target="tpu_custom_call" | custom-call | flops 8724152320 | bytes 4194304 | tf_op jit(solution)/shard_map/sums/pallas_call | solution.py:232
  152.9 0.0 collective-permute-done.10.low_msg
  152.9 0.0 collective-permute-done.11.high_msg
  152.9 2.6 %turn.3 = (f32[256,640]{1,0:T(8,128)S(1)}, s16[272,640]{1,0:T(8,128)(2,1)S(1)}, s16[272,640]{1,0:T(8,128)(2,1)S(1)}, s16[272,640]{1,0:T(8,128)(2,1)S(1)}) custom-call(s32[1]{0:T(128)} %bitcast.1.place_ref, f32[512,640]{1,0:T(8,128)S(1)} %get-tuple-element.64.low_hbm, f32[512,640]{1,0:T(8,128)S(1)} %get-tuple-element.65.high_hbm, ...), custom_call_target="tpu_custom_call" | custom-call | flops 6553600 | bytes 6553600 | tf_op jit(solution)/shard_map/turn/pallas_call | solution.py:301
  155.5 0.0 copy-start.3
  155.5 3.3 %collective-permute-start.15 = (s16[272,640]{1,0:T(8,128)(2,1)S(1)}, s16[272,640]{1,0:T(8,128)(2,1)S(1)}, u32[]{:S(2)}, u32[]{:S(2)}) collective-permute-start(s16[272,640]{1,0:T(8,128)(2,1)S(1)} %get-tuple-element.72), channel_id=1, source_target_pairs={{0,64},{8,72},{16,80},{24,88},{32,96},{40,104},{48,112},{56,120},{... | collective-permute-start | bytes 1044488 | tf_op jit(solution)/shard_map/ppermute | solution.py:374
  158.8 0.0 collective-permute-start.16
  158.8 2.7 %collective-permute-start.17 = (s16[272,640]{1,0:T(8,128)(2,1)S(1)}, s16[272,640]{1,0:T(8,128)(2,1)S(1)}, u32[]{:S(2)}, u32[]{:S(2)}) collective-permute-start(s16[272,640]{1,0:T(8,128)(2,1)S(1)} %get-tuple-element.74), channel_id=1, source_target_pairs={{0,96},{8,104},{16,112},{24,120},{32,0},{40,8},{48,16},{56,24},{64... | collective-permute-start | bytes 1044488 | tf_op jit(solution)/shard_map/ppermute | solution.py:374
  161.5 0.0 collective-permute-done.8.low_msg
  161.5 0.0 collective-permute-done.9.high_msg
  161.5 2.6 %turn.2 = (f32[256,640]{1,0:T(8,128)S(1)}, s16[272,640]{1,0:T(8,128)(2,1)S(1)}, s16[272,640]{1,0:T(8,128)(2,1)S(1)}, s16[272,640]{1,0:T(8,128)(2,1)S(1)}) custom-call(s32[1]{0:T(128)} %bitcast.place_ref, f32[512,640]{1,0:T(8,128)S(1)} %get-tuple-element.59.low_hbm, f32[512,640]{1,0:T(8,128)S(1)} %get-tuple-element.60.high_hbm, ...), custom_call_target="tpu_custom_call" | custom-call | flops 6553600 | bytes 6553600 | tf_op jit(solution)/shard_map/turn/pallas_call | solution.py:301
  164.0 0.1 collective-permute-start.12
  164.1 2.9 %collective-permute-start.13 = (s16[272,640]{1,0:T(8,128)(2,1)S(1)}, s16[272,640]{1,0:T(8,128)(2,1)S(1)}, u32[]{:S(2)}, u32[]{:S(2)}) collective-permute-start(s16[272,640]{1,0:T(8,128)(2,1)S(1)} %get-tuple-element.70), channel_id=1, source_target_pairs={{0,8},{8,16},{16,24},{24,0},{32,40},{40,48},{48,56},{56,32},{64,72... | collective-permute-start | bytes 1044488 | tf_op jit(solution)/shard_map/ppermute | solution.py:374
  167.0 0.0 collective-permute-done.15.rest_5_
  167.0 0.2 collective-permute-start.14
  167.2 2.1 collective-permute-done.16.rest_6_
  169.3 1.5 collective-permute-done.17.rest_7_
  170.8 1.3 collective-permute-done.12.rest_2_
  172.0 8.8 %collective-permute-done.13.rest_3_ = s16[272,640]{1,0:T(8,128)(2,1)S(1)} collective-permute-done((s16[272,640]{1,0:T(8,128)(2,1)S(1)}, s16[272,640]{1,0:T(8,128)(2,1)S(1)}, u32[]{:S(2)}, u32[]{:S(2)}) %collective-permute-start.13) | collective-permute-done | bytes 348192 | tf_op jit(solution)/shard_map/ppermute | solution.py:374
  180.8 0.0 collective-permute-done.14.rest_4_
  180.8 1.0 close.1
  181.8 21.7 %all-gather.1.stats_ref = f32[8,2,256]{2,1,0:T(2,128)S(1)} all-gather(f32[1,2,256]{2,1,0:T(2,128)S(1)} %bitcast.8), channel_id=2, replica_groups=mesh['cache'=16,'cls'=8] {'cls'}, dimensions={0}, use_global_device_ids=true | all-gather | bytes 18432 | tf_op jit(solution)/shard_map/all_gather | solution.py:437
  203.5 1.3 finish.1
  (17 shorter events, 0.1 us)
Async XLA Ops:
  6.5 53.6 %copy-start = (bf16[1280,1024]{1,0:T(8,128)(2,1)S(1)}, bf16[1280,1024]{1,0:T(8,128)(2,1)}, u32[]{:S(2)}) copy-start(bf16[1280,1024]{1,0:T(8,128)(2,1)} %param.7) | copy-start | bytes 7864324
  6.5 77.8 %all-gather.4.cloned.1.call-start = ((), (), s32[]{:S(2)}) async-start(), calls=%async_computation | async-start | bytes 8454144 | tf_op jit(solution)/shard_map/all_gather | solution.py:384
  6.5 1.0 copy-start.4
  62.3 2.6 %copy-start.2 = (bf16[2560,1024]{1,0:T(8,128)(2,1)S(1)}, bf16[2560,1024]{1,0:T(8,128)(2,1)}, u32[]{:S(2)}) copy-start(bf16[2560,1024]{1,0:T(8,128)(2,1)} %gather_fusion) | copy-start | bytes 15728644
  69.2 2.4 %copy-start.5 = (bf16[2560,1024]{1,0:T(8,128)(2,1)}, bf16[2560,1024]{1,0:T(8,128)(2,1)S(1)}, u32[]{:S(2)}) copy-start(bf16[2560,1024]{1,0:T(8,128)(2,1)S(1)} %get-tuple-element.46.keys_ref) | copy-start | bytes 15728644
  84.3 2.5 %copy-start.6 = (bf16[2560,1024]{1,0:T(8,128)(2,1)S(1)}, bf16[2560,1024]{1,0:T(8,128)(2,1)}, u32[]{:S(2)}) copy-start(bf16[2560,1024]{1,0:T(8,128)(2,1)} %copy-done.5) | copy-start | bytes 15728644
  98.8 18.9 %collective-permute-start = (s16[528,640]{1,0:T(8,128)(2,1)S(1)}, s16[528,640]{1,0:T(8,128)(2,1)S(1)}, u32[]{:S(2)}, u32[]{:S(2)}) collective-permute-start(s16[528,640]{1,0:T(8,128)(2,1)S(1)} %get-tuple-element.50), channel_id=1, source_target_pairs={{0,32},{8,40},{16,48},{24,56},{32,64},{40,72},{48,80},{56,88},{64,... | collective-permute-start | bytes 2027528 | tf_op jit(solution)/shard_map/ppermute | solution.py:374
  98.9 19.1 %collective-permute-start.1 = (s16[528,640]{1,0:T(8,128)(2,1)S(1)}, s16[528,640]{1,0:T(8,128)(2,1)S(1)}, u32[]{:S(2)}, u32[]{:S(2)}) collective-permute-start(s16[528,640]{1,0:T(8,128)(2,1)S(1)} %get-tuple-element.51), channel_id=1, source_target_pairs={{0,96},{8,104},{16,112},{24,120},{32,0},{40,8},{48,16},{56,24},{64... | collective-permute-start | bytes 2027528 | tf_op jit(solution)/shard_map/ppermute | solution.py:374
  101.6 19.8 %collective-permute-start.2 = (s16[528,640]{1,0:T(8,128)(2,1)S(1)}, s16[528,640]{1,0:T(8,128)(2,1)S(1)}, u32[]{:S(2)}, u32[]{:S(2)}) collective-permute-start(s16[528,640]{1,0:T(8,128)(2,1)S(1)} %get-tuple-element.52), channel_id=1, source_target_pairs={{0,8},{8,16},{16,24},{24,0},{32,40},{40,48},{48,56},{56,32},{64,72... | collective-permute-start | bytes 2027528 | tf_op jit(solution)/shard_map/ppermute | solution.py:374
  101.6 19.8 %collective-permute-start.3 = (s16[528,640]{1,0:T(8,128)(2,1)S(1)}, s16[528,640]{1,0:T(8,128)(2,1)S(1)}, u32[]{:S(2)}, u32[]{:S(2)}) collective-permute-start(s16[528,640]{1,0:T(8,128)(2,1)S(1)} %get-tuple-element.53), channel_id=1, source_target_pairs={{0,24},{8,0},{16,8},{24,16},{32,56},{40,32},{48,40},{56,48},{64,88... | collective-permute-start | bytes 2027528 | tf_op jit(solution)/shard_map/ppermute | solution.py:374
  116.5 18.4 %collective-permute-start.4 = (s16[528,640]{1,0:T(8,128)(2,1)S(1)}, s16[528,640]{1,0:T(8,128)(2,1)S(1)}, u32[]{:S(2)}, u32[]{:S(2)}) collective-permute-start(s16[528,640]{1,0:T(8,128)(2,1)S(1)} %get-tuple-element.55), channel_id=1, source_target_pairs={{0,96},{8,104},{16,112},{24,120},{32,0},{40,8},{48,16},{56,24},{64... | collective-permute-start | bytes 2027528 | tf_op jit(solution)/shard_map/ppermute | solution.py:374
  117.7 19.4 %collective-permute-start.5 = (s16[528,640]{1,0:T(8,128)(2,1)S(1)}, s16[528,640]{1,0:T(8,128)(2,1)S(1)}, u32[]{:S(2)}, u32[]{:S(2)}) collective-permute-start(s16[528,640]{1,0:T(8,128)(2,1)S(1)} %get-tuple-element.56), channel_id=1, source_target_pairs={{0,32},{8,40},{16,48},{24,56},{32,64},{40,72},{48,80},{56,88},{64,... | collective-permute-start | bytes 2027528 | tf_op jit(solution)/shard_map/ppermute | solution.py:374
  118.0 19.2 %collective-permute-start.6 = (s16[528,640]{1,0:T(8,128)(2,1)S(1)}, s16[528,640]{1,0:T(8,128)(2,1)S(1)}, u32[]{:S(2)}, u32[]{:S(2)}) collective-permute-start(s16[528,640]{1,0:T(8,128)(2,1)S(1)} %get-tuple-element.57), channel_id=1, source_target_pairs={{0,24},{8,0},{16,8},{24,16},{32,56},{40,32},{48,40},{56,48},{64,88... | collective-permute-start | bytes 2027528 | tf_op jit(solution)/shard_map/ppermute | solution.py:374
  121.4 20.6 %collective-permute-start.7 = (s16[528,640]{1,0:T(8,128)(2,1)S(1)}, s16[528,640]{1,0:T(8,128)(2,1)S(1)}, u32[]{:S(2)}, u32[]{:S(2)}) collective-permute-start(s16[528,640]{1,0:T(8,128)(2,1)S(1)} %get-tuple-element.58), channel_id=1, source_target_pairs={{0,8},{8,16},{16,24},{24,0},{32,40},{40,48},{48,56},{56,32},{64,72... | collective-permute-start | bytes 2027528 | tf_op jit(solution)/shard_map/ppermute | solution.py:374
  134.4 27.1 %collective-permute-start.8 = (s16[528,640]{1,0:T(8,128)(2,1)S(1)}, s16[528,640]{1,0:T(8,128)(2,1)S(1)}, u32[]{:S(2)}, u32[]{:S(2)}) collective-permute-start(s16[528,640]{1,0:T(8,128)(2,1)S(1)} %get-tuple-element.61), channel_id=1, source_target_pairs={{0,32},{8,40},{16,48},{24,56},{32,64},{40,72},{48,80},{56,88},{64,... | collective-permute-start | bytes 2027528 | tf_op jit(solution)/shard_map/ppermute | solution.py:374
  134.9 26.6 %collective-permute-start.9 = (s16[528,640]{1,0:T(8,128)(2,1)S(1)}, s16[528,640]{1,0:T(8,128)(2,1)S(1)}, u32[]{:S(2)}, u32[]{:S(2)}) collective-permute-start(s16[528,640]{1,0:T(8,128)(2,1)S(1)} %get-tuple-element.62), channel_id=1, source_target_pairs={{0,96},{8,104},{16,112},{24,120},{32,0},{40,8},{48,16},{56,24},{64... | collective-permute-start | bytes 2027528 | tf_op jit(solution)/shard_map/ppermute | solution.py:374
  137.1 15.8 %collective-permute-start.10 = (s16[528,640]{1,0:T(8,128)(2,1)S(1)}, s16[528,640]{1,0:T(8,128)(2,1)S(1)}, u32[]{:S(2)}, u32[]{:S(2)}) collective-permute-start(s16[528,640]{1,0:T(8,128)(2,1)S(1)} %get-tuple-element.66), channel_id=1, source_target_pairs={{0,8},{8,16},{16,24},{24,0},{32,40},{40,48},{48,56},{56,32},{64,72... | collective-permute-start | bytes 2027528 | tf_op jit(solution)/shard_map/ppermute | solution.py:374
  137.2 15.8 %collective-permute-start.11 = (s16[528,640]{1,0:T(8,128)(2,1)S(1)}, s16[528,640]{1,0:T(8,128)(2,1)S(1)}, u32[]{:S(2)}, u32[]{:S(2)}) collective-permute-start(s16[528,640]{1,0:T(8,128)(2,1)S(1)} %get-tuple-element.67), channel_id=1, source_target_pairs={{0,24},{8,0},{16,8},{24,16},{32,56},{40,32},{48,40},{56,48},{64,88... | collective-permute-start | bytes 2027528 | tf_op jit(solution)/shard_map/ppermute | solution.py:374
  155.5 25.3 %copy-start.3 = (f32[256,1280]{1,0:T(8,128)S(1)}, f32[256,1280]{1,0:T(8,128)}, u32[]{:S(2)}) copy-start(f32[256,1280]{1,0:T(8,128)} %convolution_multiply_fusion.text_ref) | copy-start | bytes 3932164
  155.5 11.5 %collective-permute-start.15 = (s16[272,640]{1,0:T(8,128)(2,1)S(1)}, s16[272,640]{1,0:T(8,128)(2,1)S(1)}, u32[]{:S(2)}, u32[]{:S(2)}) collective-permute-start(s16[272,640]{1,0:T(8,128)(2,1)S(1)} %get-tuple-element.72), channel_id=1, source_target_pairs={{0,64},{8,72},{16,80},{24,88},{32,96},{40,104},{48,112},{56,120},{... | collective-permute-start | bytes 1044488 | tf_op jit(solution)/shard_map/ppermute | solution.py:374
  158.8 10.5 %collective-permute-start.16 = (s16[272,640]{1,0:T(8,128)(2,1)S(1)}, s16[272,640]{1,0:T(8,128)(2,1)S(1)}, u32[]{:S(2)}, u32[]{:S(2)}) collective-permute-start(s16[272,640]{1,0:T(8,128)(2,1)S(1)} %get-tuple-element.73), channel_id=1, source_target_pairs={{0,32},{8,40},{16,48},{24,56},{32,64},{40,72},{48,80},{56,88},{64,... | collective-permute-start | bytes 1044488 | tf_op jit(solution)/shard_map/ppermute | solution.py:374
  158.8 12.0 %collective-permute-start.17 = (s16[272,640]{1,0:T(8,128)(2,1)S(1)}, s16[272,640]{1,0:T(8,128)(2,1)S(1)}, u32[]{:S(2)}, u32[]{:S(2)}) collective-permute-start(s16[272,640]{1,0:T(8,128)(2,1)S(1)} %get-tuple-element.74), channel_id=1, source_target_pairs={{0,96},{8,104},{16,112},{24,120},{32,0},{40,8},{48,16},{56,24},{64... | collective-permute-start | bytes 1044488 | tf_op jit(solution)/shard_map/ppermute | solution.py:374
  164.0 8.0 %collective-permute-start.12 = (s16[272,640]{1,0:T(8,128)(2,1)S(1)}, s16[272,640]{1,0:T(8,128)(2,1)S(1)}, u32[]{:S(2)}, u32[]{:S(2)}) collective-permute-start(s16[272,640]{1,0:T(8,128)(2,1)S(1)} %get-tuple-element.69), channel_id=1, source_target_pairs={{0,16},{8,24},{16,0},{24,8},{32,48},{40,56},{48,32},{56,40},{64,80... | collective-permute-start | bytes 1044488 | tf_op jit(solution)/shard_map/ppermute | solution.py:374
  164.1 16.7 %collective-permute-start.13 = (s16[272,640]{1,0:T(8,128)(2,1)S(1)}, s16[272,640]{1,0:T(8,128)(2,1)S(1)}, u32[]{:S(2)}, u32[]{:S(2)}) collective-permute-start(s16[272,640]{1,0:T(8,128)(2,1)S(1)} %get-tuple-element.70), channel_id=1, source_target_pairs={{0,8},{8,16},{16,24},{24,0},{32,40},{40,48},{48,56},{56,32},{64,72... | collective-permute-start | bytes 1044488 | tf_op jit(solution)/shard_map/ppermute | solution.py:374
  167.0 13.8 %collective-permute-start.14 = (s16[272,640]{1,0:T(8,128)(2,1)S(1)}, s16[272,640]{1,0:T(8,128)(2,1)S(1)}, u32[]{:S(2)}, u32[]{:S(2)}) collective-permute-start(s16[272,640]{1,0:T(8,128)(2,1)S(1)} %get-tuple-element.71), channel_id=1, source_target_pairs={{0,24},{8,0},{16,8},{24,16},{32,56},{40,32},{48,40},{56,48},{64,88... | collective-permute-start | bytes 1044488 | tf_op jit(solution)/shard_map/ppermute | solution.py:374
  180.8 24.0 %copy-start.1 = (bf16[1280,1024]{1,0:T(8,128)(2,1)S(1)}, bf16[1280,1024]{1,0:T(8,128)(2,1)}, u32[]{:S(2)}) copy-start(bf16[1280,1024]{1,0:T(8,128)(2,1)} %param.7) | copy-start | bytes 7864324
Sparse Core Ops, SparseCore 0:
  10.3 73.9 all-gather.3

commit v5 on v3

--- a/solution.py
+++ b/solution.py
@@ -127,25 +127,34 @@
     sharpness = float(width) ** 0.5 * math.log2(math.e)
     queries = q_ref[...].reshape(SUPER, width)
 
-    def step(t, carry):
-        at = pl.ds(aligned(t * KT), KT)
+    def scores(at):
         cosine = lax.dot_general(
             queries, keys_ref[at, :], (((1,), (1,)), ((), ())), preferred_element_type=jnp.float32
         )
         scores_ref[:, at] = jnp.exp2(sharpness * cosine).astype(jnp.bfloat16)
-        return carry
-
-    lax.fori_loop(0, tiles, step, 0)
+
     cut = COMMON * KT
+    for t in range(COMMON):
+        scores(pl.ds(t * KT, KT))
     total_ref[...] = jnp.dot(
         scores_ref[:, :cut], hot_ref[:cut, :], preferred_element_type=jnp.float32
     )
 
     @pl.when(tiles > COMMON)
     def _():
-        total_ref[...] += jnp.dot(
-            scores_ref[:, cut:], hot_ref[cut:, :], preferred_element_type=jnp.float32
-        )
+        def step(t, carry):
+            scores(pl.ds(aligned(t * KT), KT))
+            return carry
+
+        def rest(i, carry):
+            rows = pl.ds(aligned(i * HALF), HALF)
+            total_ref[rows, :] += jnp.dot(
+                scores_ref[rows, cut:], hot_ref[cut:, :], preferred_element_type=jnp.float32
+            )
+            return carry
+
+        lax.fori_loop(COMMON, tiles, step, 0)
+        lax.fori_loop(0, 2, rest, 0)
 
 
 def sums(shifts, halves, coded, facts, queries, keys, hots, arrived=()):

time: 206 us -> 207 us (level)
  waiting for transfers between devices: 28.5 us -> 37.6 us
  starting transfers between devices: 24.8 us -> 18 us
  Pallas kernels: 64.1 us -> 60.4 us
    ppermute x18, waiting for transfers between devices: 15.7 us -> 24.9 us  [send(): return lax.ppermute(message, 'cache', shifted(dx, dz))]
    ppermute x18, starting transfers between devices: 24.8 us -> 18 us  [send(): return lax.ppermute(message, 'cache', shifted(dx, dz))]
    pallas_call x4, Pallas kernels: 51.7 us -> 48.1 us  [sums(): pl.pallas_call(kernel, in_specs=[smem, anywhere, vmem, vmem] + [anywhere]...]
  transfers between devices with their start and end apart: 19 -> 19, of which waited for: 6 -> 8; matrix products, arithmetic and copies ran while one was open for 16% -> 16% of each run, Pallas kernels for 23% -> 22%
where the time goes in v5:
time: 207 us; the launch traced here: 206 us
  Pallas kernels  60.4 us (29%)
  waiting for transfers between devices  37.6 us (18%)
  local copies, waits for them, and re-layouts  30.5 us (15%)
  blocking collectives  29.2 us (14%)
  between operations  19.9 us (10%)
  starting transfers between devices  18 us (9%)
  other arithmetic  8.11 us (4%)
    pallas_call x4, Pallas kernels, sums(): pl.pallas_call(kernel, in_specs=[smem, anywhere, vmem, vmem] + [anywhere]...  48.1 us
    ppermute x18, waiting for transfers between devices, send(): return lax.ppermute(message, 'cache', shifted(dx, dz))  24.9 us
    gather x1, local copies, waits for them, and re-layouts, per_device(): rows = jnp.take(cache_keys, picked % 16384, axis=0, mode='clip')  21.8 us
    ppermute x18, starting transfers between devices, send(): return lax.ppermute(message, 'cache', shifted(dx, dz))  18 us
    all_gather x1, blocking collectives, per_device(): lax.all_gather(unit_queries, 'cls', axis=0, tiled=True)  15.6 us
    all_gather x1, blocking collectives, per_device(): return finish(logits, lax.all_gather(stats, 'cls'))  13.6 us
    all_gather x1, waiting for transfers between devices, per_device(): lax.all_gather(unit_queries, ('cache', 'cls'), axis=0, tiled=True)  12.8 us
    unnamed x16, local copies, waits for them, and re-layouts  8.54 us
  transfers between devices with their start and end apart: 19, of which 8 were waited for; matrix products, arithmetic and copies ran while one was open for 16% of the time, Pallas kernels for 22%

profile of v5, /device:TPU:1, one launch (start us, length us, event | category | flops | bytes accessed | tf_op | source)
XLA Modules:
  0.0 205.7 jit_solution(16346003266417467549)
XLA Ops:
  6.5 1.0 copy-done.4
  7.5 0.7 unit.1
  8.2 0.0 all-gather.4.cloned.1.call-update
  8.3 1.5 convert_reduce_fusion
  14.9 6.3 %sort.7 = s32[10240]{0:T(1024)S(1)} sort(s32[10240]{0:T(1024)S(1)} %get-tuple-element.82), dimensions={0}, to_apply=%region_0.1 | sort | flops 143360 | bytes 81920 | tf_op jit(solution)/shard_map/sort | solution.py:392
  22.4 0.1 pad_dynamic-slice_fusion
  22.6 0.1 fusion
  22.7 21.8 %gather_fusion = bf16[2560,1024]{1,0:T(8,128)(2,1)} fusion(bf16[10240,1024]{1,0:T(8,128)(2,1)} %param.5, s32[3072]{0:T(1024)S(1)} %pad_clamp_fusion), kind=kCustom, calls=%fused_computation | custom fusion | bytes 10496000 | tf_op jit(solution)/shard_map/jit(_take)/gather | solution.py:405
  44.5 15.6 %all_gather.12 = bf16[256,1024]{1,0:T(8,128)(2,1)S(1)} all-gather(bf16[32,1024]{1,0:T(8,128)(2,1)} %unit.1), channel_id=1, replica_groups=mesh['cache'=16,'cls'=8] {'cls'}, dimensions={0}, use_global_device_ids=true | all-gather | bytes 589824 | tf_op jit(solution)/shard_map/all_gather | solution.py:407
  60.1 1.9 convolution_multiply_fusion.text_ref
  62.0 0.1 fusion.2
  62.1 0.1 pad_add_fusion.facts_ref
  62.2 0.1 compare_select_fusion.2.labels_ref
  62.3 2.6 %copy-done.2 = bf16[2560,1024]{1,0:T(8,128)(2,1)S(1)} copy-done((bf16[2560,1024]{1,0:T(8,128)(2,1)S(1)}, bf16[2560,1024]{1,0:T(8,128)(2,1)}, u32[]{:S(2)}) %copy-start.2) | copy-done | bytes 5242904
  65.0 4.2 %prepare.1 = (bf16[2560,1024]{1,0:T(8,128)(2,1)S(1)}, bf16[2560,640]{1,0:T(8,128)(2,1)S(1)}, s32[4]{0:T(128)S(1)}) custom-call(s32[4]{0:T(128)S(1)} %pad_add_fusion.facts_ref, bf16[2560,1024]{1,0:T(8,128)(2,1)S(1)} %copy-done.2, s32[10,1,256]{2,1,0:T(1,128)S(1)} %compare_select_fusion.2.labels_ref), custom_call_target="tpu_custom_call" | custom-call | flops 10485760 | bytes 15728640 | tf_op jit(solution)/shard_map/prepare/pallas_call | solution.py:42
  69.2 2.4 %copy-done.5 = bf16[2560,1024]{1,0:T(8,128)(2,1)} copy-done((bf16[2560,1024]{1,0:T(8,128)(2,1)}, bf16[2560,1024]{1,0:T(8,128)(2,1)S(1)}, u32[]{:S(2)}) %copy-start.5) | copy-done | bytes 5242904
  71.6 12.8 %all-gather.4.cloned.1.call-done = bf16[4096,1024]{1,0:T(8,128)(2,1)} async-done(((bf16[32,1024]{1,0:T(8,128)(2,1)}), bf16[4096,1024]{1,0:T(8,128)(2,1)}) %all-gather.4.cloned.1.call-update) | async-done | bytes 8388624 | tf_op jit(solution)/shard_map/all_gather | solution.py:390
  84.3 2.5 %copy-done.6 = bf16[2560,1024]{1,0:T(8,128)(2,1)S(1)} copy-done((bf16[2560,1024]{1,0:T(8,128)(2,1)S(1)}, bf16[2560,1024]{1,0:T(8,128)(2,1)}, u32[]{:S(2)}) %copy-start.6) | copy-done | bytes 5242904
  86.8 12.0 %sums.4 = (s16[528,640]{1,0:T(8,128)(2,1)S(1)}, s16[528,640]{1,0:T(8,128)(2,1)S(1)}, s16[528,640]{1,0:T(8,128)(2,1)S(1)}, s16[528,640]{1,0:T(8,128)(2,1)S(1)}, s32[4]{0:T(128)S(1)}) custom-call(s32[4]{0:T(128)S(1)} %get-tuple-element.44.facts_ref, bf16[16,256,1024]{2,1,0:T(8,128)(2,1)} %bitcast.9, bf16[2560,1024]{1,0:T(8,128)(2,1)S(1)} %copy-done.6, ...), custom_call_target="tpu_custom_call" | custom-call | flops 8724152320 | bytes 4194304 | tf_op jit(solution)/shard_map/sums/pallas_call | solution.py:238
  98.8 0.1 collective-permute-start
  98.9 2.7 %collective-permute-start.1 = (s16[528,640]{1,0:T(8,128)(2,1)S(1)}, s16[528,640]{1,0:T(8,128)(2,1)S(1)}, u32[]{:S(2)}, u32[]{:S(2)}) collective-permute-start(s16[528,640]{1,0:T(8,128)(2,1)S(1)} %get-tuple-element.51), channel_id=1, source_target_pairs={{0,96},{8,104},{16,112},{24,120},{32,0},{40,8},{48,16},{56,24},{64... | collective-permute-start | bytes 2027528 | tf_op jit(solution)/shard_map/ppermute | solution.py:380
  101.6 0.0 collective-permute-start.2
  101.6 2.7 %collective-permute-start.3 = (s16[528,640]{1,0:T(8,128)(2,1)S(1)}, s16[528,640]{1,0:T(8,128)(2,1)S(1)}, u32[]{:S(2)}, u32[]{:S(2)}) collective-permute-start(s16[528,640]{1,0:T(8,128)(2,1)S(1)} %get-tuple-element.53), channel_id=1, source_target_pairs={{0,24},{8,0},{16,8},{24,16},{32,56},{40,32},{48,40},{56,48},{64,88... | collective-permute-start | bytes 2027528 | tf_op jit(solution)/shard_map/ppermute | solution.py:380
  104.3 12.2 %sums.5 = (s16[528,640]{1,0:T(8,128)(2,1)S(1)}, s16[528,640]{1,0:T(8,128)(2,1)S(1)}, s16[528,640]{1,0:T(8,128)(2,1)S(1)}, s16[528,640]{1,0:T(8,128)(2,1)S(1)}, s32[4]{0:T(128)S(1)}) custom-call(s32[4]{0:T(128)S(1)} %get-tuple-element.48.facts_ref, bf16[16,256,1024]{2,1,0:T(8,128)(2,1)} %bitcast.10, bf16[2560,1024]{1,0:T(8,128)(2,1)S(1)} %copy-done.6, ...), custom_call_target="tpu_custom_call" | custom-call | flops 8724152320 | bytes 4194304 | tf_op jit(solution)/shard_map/sums/pallas_call | solution.py:238
  116.5 0.3 collective-permute-start.4
  116.7 0.0 collective-permute-done.rest_0_
  116.7 1.3 collective-permute-start.5
  118.0 0.0 collective-permute-done.1.rest_1_
  118.0 0.5 collective-permute-start.6
  118.5 0.2 collective-permute-done.2.rest_2_
  118.7 0.8 collective-permute-start.7
  119.5 0.6 collective-permute-done.3.rest_3_
  120.0 13.0 %sums.6 = (s16[528,640]{1,0:T(8,128)(2,1)S(1)}, s16[528,640]{1,0:T(8,128)(2,1)S(1)}, s16[528,640]{1,0:T(8,128)(2,1)S(1)}, s16[528,640]{1,0:T(8,128)(2,1)S(1)}, s32[4]{0:T(128)S(1)}) custom-call(s32[4]{0:T(128)S(1)} %get-tuple-element.49.facts_ref, bf16[16,256,1024]{2,1,0:T(8,128)(2,1)} %bitcast.11, bf16[2560,1024]{1,0:T(8,128)(2,1)S(1)} %copy-done.6, ...), custom_call_target="tpu_custom_call" | custom-call | flops 8724152320 | bytes 4194304 | tf_op jit(solution)/shard_map/sums/pallas_call | solution.py:238
  133.0 0.1 collective-permute-start.8
  133.1 0.0 collective-permute-done.4.rest_0_
  133.1 2.7 %collective-permute-start.9 = (s16[528,640]{1,0:T(8,128)(2,1)S(1)}, s16[528,640]{1,0:T(8,128)(2,1)S(1)}, u32[]{:S(2)}, u32[]{:S(2)}) collective-permute-start(s16[528,640]{1,0:T(8,128)(2,1)S(1)} %get-tuple-element.62), channel_id=1, source_target_pairs={{0,96},{8,104},{16,112},{24,120},{32,0},{40,8},{48,16},{56,24},{64... | collective-permute-start | bytes 2027528 | tf_op jit(solution)/shard_map/ppermute | solution.py:380
  135.8 0.0 collective-permute-done.5.rest_1_
  135.8 1.6 collective-permute-start.10
  137.4 0.0 collective-permute-done.6.rest_2_
  137.4 1.1 collective-permute-start.11
  138.4 0.0 collective-permute-done.7.rest_3_
  138.5 10.9 %sums.7 = (f32[512,640]{1,0:T(8,128)S(1)}, f32[512,640]{1,0:T(8,128)S(1)}, f32[512,640]{1,0:T(8,128)S(1)}, f32[512,640]{1,0:T(8,128)S(1)}, s32[4]{0:T(128)}) custom-call(s32[4]{0:T(128)S(1)} %get-tuple-element.54.facts_ref, bf16[16,256,1024]{2,1,0:T(8,128)(2,1)} %bitcast.12, bf16[2560,1024]{1,0:T(8,128)(2,1)S(1)} %copy-done.6, ...), custom_call_target="tpu_custom_call" | custom-call | flops 8724152320 | bytes 4194304 | tf_op jit(solution)/shard_map/sums/pallas_call | solution.py:238
  149.4 1.9 collective-permute-done.10.low_msg
  151.2 4.6 %collective-permute-done.11.high_msg = s16[528,640]{1,0:T(8,128)(2,1)S(1)} collective-permute-done((s16[528,640]{1,0:T(8,128)(2,1)S(1)}, s16[528,640]{1,0:T(8,128)(2,1)S(1)}, u32[]{:S(2)}, u32[]{:S(2)}) %collective-permute-start.11) | collective-permute-done | bytes 675872 | tf_op jit(solution)/shard_map/ppermute | solution.py:380
  155.9 2.6 %turn.3 = (f32[256,640]{1,0:T(8,128)S(1)}, s16[272,640]{1,0:T(8,128)(2,1)S(1)}, s16[272,640]{1,0:T(8,128)(2,1)S(1)}, s16[272,640]{1,0:T(8,128)(2,1)S(1)}) custom-call(s32[1]{0:T(128)} %bitcast.1.place_ref, f32[512,640]{1,0:T(8,128)S(1)} %get-tuple-element.64.low_hbm, f32[512,640]{1,0:T(8,128)S(1)} %get-tuple-element.65.high_hbm, ...), custom_call_target="tpu_custom_call" | custom-call | flops 6553600 | bytes 6553600 | tf_op jit(solution)/shard_map/turn/pallas_call | solution.py:307
  158.4 0.0 copy-start.3
  158.4 0.1 collective-permute-start.15
  158.5 0.1 collective-permute-start.16
  158.6 2.7 %collective-permute-start.17 = (s16[272,640]{1,0:T(8,128)(2,1)S(1)}, s16[272,640]{1,0:T(8,128)(2,1)S(1)}, u32[]{:S(2)}, u32[]{:S(2)}) collective-permute-start(s16[272,640]{1,0:T(8,128)(2,1)S(1)} %get-tuple-element.74), channel_id=1, source_target_pairs={{0,96},{8,104},{16,112},{24,120},{32,0},{40,8},{48,16},{56,24},{64... | collective-permute-start | bytes 1044488 | tf_op jit(solution)/shard_map/ppermute | solution.py:380
  161.3 0.0 collective-permute-done.8.low_msg
  161.3 0.0 collective-permute-done.9.high_msg
  161.3 2.6 %turn.2 = (f32[256,640]{1,0:T(8,128)S(1)}, s16[272,640]{1,0:T(8,128)(2,1)S(1)}, s16[272,640]{1,0:T(8,128)(2,1)S(1)}, s16[272,640]{1,0:T(8,128)(2,1)S(1)}) custom-call(s32[1]{0:T(128)} %bitcast.place_ref, f32[512,640]{1,0:T(8,128)S(1)} %get-tuple-element.59.low_hbm, f32[512,640]{1,0:T(8,128)S(1)} %get-tuple-element.60.high_hbm, ...), custom_call_target="tpu_custom_call" | custom-call | flops 6553600 | bytes 6553600 | tf_op jit(solution)/shard_map/turn/pallas_call | solution.py:307
  163.9 1.5 collective-permute-start.12
  165.4 0.0 collective-permute-start.13
  165.4 4.0 %collective-permute-done.15.rest_5_ = s16[272,640]{1,0:T(8,128)(2,1)S(1)} collective-permute-done((s16[272,640]{1,0:T(8,128)(2,1)S(1)}, s16[272,640]{1,0:T(8,128)(2,1)S(1)}, u32[]{:S(2)}, u32[]{:S(2)}) %collective-permute-start.15) | collective-permute-done | bytes 348192 | tf_op jit(solution)/shard_map/ppermute | solution.py:380
  169.4 0.0 collective-permute-start.14
  169.4 7.7 %collective-permute-done.16.rest_6_ = s16[272,640]{1,0:T(8,128)(2,1)S(1)} collective-permute-done((s16[272,640]{1,0:T(8,128)(2,1)S(1)}, s16[272,640]{1,0:T(8,128)(2,1)S(1)}, u32[]{:S(2)}, u32[]{:S(2)}) %collective-permute-start.16) | collective-permute-done | bytes 348192 | tf_op jit(solution)/shard_map/ppermute | solution.py:380
  177.1 0.0 collective-permute-done.17.rest_7_
  177.1 0.0 collective-permute-done.12.rest_2_
  177.1 5.8 %collective-permute-done.13.rest_3_ = s16[272,640]{1,0:T(8,128)(2,1)S(1)} collective-permute-done((s16[272,640]{1,0:T(8,128)(2,1)S(1)}, s16[272,640]{1,0:T(8,128)(2,1)S(1)}, u32[]{:S(2)}, u32[]{:S(2)}) %collective-permute-start.13) | collective-permute-done | bytes 348192 | tf_op jit(solution)/shard_map/ppermute | solution.py:380
  183.0 0.0 collective-permute-done.14.rest_4_
  183.0 1.0 close.1
  184.0 13.6 %all-gather.1.stats_ref = f32[8,2,256]{2,1,0:T(2,128)S(1)} all-gather(f32[1,2,256]{2,1,0:T(2,128)S(1)} %bitcast.8), channel_id=2, replica_groups=mesh['cache'=16,'cls'=8] {'cls'}, dimensions={0}, use_global_device_ids=true | all-gather | bytes 18432 | tf_op jit(solution)/shard_map/all_gather | solution.py:443
  197.6 1.3 finish.1
  (17 shorter events, 0.1 us)
Async XLA Ops:
  6.5 53.6 %copy-start = (bf16[1280,1024]{1,0:T(8,128)(2,1)S(1)}, bf16[1280,1024]{1,0:T(8,128)(2,1)}, u32[]{:S(2)}) copy-start(bf16[1280,1024]{1,0:T(8,128)(2,1)} %param.7) | copy-start | bytes 7864324
  6.5 77.8 %all-gather.4.cloned.1.call-start = ((), (), s32[]{:S(2)}) async-start(), calls=%async_computation | async-start | bytes 8454144 | tf_op jit(solution)/shard_map/all_gather | solution.py:390
  6.5 1.0 copy-start.4
  62.3 2.6 %copy-start.2 = (bf16[2560,1024]{1,0:T(8,128)(2,1)S(1)}, bf16[2560,1024]{1,0:T(8,128)(2,1)}, u32[]{:S(2)}) copy-start(bf16[2560,1024]{1,0:T(8,128)(2,1)} %gather_fusion) | copy-start | bytes 15728644
  69.2 2.4 %copy-start.5 = (bf16[2560,1024]{1,0:T(8,128)(2,1)}, bf16[2560,1024]{1,0:T(8,128)(2,1)S(1)}, u32[]{:S(2)}) copy-start(bf16[2560,1024]{1,0:T(8,128)(2,1)S(1)} %get-tuple-element.46.keys_ref) | copy-start | bytes 15728644
  84.3 2.5 %copy-start.6 = (bf16[2560,1024]{1,0:T(8,128)(2,1)S(1)}, bf16[2560,1024]{1,0:T(8,128)(2,1)}, u32[]{:S(2)}) copy-start(bf16[2560,1024]{1,0:T(8,128)(2,1)} %copy-done.5) | copy-start | bytes 15728644
  98.8 17.9 %collective-permute-start = (s16[528,640]{1,0:T(8,128)(2,1)S(1)}, s16[528,640]{1,0:T(8,128)(2,1)S(1)}, u32[]{:S(2)}, u32[]{:S(2)}) collective-permute-start(s16[528,640]{1,0:T(8,128)(2,1)S(1)} %get-tuple-element.50), channel_id=1, source_target_pairs={{0,32},{8,40},{16,48},{24,56},{32,64},{40,72},{48,80},{56,88},{64,... | collective-permute-start | bytes 2027528 | tf_op jit(solution)/shard_map/ppermute | solution.py:380
  98.9 19.1 %collective-permute-start.1 = (s16[528,640]{1,0:T(8,128)(2,1)S(1)}, s16[528,640]{1,0:T(8,128)(2,1)S(1)}, u32[]{:S(2)}, u32[]{:S(2)}) collective-permute-start(s16[528,640]{1,0:T(8,128)(2,1)S(1)} %get-tuple-element.51), channel_id=1, source_target_pairs={{0,96},{8,104},{16,112},{24,120},{32,0},{40,8},{48,16},{56,24},{64... | collective-permute-start | bytes 2027528 | tf_op jit(solution)/shard_map/ppermute | solution.py:380
  101.6 17.1 %collective-permute-start.2 = (s16[528,640]{1,0:T(8,128)(2,1)S(1)}, s16[528,640]{1,0:T(8,128)(2,1)S(1)}, u32[]{:S(2)}, u32[]{:S(2)}) collective-permute-start(s16[528,640]{1,0:T(8,128)(2,1)S(1)} %get-tuple-element.52), channel_id=1, source_target_pairs={{0,8},{8,16},{16,24},{24,0},{32,40},{40,48},{48,56},{56,32},{64,72... | collective-permute-start | bytes 2027528 | tf_op jit(solution)/shard_map/ppermute | solution.py:380
  101.6 18.4 %collective-permute-start.3 = (s16[528,640]{1,0:T(8,128)(2,1)S(1)}, s16[528,640]{1,0:T(8,128)(2,1)S(1)}, u32[]{:S(2)}, u32[]{:S(2)}) collective-permute-start(s16[528,640]{1,0:T(8,128)(2,1)S(1)} %get-tuple-element.53), channel_id=1, source_target_pairs={{0,24},{8,0},{16,8},{24,16},{32,56},{40,32},{48,40},{56,48},{64,88... | collective-permute-start | bytes 2027528 | tf_op jit(solution)/shard_map/ppermute | solution.py:380
  116.5 16.6 %collective-permute-start.4 = (s16[528,640]{1,0:T(8,128)(2,1)S(1)}, s16[528,640]{1,0:T(8,128)(2,1)S(1)}, u32[]{:S(2)}, u32[]{:S(2)}) collective-permute-start(s16[528,640]{1,0:T(8,128)(2,1)S(1)} %get-tuple-element.55), channel_id=1, source_target_pairs={{0,96},{8,104},{16,112},{24,120},{32,0},{40,8},{48,16},{56,24},{64... | collective-permute-start | bytes 2027528 | tf_op jit(solution)/shard_map/ppermute | solution.py:380
  116.7 19.1 %collective-permute-start.5 = (s16[528,640]{1,0:T(8,128)(2,1)S(1)}, s16[528,640]{1,0:T(8,128)(2,1)S(1)}, u32[]{:S(2)}, u32[]{:S(2)}) collective-permute-start(s16[528,640]{1,0:T(8,128)(2,1)S(1)} %get-tuple-element.56), channel_id=1, source_target_pairs={{0,32},{8,40},{16,48},{24,56},{32,64},{40,72},{48,80},{56,88},{64,... | collective-permute-start | bytes 2027528 | tf_op jit(solution)/shard_map/ppermute | solution.py:380
  118.0 19.4 %collective-permute-start.6 = (s16[528,640]{1,0:T(8,128)(2,1)S(1)}, s16[528,640]{1,0:T(8,128)(2,1)S(1)}, u32[]{:S(2)}, u32[]{:S(2)}) collective-permute-start(s16[528,640]{1,0:T(8,128)(2,1)S(1)} %get-tuple-element.57), channel_id=1, source_target_pairs={{0,24},{8,0},{16,8},{24,16},{32,56},{40,32},{48,40},{56,48},{64,88... | collective-permute-start | bytes 2027528 | tf_op jit(solution)/shard_map/ppermute | solution.py:380
  118.7 19.8 %collective-permute-start.7 = (s16[528,640]{1,0:T(8,128)(2,1)S(1)}, s16[528,640]{1,0:T(8,128)(2,1)S(1)}, u32[]{:S(2)}, u32[]{:S(2)}) collective-permute-start(s16[528,640]{1,0:T(8,128)(2,1)S(1)} %get-tuple-element.58), channel_id=1, source_target_pairs={{0,8},{8,16},{16,24},{24,0},{32,40},{40,48},{48,56},{56,32},{64,72... | collective-permute-start | bytes 2027528 | tf_op jit(solution)/shard_map/ppermute | solution.py:380
  133.0 28.3 %collective-permute-start.8 = (s16[528,640]{1,0:T(8,128)(2,1)S(1)}, s16[528,640]{1,0:T(8,128)(2,1)S(1)}, u32[]{:S(2)}, u32[]{:S(2)}) collective-permute-start(s16[528,640]{1,0:T(8,128)(2,1)S(1)} %get-tuple-element.61), channel_id=1, source_target_pairs={{0,32},{8,40},{16,48},{24,56},{32,64},{40,72},{48,80},{56,88},{64,... | collective-permute-start | bytes 2027528 | tf_op jit(solution)/shard_map/ppermute | solution.py:380
  133.1 28.2 %collective-permute-start.9 = (s16[528,640]{1,0:T(8,128)(2,1)S(1)}, s16[528,640]{1,0:T(8,128)(2,1)S(1)}, u32[]{:S(2)}, u32[]{:S(2)}) collective-permute-start(s16[528,640]{1,0:T(8,128)(2,1)S(1)} %get-tuple-element.62), channel_id=1, source_target_pairs={{0,96},{8,104},{16,112},{24,120},{32,0},{40,8},{48,16},{56,24},{64... | collective-permute-start | bytes 2027528 | tf_op jit(solution)/shard_map/ppermute | solution.py:380
  135.8 15.5 %collective-permute-start.10 = (s16[528,640]{1,0:T(8,128)(2,1)S(1)}, s16[528,640]{1,0:T(8,128)(2,1)S(1)}, u32[]{:S(2)}, u32[]{:S(2)}) collective-permute-start(s16[528,640]{1,0:T(8,128)(2,1)S(1)} %get-tuple-element.66), channel_id=1, source_target_pairs={{0,8},{8,16},{16,24},{24,0},{32,40},{40,48},{48,56},{56,32},{64,72... | collective-permute-start | bytes 2027528 | tf_op jit(solution)/shard_map/ppermute | solution.py:380
  137.4 18.5 %collective-permute-start.11 = (s16[528,640]{1,0:T(8,128)(2,1)S(1)}, s16[528,640]{1,0:T(8,128)(2,1)S(1)}, u32[]{:S(2)}, u32[]{:S(2)}) collective-permute-start(s16[528,640]{1,0:T(8,128)(2,1)S(1)} %get-tuple-element.67), channel_id=1, source_target_pairs={{0,24},{8,0},{16,8},{24,16},{32,56},{40,32},{48,40},{56,48},{64,88... | collective-permute-start | bytes 2027528 | tf_op jit(solution)/shard_map/ppermute | solution.py:380
  158.4 24.5 %copy-start.3 = (f32[256,1280]{1,0:T(8,128)S(1)}, f32[256,1280]{1,0:T(8,128)}, u32[]{:S(2)}) copy-start(f32[256,1280]{1,0:T(8,128)} %convolution_multiply_fusion.text_ref) | copy-start | bytes 3932164
  158.4 11.0 %collective-permute-start.15 = (s16[272,640]{1,0:T(8,128)(2,1)S(1)}, s16[272,640]{1,0:T(8,128)(2,1)S(1)}, u32[]{:S(2)}, u32[]{:S(2)}) collective-permute-start(s16[272,640]{1,0:T(8,128)(2,1)S(1)} %get-tuple-element.72), channel_id=1, source_target_pairs={{0,64},{8,72},{16,80},{24,88},{32,96},{40,104},{48,112},{56,120},{... | collective-permute-start | bytes 1044488 | tf_op jit(solution)/shard_map/ppermute | solution.py:380
  158.5 18.6 %collective-permute-start.16 = (s16[272,640]{1,0:T(8,128)(2,1)S(1)}, s16[272,640]{1,0:T(8,128)(2,1)S(1)}, u32[]{:S(2)}, u32[]{:S(2)}) collective-permute-start(s16[272,640]{1,0:T(8,128)(2,1)S(1)} %get-tuple-element.73), channel_id=1, source_target_pairs={{0,32},{8,40},{16,48},{24,56},{32,64},{40,72},{48,80},{56,88},{64,... | collective-permute-start | bytes 1044488 | tf_op jit(solution)/shard_map/ppermute | solution.py:380
  158.6 18.5 %collective-permute-start.17 = (s16[272,640]{1,0:T(8,128)(2,1)S(1)}, s16[272,640]{1,0:T(8,128)(2,1)S(1)}, u32[]{:S(2)}, u32[]{:S(2)}) collective-permute-start(s16[272,640]{1,0:T(8,128)(2,1)S(1)} %get-tuple-element.74), channel_id=1, source_target_pairs={{0,96},{8,104},{16,112},{24,120},{32,0},{40,8},{48,16},{56,24},{64... | collective-permute-start | bytes 1044488 | tf_op jit(solution)/shard_map/ppermute | solution.py:380
  163.9 13.3 %collective-permute-start.12 = (s16[272,640]{1,0:T(8,128)(2,1)S(1)}, s16[272,640]{1,0:T(8,128)(2,1)S(1)}, u32[]{:S(2)}, u32[]{:S(2)}) collective-permute-start(s16[272,640]{1,0:T(8,128)(2,1)S(1)} %get-tuple-element.69), channel_id=1, source_target_pairs={{0,16},{8,24},{16,0},{24,8},{32,48},{40,56},{48,32},{56,40},{64,80... | collective-permute-start | bytes 1044488 | tf_op jit(solution)/shard_map/ppermute | solution.py:380
  165.4 17.6 %collective-permute-start.13 = (s16[272,640]{1,0:T(8,128)(2,1)S(1)}, s16[272,640]{1,0:T(8,128)(2,1)S(1)}, u32[]{:S(2)}, u32[]{:S(2)}) collective-permute-start(s16[272,640]{1,0:T(8,128)(2,1)S(1)} %get-tuple-element.70), channel_id=1, source_target_pairs={{0,8},{8,16},{16,24},{24,0},{32,40},{40,48},{48,56},{56,32},{64,72... | collective-permute-start | bytes 1044488 | tf_op jit(solution)/shard_map/ppermute | solution.py:380
  169.4 13.6 %collective-permute-start.14 = (s16[272,640]{1,0:T(8,128)(2,1)S(1)}, s16[272,640]{1,0:T(8,128)(2,1)S(1)}, u32[]{:S(2)}, u32[]{:S(2)}) collective-permute-start(s16[272,640]{1,0:T(8,128)(2,1)S(1)} %get-tuple-element.71), channel_id=1, source_target_pairs={{0,24},{8,0},{16,8},{24,16},{32,56},{40,32},{48,40},{56,48},{64,88... | collective-permute-start | bytes 1044488 | tf_op jit(solution)/shard_map/ppermute | solution.py:380
  183.0 15.9 %copy-start.1 = (bf16[1280,1024]{1,0:T(8,128)(2,1)S(1)}, bf16[1280,1024]{1,0:T(8,128)(2,1)}, u32[]{:S(2)}) copy-start(bf16[1280,1024]{1,0:T(8,128)(2,1)} %param.7) | copy-start | bytes 7864324
Sparse Core Ops, SparseCore 0:
  10.3 73.9 all-gather.3

commit v6 on v3

--- a/solution.py
+++ b/solution.py
@@ -173,11 +173,8 @@
             source = msg_ref.at[at] if coded else total_ref.at[at // 2, pl.ds(at % 2 * HALF, HALF), :]
             return pltpu.make_async_copy(source, outs[at], out_sems.at[at])
 
-        for block in range(2):
-            for part in range(SIDE):
-                copy_queries(block, part).start()
-        for at in range(joined):
-            copy_came(at).start()
+        for part in range(SIDE):
+            copy_queries(0, part).start()
         scores_ref[:, COMMON * KT :] = jnp.zeros((SUPER, CAP - COMMON * KT), jnp.bfloat16)
         if coded:
             for at in range(4):
@@ -186,6 +183,14 @@
         def run(block, carry):
             for part in range(SIDE):
                 copy_queries(block, part).wait()
+
+            @pl.when(block == 0)
+            def _():
+                for part in range(SIDE):
+                    copy_queries(1, part).start()
+                for at in range(joined):
+                    copy_came(at).start()
+
             super_sums(
                 facts_ref[2 + block],
                 q_ref.at[block],

time: 206 us -> 212 us (1.029); the launches traced: 206 us -> 209 us
  Pallas kernels: 64.1 us -> 72.6 us
  waiting for transfers between devices: 28.5 us -> 25.7 us
    pallas_call x4, Pallas kernels: 51.7 us -> 60.3 us  [sums(): pl.pallas_call(kernel, in_specs=[smem, anywhere, vmem, vmem] + [anywhere]...]
    ppermute x18, waiting for transfers between devices: 15.7 us -> 13 us  [send(): return lax.ppermute(message, 'cache', shifted(dx, dz))]
  transfers between devices with their start and end apart: 19 -> 19, of which waited for: 6 -> 4; matrix products, arithmetic and copies ran while one was open for 16% -> 15% of each run, Pallas kernels for 23% -> 26%
where the time goes in v6:
time: 212 us; the launch traced here: 209 us
  Pallas kernels  72.6 us (34%)
  local copies, waits for them, and re-layouts  30.5 us (14%)
  blocking collectives  27.2 us (13%)
  waiting for transfers between devices  25.7 us (12%)
  starting transfers between devices  22.8 us (11%)
  between operations  20 us (9%)
  other arithmetic  8.11 us (4%)
    pallas_call x4, Pallas kernels, sums(): pl.pallas_call(kernel, in_specs=[smem, anywhere, vmem, vmem] + [anywhere]...  60.3 us
    ppermute x18, starting transfers between devices, send(): return lax.ppermute(message, 'cache', shifted(dx, dz))  22.8 us
    gather x1, local copies, waits for them, and re-layouts, per_device(): rows = jnp.take(cache_keys, picked % 16384, axis=0, mode='clip')  21.8 us
    all_gather x1, blocking collectives, per_device(): lax.all_gather(unit_queries, 'cls', axis=0, tiled=True)  15.6 us
    ppermute x18, waiting for transfers between devices, send(): return lax.ppermute(message, 'cache', shifted(dx, dz))  13 us
    all_gather x1, waiting for transfers between devices, per_device(): lax.all_gather(unit_queries, ('cache', 'cls'), axis=0, tiled=True)  12.8 us
    all_gather x1, blocking collectives, per_device(): return finish(logits, lax.all_gather(stats, 'cls'))  11.5 us
    unnamed x16, local copies, waits for them, and re-layouts  8.54 us
  transfers between devices with their start and end apart: 19, of which 4 were waited for; matrix products, arithmetic and copies ran while one was open for 15% of the time, Pallas kernels for 26%

profile of v6, /device:TPU:1, one launch (start us, length us, event | category | flops | bytes accessed | tf_op | source)
XLA Modules:
  0.0 208.8 jit_solution(8861653695727485801)
XLA Ops:
  6.5 1.0 copy-done.4
  7.5 0.7 unit.1
  8.2 0.0 all-gather.4.cloned.1.call-update
  8.3 1.5 convert_reduce_fusion
  14.9 6.3 %sort.7 = s32[10240]{0:T(1024)S(1)} sort(s32[10240]{0:T(1024)S(1)} %get-tuple-element.82), dimensions={0}, to_apply=%region_0.1 | sort | flops 143360 | bytes 81920 | tf_op jit(solution)/shard_map/sort | solution.py:388
  22.4 0.1 pad_dynamic-slice_fusion
  22.6 0.1 fusion
  22.7 21.8 %gather_fusion = bf16[2560,1024]{1,0:T(8,128)(2,1)} fusion(bf16[10240,1024]{1,0:T(8,128)(2,1)} %param.5, s32[3072]{0:T(1024)S(1)} %pad_clamp_fusion), kind=kCustom, calls=%fused_computation | custom fusion | bytes 10496000 | tf_op jit(solution)/shard_map/jit(_take)/gather | solution.py:401
  44.5 15.6 %all_gather.12 = bf16[256,1024]{1,0:T(8,128)(2,1)S(1)} all-gather(bf16[32,1024]{1,0:T(8,128)(2,1)} %unit.1), channel_id=1, replica_groups=mesh['cache'=16,'cls'=8] {'cls'}, dimensions={0}, use_global_device_ids=true | all-gather | bytes 589824 | tf_op jit(solution)/shard_map/all_gather | solution.py:403
  60.1 1.9 convolution_multiply_fusion.text_ref
  62.0 0.1 fusion.2
  62.1 0.1 pad_add_fusion.facts_ref
  62.2 0.1 compare_select_fusion.2.labels_ref
  62.3 2.6 %copy-done.2 = bf16[2560,1024]{1,0:T(8,128)(2,1)S(1)} copy-done((bf16[2560,1024]{1,0:T(8,128)(2,1)S(1)}, bf16[2560,1024]{1,0:T(8,128)(2,1)}, u32[]{:S(2)}) %copy-start.2) | copy-done | bytes 5242904
  65.0 4.2 %prepare.1 = (bf16[2560,1024]{1,0:T(8,128)(2,1)S(1)}, bf16[2560,640]{1,0:T(8,128)(2,1)S(1)}, s32[4]{0:T(128)S(1)}) custom-call(s32[4]{0:T(128)S(1)} %pad_add_fusion.facts_ref, bf16[2560,1024]{1,0:T(8,128)(2,1)S(1)} %copy-done.2, s32[10,1,256]{2,1,0:T(1,128)S(1)} %compare_select_fusion.2.labels_ref), custom_call_target="tpu_custom_call" | custom-call | flops 10485760 | bytes 15728640 | tf_op jit(solution)/shard_map/prepare/pallas_call | solution.py:42
  69.2 2.4 %copy-done.5 = bf16[2560,1024]{1,0:T(8,128)(2,1)} copy-done((bf16[2560,1024]{1,0:T(8,128)(2,1)}, bf16[2560,1024]{1,0:T(8,128)(2,1)S(1)}, u32[]{:S(2)}) %copy-start.5) | copy-done | bytes 5242904
  71.6 12.8 %all-gather.4.cloned.1.call-done = bf16[4096,1024]{1,0:T(8,128)(2,1)} async-done(((bf16[32,1024]{1,0:T(8,128)(2,1)}), bf16[4096,1024]{1,0:T(8,128)(2,1)}) %all-gather.4.cloned.1.call-update) | async-done | bytes 8388624 | tf_op jit(solution)/shard_map/all_gather | solution.py:386
  84.3 2.5 %copy-done.6 = bf16[2560,1024]{1,0:T(8,128)(2,1)S(1)} copy-done((bf16[2560,1024]{1,0:T(8,128)(2,1)S(1)}, bf16[2560,1024]{1,0:T(8,128)(2,1)}, u32[]{:S(2)}) %copy-start.6) | copy-done | bytes 5242904
  86.8 14.6 %sums.4 = (s16[528,640]{1,0:T(8,128)(2,1)S(1)}, s16[528,640]{1,0:T(8,128)(2,1)S(1)}, s16[528,640]{1,0:T(8,128)(2,1)S(1)}, s16[528,640]{1,0:T(8,128)(2,1)S(1)}, s32[4]{0:T(128)S(1)}) custom-call(s32[4]{0:T(128)S(1)} %get-tuple-element.44.facts_ref, bf16[16,256,1024]{2,1,0:T(8,128)(2,1)} %bitcast.9, bf16[2560,1024]{1,0:T(8,128)(2,1)S(1)} %copy-done.6, ...), custom_call_target="tpu_custom_call" | custom-call | flops 8724152320 | bytes 4194304 | tf_op jit(solution)/shard_map/sums/pallas_call | solution.py:234
  101.5 0.1 collective-permute-start
  101.6 2.7 %collective-permute-start.1 = (s16[528,640]{1,0:T(8,128)(2,1)S(1)}, s16[528,640]{1,0:T(8,128)(2,1)S(1)}, u32[]{:S(2)}, u32[]{:S(2)}) collective-permute-start(s16[528,640]{1,0:T(8,128)(2,1)S(1)} %get-tuple-element.51), channel_id=1, source_target_pairs={{0,96},{8,104},{16,112},{24,120},{32,0},{40,8},{48,16},{56,24},{64... | collective-permute-start | bytes 2027528 | tf_op jit(solution)/shard_map/ppermute | solution.py:376
  104.2 0.0 collective-permute-start.2
  104.2 2.7 %collective-permute-start.3 = (s16[528,640]{1,0:T(8,128)(2,1)S(1)}, s16[528,640]{1,0:T(8,128)(2,1)S(1)}, u32[]{:S(2)}, u32[]{:S(2)}) collective-permute-start(s16[528,640]{1,0:T(8,128)(2,1)S(1)} %get-tuple-element.53), channel_id=1, source_target_pairs={{0,24},{8,0},{16,8},{24,16},{32,56},{40,32},{48,40},{56,48},{64,88... | collective-permute-start | bytes 2027528 | tf_op jit(solution)/shard_map/ppermute | solution.py:376
  106.9 14.6 %sums.5 = (s16[528,640]{1,0:T(8,128)(2,1)S(1)}, s16[528,640]{1,0:T(8,128)(2,1)S(1)}, s16[528,640]{1,0:T(8,128)(2,1)S(1)}, s16[528,640]{1,0:T(8,128)(2,1)S(1)}, s32[4]{0:T(128)S(1)}) custom-call(s32[4]{0:T(128)S(1)} %get-tuple-element.48.facts_ref, bf16[16,256,1024]{2,1,0:T(8,128)(2,1)} %bitcast.10, bf16[2560,1024]{1,0:T(8,128)(2,1)S(1)} %copy-done.6, ...), custom_call_target="tpu_custom_call" | custom-call | flops 8724152320 | bytes 4194304 | tf_op jit(solution)/shard_map/sums/pallas_call | solution.py:234
  121.5 0.1 collective-permute-start.4
  121.6 0.0 collective-permute-done.rest_0_
  121.6 1.4 collective-permute-start.5
  123.1 0.0 collective-permute-done.1.rest_1_
  123.1 0.0 collective-permute-start.6
  123.1 0.0 collective-permute-done.2.rest_2_
  123.1 1.5 collective-permute-start.7
  124.6 0.0 collective-permute-done.3.rest_3_
  124.6 16.6 %sums.6 = (s16[528,640]{1,0:T(8,128)(2,1)S(1)}, s16[528,640]{1,0:T(8,128)(2,1)S(1)}, s16[528,640]{1,0:T(8,128)(2,1)S(1)}, s16[528,640]{1,0:T(8,128)(2,1)S(1)}, s32[4]{0:T(128)S(1)}) custom-call(s32[4]{0:T(128)S(1)} %get-tuple-element.49.facts_ref, bf16[16,256,1024]{2,1,0:T(8,128)(2,1)} %bitcast.11, bf16[2560,1024]{1,0:T(8,128)(2,1)S(1)} %copy-done.6, ...), custom_call_target="tpu_custom_call" | custom-call | flops 8724152320 | bytes 4194304 | tf_op jit(solution)/shard_map/sums/pallas_call | solution.py:234
  141.1 0.1 collective-permute-start.8
  141.2 0.0 collective-permute-done.4.rest_0_
  141.2 2.7 %collective-permute-start.9 = (s16[528,640]{1,0:T(8,128)(2,1)S(1)}, s16[528,640]{1,0:T(8,128)(2,1)S(1)}, u32[]{:S(2)}, u32[]{:S(2)}) collective-permute-start(s16[528,640]{1,0:T(8,128)(2,1)S(1)} %get-tuple-element.62), channel_id=1, source_target_pairs={{0,96},{8,104},{16,112},{24,120},{32,0},{40,8},{48,16},{56,24},{64... | collective-permute-start | bytes 2027528 | tf_op jit(solution)/shard_map/ppermute | solution.py:376
  143.9 0.0 collective-permute-done.5.rest_1_
  143.9 0.0 collective-permute-start.10
  143.9 0.0 collective-permute-done.6.rest_2_
  143.9 2.7 %collective-permute-start.11 = (s16[528,640]{1,0:T(8,128)(2,1)S(1)}, s16[528,640]{1,0:T(8,128)(2,1)S(1)}, u32[]{:S(2)}, u32[]{:S(2)}) collective-permute-start(s16[528,640]{1,0:T(8,128)(2,1)S(1)} %get-tuple-element.67), channel_id=1, source_target_pairs={{0,24},{8,0},{16,8},{24,16},{32,56},{40,32},{48,40},{56,48},{64,88... | collective-permute-start | bytes 2027528 | tf_op jit(solution)/shard_map/ppermute | solution.py:376
  146.6 0.0 collective-permute-done.7.rest_3_
  146.6 14.4 %sums.7 = (f32[512,640]{1,0:T(8,128)S(1)}, f32[512,640]{1,0:T(8,128)S(1)}, f32[512,640]{1,0:T(8,128)S(1)}, f32[512,640]{1,0:T(8,128)S(1)}, s32[4]{0:T(128)}) custom-call(s32[4]{0:T(128)S(1)} %get-tuple-element.54.facts_ref, bf16[16,256,1024]{2,1,0:T(8,128)(2,1)} %bitcast.12, bf16[2560,1024]{1,0:T(8,128)(2,1)S(1)} %copy-done.6, ...), custom_call_target="tpu_custom_call" | custom-call | flops 8724152320 | bytes 4194304 | tf_op jit(solution)/shard_map/sums/pallas_call | solution.py:234
  161.0 0.0 collective-permute-done.10.low_msg
  161.0 0.0 collective-permute-done.11.high_msg
  161.0 2.6 %turn.3 = (f32[256,640]{1,0:T(8,128)S(1)}, s16[272,640]{1,0:T(8,128)(2,1)S(1)}, s16[272,640]{1,0:T(8,128)(2,1)S(1)}, s16[272,640]{1,0:T(8,128)(2,1)S(1)}) custom-call(s32[1]{0:T(128)} %bitcast.1.place_ref, f32[512,640]{1,0:T(8,128)S(1)} %get-tuple-element.64.low_hbm, f32[512,640]{1,0:T(8,128)S(1)} %get-tuple-element.65.high_hbm, ...), custom_call_target="tpu_custom_call" | custom-call | flops 6553600 | bytes 6553600 | tf_op jit(solution)/shard_map/turn/pallas_call | solution.py:303
  163.6 0.0 copy-start.3
  163.6 0.1 collective-permute-start.15
  163.7 0.1 collective-permute-start.16
  163.8 2.7 %collective-permute-start.17 = (s16[272,640]{1,0:T(8,128)(2,1)S(1)}, s16[272,640]{1,0:T(8,128)(2,1)S(1)}, u32[]{:S(2)}, u32[]{:S(2)}) collective-permute-start(s16[272,640]{1,0:T(8,128)(2,1)S(1)} %get-tuple-element.74), channel_id=1, source_target_pairs={{0,96},{8,104},{16,112},{24,120},{32,0},{40,8},{48,16},{56,24},{64... | collective-permute-start | bytes 1044488 | tf_op jit(solution)/shard_map/ppermute | solution.py:376
  166.5 0.0 collective-permute-done.8.low_msg
  166.5 0.0 collective-permute-done.9.high_msg
  166.5 2.6 %turn.2 = (f32[256,640]{1,0:T(8,128)S(1)}, s16[272,640]{1,0:T(8,128)(2,1)S(1)}, s16[272,640]{1,0:T(8,128)(2,1)S(1)}, s16[272,640]{1,0:T(8,128)(2,1)S(1)}) custom-call(s32[1]{0:T(128)} %bitcast.place_ref, f32[512,640]{1,0:T(8,128)S(1)} %get-tuple-element.59.low_hbm, f32[512,640]{1,0:T(8,128)S(1)} %get-tuple-element.60.high_hbm, ...), custom_call_target="tpu_custom_call" | custom-call | flops 6553600 | bytes 6553600 | tf_op jit(solution)/shard_map/turn/pallas_call | solution.py:303
  169.0 1.3 collective-permute-start.12
  170.3 1.6 collective-permute-start.13
  172.0 2.5 %collective-permute-done.15.rest_5_ = s16[272,640]{1,0:T(8,128)(2,1)S(1)} collective-permute-done((s16[272,640]{1,0:T(8,128)(2,1)S(1)}, s16[272,640]{1,0:T(8,128)(2,1)S(1)}, u32[]{:S(2)}, u32[]{:S(2)}) %collective-permute-start.15) | collective-permute-done | bytes 348192 | tf_op jit(solution)/shard_map/ppermute | solution.py:376
  174.5 3.2 %collective-permute-start.14 = (s16[272,640]{1,0:T(8,128)(2,1)S(1)}, s16[272,640]{1,0:T(8,128)(2,1)S(1)}, u32[]{:S(2)}, u32[]{:S(2)}) collective-permute-start(s16[272,640]{1,0:T(8,128)(2,1)S(1)} %get-tuple-element.71), channel_id=1, source_target_pairs={{0,24},{8,0},{16,8},{24,16},{32,56},{40,32},{48,40},{56,48},{64,88... | collective-permute-start | bytes 1044488 | tf_op jit(solution)/shard_map/ppermute | solution.py:376
  177.7 4.6 %collective-permute-done.16.rest_6_ = s16[272,640]{1,0:T(8,128)(2,1)S(1)} collective-permute-done((s16[272,640]{1,0:T(8,128)(2,1)S(1)}, s16[272,640]{1,0:T(8,128)(2,1)S(1)}, u32[]{:S(2)}, u32[]{:S(2)}) %collective-permute-start.16) | collective-permute-done | bytes 348192 | tf_op jit(solution)/shard_map/ppermute | solution.py:376
  182.3 0.0 collective-permute-done.17.rest_7_
  182.3 0.0 collective-permute-done.12.rest_2_
  182.3 5.8 %collective-permute-done.13.rest_3_ = s16[272,640]{1,0:T(8,128)(2,1)S(1)} collective-permute-done((s16[272,640]{1,0:T(8,128)(2,1)S(1)}, s16[272,640]{1,0:T(8,128)(2,1)S(1)}, u32[]{:S(2)}, u32[]{:S(2)}) %collective-permute-start.13) | collective-permute-done | bytes 348192 | tf_op jit(solution)/shard_map/ppermute | solution.py:376
  188.2 0.0 collective-permute-done.14.rest_4_
  188.2 1.0 close.1
  189.2 11.5 %all-gather.1.stats_ref = f32[8,2,256]{2,1,0:T(2,128)S(1)} all-gather(f32[1,2,256]{2,1,0:T(2,128)S(1)} %bitcast.8), channel_id=2, replica_groups=mesh['cache'=16,'cls'=8] {'cls'}, dimensions={0}, use_global_device_ids=true | all-gather | bytes 18432 | tf_op jit(solution)/shard_map/all_gather | solution.py:439
  200.7 1.3 finish.1
  (17 shorter events, 0.1 us)
Async XLA Ops:
  6.5 53.6 %copy-start = (bf16[1280,1024]{1,0:T(8,128)(2,1)S(1)}, bf16[1280,1024]{1,0:T(8,128)(2,1)}, u32[]{:S(2)}) copy-start(bf16[1280,1024]{1,0:T(8,128)(2,1)} %param.7) | copy-start | bytes 7864324
  6.5 77.8 %all-gather.4.cloned.1.call-start = ((), (), s32[]{:S(2)}) async-start(), calls=%async_computation | async-start | bytes 8454144 | tf_op jit(solution)/shard_map/all_gather | solution.py:386
  6.5 1.0 copy-start.4
  62.3 2.6 %copy-start.2 = (bf16[2560,1024]{1,0:T(8,128)(2,1)S(1)}, bf16[2560,1024]{1,0:T(8,128)(2,1)}, u32[]{:S(2)}) copy-start(bf16[2560,1024]{1,0:T(8,128)(2,1)} %gather_fusion) | copy-start | bytes 15728644
  69.2 2.4 %copy-start.5 = (bf16[2560,1024]{1,0:T(8,128)(2,1)}, bf16[2560,1024]{1,0:T(8,128)(2,1)S(1)}, u32[]{:S(2)}) copy-start(bf16[2560,1024]{1,0:T(8,128)(2,1)S(1)} %get-tuple-element.46.keys_ref) | copy-start | bytes 15728644
  84.3 2.5 %copy-start.6 = (bf16[2560,1024]{1,0:T(8,128)(2,1)S(1)}, bf16[2560,1024]{1,0:T(8,128)(2,1)}, u32[]{:S(2)}) copy-start(bf16[2560,1024]{1,0:T(8,128)(2,1)} %copy-done.5) | copy-start | bytes 15728644
  101.5 20.2 %collective-permute-start = (s16[528,640]{1,0:T(8,128)(2,1)S(1)}, s16[528,640]{1,0:T(8,128)(2,1)S(1)}, u32[]{:S(2)}, u32[]{:S(2)}) collective-permute-start(s16[528,640]{1,0:T(8,128)(2,1)S(1)} %get-tuple-element.50), channel_id=1, source_target_pairs={{0,32},{8,40},{16,48},{24,56},{32,64},{40,72},{48,80},{56,88},{64,... | collective-permute-start | bytes 2027528 | tf_op jit(solution)/shard_map/ppermute | solution.py:376
  101.6 21.5 %collective-permute-start.1 = (s16[528,640]{1,0:T(8,128)(2,1)S(1)}, s16[528,640]{1,0:T(8,128)(2,1)S(1)}, u32[]{:S(2)}, u32[]{:S(2)}) collective-permute-start(s16[528,640]{1,0:T(8,128)(2,1)S(1)} %get-tuple-element.51), channel_id=1, source_target_pairs={{0,96},{8,104},{16,112},{24,120},{32,0},{40,8},{48,16},{56,24},{64... | collective-permute-start | bytes 2027528 | tf_op jit(solution)/shard_map/ppermute | solution.py:376
  104.2 18.9 %collective-permute-start.2 = (s16[528,640]{1,0:T(8,128)(2,1)S(1)}, s16[528,640]{1,0:T(8,128)(2,1)S(1)}, u32[]{:S(2)}, u32[]{:S(2)}) collective-permute-start(s16[528,640]{1,0:T(8,128)(2,1)S(1)} %get-tuple-element.52), channel_id=1, source_target_pairs={{0,8},{8,16},{16,24},{24,0},{32,40},{40,48},{48,56},{56,32},{64,72... | collective-permute-start | bytes 2027528 | tf_op jit(solution)/shard_map/ppermute | solution.py:376
  104.2 20.3 %collective-permute-start.3 = (s16[528,640]{1,0:T(8,128)(2,1)S(1)}, s16[528,640]{1,0:T(8,128)(2,1)S(1)}, u32[]{:S(2)}, u32[]{:S(2)}) collective-permute-start(s16[528,640]{1,0:T(8,128)(2,1)S(1)} %get-tuple-element.53), channel_id=1, source_target_pairs={{0,24},{8,0},{16,8},{24,16},{32,56},{40,32},{48,40},{56,48},{64,88... | collective-permute-start | bytes 2027528 | tf_op jit(solution)/shard_map/ppermute | solution.py:376
  121.5 19.7 %collective-permute-start.4 = (s16[528,640]{1,0:T(8,128)(2,1)S(1)}, s16[528,640]{1,0:T(8,128)(2,1)S(1)}, u32[]{:S(2)}, u32[]{:S(2)}) collective-permute-start(s16[528,640]{1,0:T(8,128)(2,1)S(1)} %get-tuple-element.55), channel_id=1, source_target_pairs={{0,96},{8,104},{16,112},{24,120},{32,0},{40,8},{48,16},{56,24},{64... | collective-permute-start | bytes 2027528 | tf_op jit(solution)/shard_map/ppermute | solution.py:376
  121.6 22.2 %collective-permute-start.5 = (s16[528,640]{1,0:T(8,128)(2,1)S(1)}, s16[528,640]{1,0:T(8,128)(2,1)S(1)}, u32[]{:S(2)}, u32[]{:S(2)}) collective-permute-start(s16[528,640]{1,0:T(8,128)(2,1)S(1)} %get-tuple-element.56), channel_id=1, source_target_pairs={{0,32},{8,40},{16,48},{24,56},{32,64},{40,72},{48,80},{56,88},{64,... | collective-permute-start | bytes 2027528 | tf_op jit(solution)/shard_map/ppermute | solution.py:376
  123.1 20.8 %collective-permute-start.6 = (s16[528,640]{1,0:T(8,128)(2,1)S(1)}, s16[528,640]{1,0:T(8,128)(2,1)S(1)}, u32[]{:S(2)}, u32[]{:S(2)}) collective-permute-start(s16[528,640]{1,0:T(8,128)(2,1)S(1)} %get-tuple-element.57), channel_id=1, source_target_pairs={{0,24},{8,0},{16,8},{24,16},{32,56},{40,32},{48,40},{56,48},{64,88... | collective-permute-start | bytes 2027528 | tf_op jit(solution)/shard_map/ppermute | solution.py:376
  123.1 23.5 %collective-permute-start.7 = (s16[528,640]{1,0:T(8,128)(2,1)S(1)}, s16[528,640]{1,0:T(8,128)(2,1)S(1)}, u32[]{:S(2)}, u32[]{:S(2)}) collective-permute-start(s16[528,640]{1,0:T(8,128)(2,1)S(1)} %get-tuple-element.58), channel_id=1, source_target_pairs={{0,8},{8,16},{16,24},{24,0},{32,40},{40,48},{48,56},{56,32},{64,72... | collective-permute-start | bytes 2027528 | tf_op jit(solution)/shard_map/ppermute | solution.py:376
  141.1 25.3 %collective-permute-start.8 = (s16[528,640]{1,0:T(8,128)(2,1)S(1)}, s16[528,640]{1,0:T(8,128)(2,1)S(1)}, u32[]{:S(2)}, u32[]{:S(2)}) collective-permute-start(s16[528,640]{1,0:T(8,128)(2,1)S(1)} %get-tuple-element.61), channel_id=1, source_target_pairs={{0,32},{8,40},{16,48},{24,56},{32,64},{40,72},{48,80},{56,88},{64,... | collective-permute-start | bytes 2027528 | tf_op jit(solution)/shard_map/ppermute | solution.py:376
  141.2 25.3 %collective-permute-start.9 = (s16[528,640]{1,0:T(8,128)(2,1)S(1)}, s16[528,640]{1,0:T(8,128)(2,1)S(1)}, u32[]{:S(2)}, u32[]{:S(2)}) collective-permute-start(s16[528,640]{1,0:T(8,128)(2,1)S(1)} %get-tuple-element.62), channel_id=1, source_target_pairs={{0,96},{8,104},{16,112},{24,120},{32,0},{40,8},{48,16},{56,24},{64... | collective-permute-start | bytes 2027528 | tf_op jit(solution)/shard_map/ppermute | solution.py:376
  143.9 17.1 %collective-permute-start.10 = (s16[528,640]{1,0:T(8,128)(2,1)S(1)}, s16[528,640]{1,0:T(8,128)(2,1)S(1)}, u32[]{:S(2)}, u32[]{:S(2)}) collective-permute-start(s16[528,640]{1,0:T(8,128)(2,1)S(1)} %get-tuple-element.66), channel_id=1, source_target_pairs={{0,8},{8,16},{16,24},{24,0},{32,40},{40,48},{48,56},{56,32},{64,72... | collective-permute-start | bytes 2027528 | tf_op jit(solution)/shard_map/ppermute | solution.py:376
  143.9 17.1 %collective-permute-start.11 = (s16[528,640]{1,0:T(8,128)(2,1)S(1)}, s16[528,640]{1,0:T(8,128)(2,1)S(1)}, u32[]{:S(2)}, u32[]{:S(2)}) collective-permute-start(s16[528,640]{1,0:T(8,128)(2,1)S(1)} %get-tuple-element.67), channel_id=1, source_target_pairs={{0,24},{8,0},{16,8},{24,16},{32,56},{40,32},{48,40},{56,48},{64,88... | collective-permute-start | bytes 2027528 | tf_op jit(solution)/shard_map/ppermute | solution.py:376
  163.6 24.5 %copy-start.3 = (f32[256,1280]{1,0:T(8,128)S(1)}, f32[256,1280]{1,0:T(8,128)}, u32[]{:S(2)}) copy-start(f32[256,1280]{1,0:T(8,128)} %convolution_multiply_fusion.text_ref) | copy-start | bytes 3932164
  163.6 10.9 %collective-permute-start.15 = (s16[272,640]{1,0:T(8,128)(2,1)S(1)}, s16[272,640]{1,0:T(8,128)(2,1)S(1)}, u32[]{:S(2)}, u32[]{:S(2)}) collective-permute-start(s16[272,640]{1,0:T(8,128)(2,1)S(1)} %get-tuple-element.72), channel_id=1, source_target_pairs={{0,64},{8,72},{16,80},{24,88},{32,96},{40,104},{48,112},{56,120},{... | collective-permute-start | bytes 1044488 | tf_op jit(solution)/shard_map/ppermute | solution.py:376
  163.7 18.6 %collective-permute-start.16 = (s16[272,640]{1,0:T(8,128)(2,1)S(1)}, s16[272,640]{1,0:T(8,128)(2,1)S(1)}, u32[]{:S(2)}, u32[]{:S(2)}) collective-permute-start(s16[272,640]{1,0:T(8,128)(2,1)S(1)} %get-tuple-element.73), channel_id=1, source_target_pairs={{0,32},{8,40},{16,48},{24,56},{32,64},{40,72},{48,80},{56,88},{64,... | collective-permute-start | bytes 1044488 | tf_op jit(solution)/shard_map/ppermute | solution.py:376
  163.8 18.5 %collective-permute-start.17 = (s16[272,640]{1,0:T(8,128)(2,1)S(1)}, s16[272,640]{1,0:T(8,128)(2,1)S(1)}, u32[]{:S(2)}, u32[]{:S(2)}) collective-permute-start(s16[272,640]{1,0:T(8,128)(2,1)S(1)} %get-tuple-element.74), channel_id=1, source_target_pairs={{0,96},{8,104},{16,112},{24,120},{32,0},{40,8},{48,16},{56,24},{64... | collective-permute-start | bytes 1044488 | tf_op jit(solution)/shard_map/ppermute | solution.py:376
  169.0 13.3 %collective-permute-start.12 = (s16[272,640]{1,0:T(8,128)(2,1)S(1)}, s16[272,640]{1,0:T(8,128)(2,1)S(1)}, u32[]{:S(2)}, u32[]{:S(2)}) collective-permute-start(s16[272,640]{1,0:T(8,128)(2,1)S(1)} %get-tuple-element.69), channel_id=1, source_target_pairs={{0,16},{8,24},{16,0},{24,8},{32,48},{40,56},{48,32},{56,40},{64,80... | collective-permute-start | bytes 1044488 | tf_op jit(solution)/shard_map/ppermute | solution.py:376
  170.3 17.8 %collective-permute-start.13 = (s16[272,640]{1,0:T(8,128)(2,1)S(1)}, s16[272,640]{1,0:T(8,128)(2,1)S(1)}, u32[]{:S(2)}, u32[]{:S(2)}) collective-permute-start(s16[272,640]{1,0:T(8,128)(2,1)S(1)} %get-tuple-element.70), channel_id=1, source_target_pairs={{0,8},{8,16},{16,24},{24,0},{32,40},{40,48},{48,56},{56,32},{64,72... | collective-permute-start | bytes 1044488 | tf_op jit(solution)/shard_map/ppermute | solution.py:376
  174.5 13.7 %collective-permute-start.14 = (s16[272,640]{1,0:T(8,128)(2,1)S(1)}, s16[272,640]{1,0:T(8,128)(2,1)S(1)}, u32[]{:S(2)}, u32[]{:S(2)}) collective-permute-start(s16[272,640]{1,0:T(8,128)(2,1)S(1)} %get-tuple-element.71), channel_id=1, source_target_pairs={{0,24},{8,0},{16,8},{24,16},{32,56},{40,32},{48,40},{56,48},{64,88... | collective-permute-start | bytes 1044488 | tf_op jit(solution)/shard_map/ppermute | solution.py:376
  188.2 13.8 %copy-start.1 = (bf16[1280,1024]{1,0:T(8,128)(2,1)S(1)}, bf16[1280,1024]{1,0:T(8,128)(2,1)}, u32[]{:S(2)}) copy-start(bf16[1280,1024]{1,0:T(8,128)(2,1)} %param.7) | copy-start | bytes 7864324
Sparse Core Ops, SparseCore 0:
  10.3 73.9 all-gather.3
